TPU v7x, 512 devices: a whole 4x8x8 slice. The times are simulated.
512 devices in a mesh: dp: 64 (over x, y, core), pool: 8 (over z).
Axes of the slice: x: 4, y: 8, z: 8, core: 2. Of those that a mesh axis runs over, the one named last changes fastest.
Arguments:
- query_act: bfloat16 [131072, 1024], P(('dp', 'pool')), may hold values from -6 to 6
- key_act: bfloat16 [131072, 1024], P(('dp', 'pool')), may hold values from -6 to 6
- value_act: bfloat16 [131072, 1024], P(('dp', 'pool')), may hold values from -6 to 6
- gate_act: bfloat16 [131072, 1024], P(('dp', 'pool')), may hold values from -6 to 6
- lengths: int32 [512, 4], P(('dp', 'pool')), may hold values from 1 to 192, 256 in all within a row
- targets: int32 [131072], P(('dp', 'pool')), may hold values from 0 to 767
- pool_rows: bfloat16 [49152, 1024], P(('dp', 'pool')), may hold values from -8 to 8
- pool_ids: int32 [49152], P(('dp', 'pool')), may hold values from 0 to 3071
- norm_gain: float32 [1024], replicated, may hold values from 0.1 to 1.9
Outputs:
- query_grad: bfloat16 [131072, 1024], P(('dp', 'pool'))
- key_grad: bfloat16 [131072, 1024], P(('dp', 'pool'))
- value_grad: bfloat16 [131072, 1024], P(('dp', 'pool'))
- gate_grad: bfloat16 [131072, 1024], P(('dp', 'pool'))
- pool_grad: float32 [49152, 1024], P(('dp', 'pool'))
- gain_grad: float32 [1024], replicated
Inputs may be any that keep to these rules, and one draw needn't show every extreme that they name: In each device's row the 4 lengths sum to 256 and the longest is exactly 192.
All inputs are finite; a program needn't handle non-finite values.
Results may differ from a plain program's by a relative error of at most 0.015.
The roundings to bfloat16 on the way count: a program that leaves them out, or rounds other values in their place, can miss the bound.
Values may be sent and summed in bfloat16 or wider, within the bound.
No kernel may reach another device: no remote copies, remote signals or barrier semaphores. Data moves between devices by JAX's collectives and lax.ppermute only.
A program may use at most 64 MiB of HBM per device.

v0:
```python
import jax
import jax.numpy as jnp
from jax import lax
from jax.sharding import PartitionSpec as P

HEADS = 8
LMAX = 192


EPSILON = 1e-05


def split_heads(matrix, heads):
    return matrix.reshape(matrix.shape[0], heads, matrix.shape[1] // heads)


def body(query_act, key_act, value_act, gate_act, lengths, targets, pool_rows, pool_ids, norm_gain):
    count = query_act.shape[0]
    width = query_act.shape[1]
    scaling = (width // HEADS) ** (-0.5)
    finish = jnp.cumsum(lengths[0])
    position = jnp.arange(count, dtype=jnp.int32)
    segment = jnp.sum((position[:, None] >= finish[None, :]).astype(jnp.int32), axis=1)
    following = jnp.sum((position[:, None] + 1 >= finish[None, :]).astype(jnp.int32), axis=1)
    usable = (following == segment).astype(jnp.float32)
    allowed = (segment[:, None] == segment[None, :]) & (position[None, :] <= position[:, None])
    queries = split_heads(query_act, HEADS)
    keys_all = split_heads(key_act, HEADS)
    values_all = split_heads(value_act, HEADS)
    everything, all_ids = (
        lax.all_gather(pool_rows, "pool", axis=0, tiled=True),
        lax.all_gather(pool_ids, "pool", axis=0, tiled=True),
    )
    scores = (
        jnp.einsum("thd,shd->hts", queries, keys_all, preferred_element_type=jnp.float32) * scaling
    )
    squash = jax.nn.sigmoid(scores)
    attend = jnp.where(allowed[None], scores * squash, 0.0) / LMAX
    attend_b = attend.astype(jnp.bfloat16)
    mixed = jnp.einsum(
        "hts,shd->thd", attend_b, values_all, preferred_element_type=jnp.float32
    ).reshape(count, width)
    center = mixed - jnp.mean(mixed, axis=1, keepdims=True)
    inv_dev = lax.rsqrt(jnp.mean(center * center, axis=1, keepdims=True) + EPSILON)
    normed = center * inv_dev
    scaled = normed * norm_gain
    gate_f = gate_act.astype(jnp.float32)
    embedded = (scaled * gate_f).astype(jnp.bfloat16)
    contract_last = (((1,), (1,)), ((), ()))
    contract_first = (((0,), (0,)), ((), ()))
    logits = lax.dot_general(
        embedded, everything, contract_last, preferred_element_type=jnp.float32
    )
    columns = jnp.arange(everything.shape[0], dtype=jnp.int32)
    chosen = targets[:, None] == columns[None, :]
    target_ids = jnp.sum(jnp.where(chosen, all_ids[None, :], 0), axis=1).astype(jnp.int32)
    clash = (all_ids[None, :] == target_ids[:, None]) & jnp.logical_not(chosen)
    masked = jnp.where(clash, -1e30, logits)
    peak = jnp.max(masked, axis=1, keepdims=True)
    total = jnp.sum(jnp.exp(masked - peak), axis=1, keepdims=True)
    log_total = peak + jnp.log(total)
    probs = jnp.where(clash, 0.0, jnp.exp(logits - log_total))
    slopes = (usable[:, None] * (probs - chosen.astype(jnp.float32))).astype(jnp.bfloat16)
    pool_grad = lax.psum_scatter(
        lax.dot_general(
            slopes, embedded, contract_first, preferred_element_type=jnp.float32
        ).astype(jnp.bfloat16),
        "pool",
        scatter_dimension=0,
        tiled=True,
    ).astype(jnp.float32)
    back = jnp.dot(slopes, everything, preferred_element_type=jnp.float32)
    dscaled = back * gate_f
    gate_grad = (back * scaled).astype(jnp.bfloat16)
    gain_part = jnp.sum(dscaled * normed, axis=0)
    gain_grad = lax.psum(gain_part, ("dp", "pool"))
    dnormed = dscaled * norm_gain
    dmixed = (
        dnormed
        - jnp.mean(dnormed, axis=1, keepdims=True)
        - normed * jnp.mean(dnormed * normed, axis=1, keepdims=True)
    ) * inv_dev
    dmixed_h = split_heads(dmixed.astype(jnp.bfloat16), HEADS)
    dattend = jnp.einsum("thd,shd->hts", dmixed_h, values_all, preferred_element_type=jnp.float32)
    value_grad = (
        jnp.einsum("hts,thd->shd", attend_b, dmixed_h, preferred_element_type=jnp.float32)
        .reshape(count, width)
        .astype(jnp.bfloat16)
    )
    dscores = jnp.where(allowed[None], dattend * squash * (1.0 + scores * (1.0 - squash)), 0.0) * (
        scaling / LMAX
    )
    dscores_b = dscores.astype(jnp.bfloat16)
    query_grad = (
        jnp.einsum("hts,shd->thd", dscores_b, keys_all, preferred_element_type=jnp.float32)
        .reshape(count, width)
        .astype(jnp.bfloat16)
    )
    key_grad = (
        jnp.einsum("hts,thd->shd", dscores_b, queries, preferred_element_type=jnp.float32)
        .reshape(count, width)
        .astype(jnp.bfloat16)
    )
    return (query_grad, key_grad, value_grad, gate_grad, pool_grad, gain_grad)


def solution(mesh):
    in_specs = (
        P(("dp", "pool"), None),
        P(("dp", "pool"), None),
        P(("dp", "pool"), None),
        P(("dp", "pool"), None),
        P(("dp", "pool"), None),
        P(("dp", "pool")),
        P(("dp", "pool"), None),
        P(("dp", "pool")),
        P(),
    )
    out_specs = (
        P(("dp", "pool"), None),
        P(("dp", "pool"), None),
        P(("dp", "pool"), None),
        P(("dp", "pool"), None),
        P(("dp", "pool"), None),
        P(),
    )
    return jax.shard_map(body, mesh=mesh, in_specs=in_specs, out_specs=out_specs, check_vma=False)
```

profile of v0, /device:TPU:1, one launch (start us, length us, event | category | flops | bytes accessed | tf_op | source)
XLA Modules:
  0.0 182.5 jit_solution(17288248518671332621)
XLA Ops:
  7.2 0.7 all-gather.2.cloned.1.call-update
  8.0 1.2 copy.39
  9.2 1.4 copy.40
  11.1 2.2 %multiply_convert_fusion.1 = (bf16[8,256,256]{2,1,0:T(8,128)(2,1)S(1)}, f32[8,256,256]{2,1,0:T(8,128)}) fusion(pred[256,256]{1,0:T(8,128)(4,1)S(1)} %fusion.12, bf16[256,8,128]{0,2,1:T(8,128)(2,1)S(1)} %bitcast.52, bf16[256,8,128]{0,2,1:T(8,128)(2,1)S(1)} %bitcast.54), kind=kOutput, calls=%fused_computation.1 | convolution fusion | flops 138412032 | bytes 4259840 | tf_op jit(solution)/shard_map/thd,shd->hts/dot_general | solution.py:35
  13.3 0.5 fusion.14
  13.9 0.4 copy-done.1
  14.3 0.3 copy.30
  14.7 1.3 dynamic-slice
  16.9 16.8 %all-reduce = s32[768]{0:T(1024)S(1)} all-reduce(s32[768]{0:T(1024)S(1)} %dynamic-update-slice), channel_id=1, replica_groups=mesh['dp'=64,'pool'=8] {'pool'}, use_global_device_ids=true, to_apply=%add | all-reduce | flops 768 | bytes 6144
  34.4 20.9 %all-gather.2.cloned.1.call-done = bf16[768,1024]{1,0:T(8,128)(2,1)} async-done(((bf16[96,1024]{1,0:T(8,128)(2,1)}), bf16[768,1024]{1,0:T(8,128)(2,1)}) %all-gather.2.cloned.1.call-update) | async-done | bytes 1572880 | tf_op jit(solution)/shard_map/all_gather | solution.py:31
  55.2 2.2 %fusion.11 = (f32[256]{0:T(256)S(1)}, f32[256,768]{1,0:T(8,128)S(1)}) fusion(s32[256]{0:T(256)S(1)} %copy-done.9, s32[768]{0:T(1024)S(1)} %all-reduce, s32[256]{0:T(256)S(1)} %select_reduce_fusion, bf16[256,1024]{1,0:T(8,128)(2,1)S(1)} %fusion, bf16[768,1024]{1,0:T(8,128)(2,1)} %all-gather.2.cloned.1.call-done), kind=kOutput, calls=%fused_computation.31 | convolution fusion | flops 403832576 | bytes 2889728 | tf_op jit(solution)/shard_map/dot_general | solution.py:51
  57.4 0.5 exponential_reduce_fusion
  57.9 2.1 %convolution_convert_fusion = bf16[768,1024]{1,0:T(8,128)(2,1)} fusion(bf16[256,1024]{1,0:T(8,128)(2,1)S(1)} %fusion, f32[256,768]{1,0:T(8,128)S(1)} %get-tuple-element.30, f32[256]{0:T(256)S(1)} %log_add_fusion, s32[256]{0:T(256)S(1)} %copy-done.9, s32[768]{0:T(1024)S(1)} %all-reduce, f32[256]{0:T(256)S(1)} %compare_convert_fusion, ...), kind=kOutput, calls=%fused_computation.3 | convolution fusion | flops 405405696 | bytes 2890752 | tf_op jit(solution)/shard_map/dot_general | solution.py:65
  60.1 2.6 %multiply_reduce_fusion = (f32[1024]{0:T(1024)S(1)}, f32[256]{0:T(256)S(1)}, f32[256]{0:T(256)S(1)}, f32[256,1024]{1,0:T(8,128)S(1)}) fusion(f32[256,1024]{1,0:T(8,128)S(1)} %copy.30, f32[256]{0:T(256)S(1)} %add_rsqrt_fusion, f32[256]{0:T(256)S(1)} %broadcast_multiply_fusion.2, bf16[256,1024]{1,0:T(8,128)(2,1)S(1)} %copy-done.3, f32[1024]{0:T(1024)S(1)} %copy-done.8, ...), kind=kOutput, calls=%fused_computation.13 | convolution fusion | flops 407239168 | bytes 5000192 | tf_op jit(solution)/shard_map/dot_general | solution.py:72
  62.7 1.4 multiply_convert_fusion.2
  64.2 1.2 copy.41
  65.4 0.3 convolution_convert_fusion.2
  65.7 1.0 copy.38
  66.7 2.9 %multiply_convert_fusion = bf16[8,256,256]{2,1,0:T(8,128)(2,1)S(1)} fusion(f32[8,256,256]{2,1,0:T(8,128)} %get-tuple-element.26, bf16[256,8,128]{0,2,1:T(8,128)(2,1)S(1)} %bitcast.57, pred[256,256]{1,0:T(8,128)(4,1)S(1)} %fusion.12, bf16[256,1024]{1,0:T(8,128)(2,1)S(1)} %copy-done), kind=kOutput, calls=%fused_computation | convolution fusion | flops 140509184 | bytes 4259840 | tf_op jit(solution)/shard_map/thd,shd->hts/dot_general | solution.py:84
  69.6 0.5 convolution_convert_fusion.3
  70.1 1.0 copy.36
  71.4 1.0 copy.37
  72.4 101.5 %psum.7 = f32[1024]{0:T(1024)} all-reduce(f32[1024]{0:T(1024)S(1)} %get-tuple-element.18), channel_id=1, replica_groups=mesh['dp'=64,'pool'=8] {'dp','pool'}, use_global_device_ids=true, to_apply=%region_12.13 | all-reduce | flops 1024 | bytes 8192 | tf_op jit(solution)/shard_map/psum | solution.py:76
  173.9 1.7 convert_element_type.91
  (42 shorter events, 1.8 us)
Async XLA Ops:
  7.2 6.2 %copy-start = (bf16[256,1024]{1,0:T(8,128)(2,1)S(1)}, bf16[256,1024]{1,0:T(8,128)(2,1)}, u32[]{:S(2)}) copy-start(bf16[256,1024]{1,0:T(8,128)(2,1)} %param.11) | copy-start | bytes 1572868
  7.2 3.5 %copy-start.10 = (s32[1,4]{1,0:T(1,128)S(1)}, s32[1,4]{1,0:T(1,128)}, u32[]{:S(2)}) copy-start(s32[1,4]{1,0:T(1,128)} %param.13) | copy-start | bytes 52
  7.2 48.0 %all-gather.2.cloned.1.call-start = ((), (), s32[]{:S(2)}) async-start(), calls=%async_computation.1 | async-start | bytes 1769472 | tf_op jit(solution)/shard_map/all_gather | solution.py:31
  7.9 166.0 %reduce-scatter.2.cloned.1.call-start = ((), (), s32[]{:S(2)}) async-start(), calls=%async_computation.2 | async-start | bytes 1769472 | tf_op jit(solution)/shard_map/reduce_scatter | solution.py:64
  9.2 4.1 %copy-start.4 = (bf16[256,1024]{0,1:T(8,128)(2,1)}, bf16[256,1024]{0,1:T(8,128)(2,1)S(1)}, u32[]{:S(2)}) copy-start(bf16[256,1024]{0,1:T(8,128)(2,1)S(1)} %copy.39) | copy-start | bytes 1572868
  10.7 2.6 %copy-start.6 = (bf16[256,1024]{0,1:T(8,128)(2,1)}, bf16[256,1024]{0,1:T(8,128)(2,1)S(1)}, u32[]{:S(2)}) copy-start(bf16[256,1024]{0,1:T(8,128)(2,1)S(1)} %copy.40) | copy-start | bytes 1572868
  13.3 1.0 copy-start.1
  13.3 3.3 %copy-start.11 = (s32[96]{0:T(128)S(1)}, s32[96]{0:T(128)}, u32[]{:S(2)}) copy-start(s32[96]{0:T(128)} %param.16) | copy-start | bytes 1156
  13.3 20.3 %copy-start.9 = (s32[256]{0:T(256)S(1)}, s32[256]{0:T(256)}, u32[]{:S(2)}) copy-start(s32[256]{0:T(256)} %param.14) | copy-start | bytes 3076
  13.9 20.2 %copy-start.3 = (bf16[256,1024]{1,0:T(8,128)(2,1)S(1)}, bf16[256,1024]{1,0:T(8,128)(2,1)}, u32[]{:S(2)}) copy-start(bf16[256,1024]{1,0:T(8,128)(2,1)} %param.12) | copy-start | bytes 1572868
  13.9 20.2 %copy-start.8 = (f32[1024]{0:T(1024)S(1)}, f32[1024]{0:T(1024)}, u32[]{:S(2)}) copy-start(f32[1024]{0:T(1024)} %param.17) | copy-start | bytes 12292
  62.7 2.7 %copy-start.2 = (bf16[8,256,256]{2,1,0:T(8,128)(2,1)S(1)}, bf16[8,256,256]{2,1,0:T(8,128)(2,1)}, u32[]{:S(2)}) copy-start(bf16[8,256,256]{2,1,0:T(8,128)(2,1)} %copy-done.1) | copy-start | bytes 3145732
  66.7 2.9 %copy-start.7 = (bf16[256,1024]{0,1:T(8,128)(2,1)S(1)}, bf16[256,1024]{0,1:T(8,128)(2,1)}, u32[]{:S(2)}) copy-start(bf16[256,1024]{0,1:T(8,128)(2,1)} %copy-done.6) | copy-start | bytes 1572868
  69.6 1.5 copy-start.5
Sparse Core Ops, SparseCore 0:
  10.1 45.0 all-gather.1
  60.2 42.0 reduce-scatter.1
where the time goes:
time: 183 us; the launch traced here: 182 us
  blocking collectives  118 us (64%)
  waiting for transfers between devices  21.6 us (12%)
  between operations  14.9 us (8%)
  matrix products  13.6 us (7%)
  local copies, waits for them, and re-layouts  9.28 us (5%)
  other arithmetic  4.71 us (3%)
    psum x1, blocking collectives, body(): gain_grad = lax.psum(gain_part, ('dp', 'pool'))  101 us
    all_gather x1, waiting for transfers between devices, body(): lax.all_gather(pool_rows, 'pool', axis=0, tiled=True)  20.9 us
    unnamed x1, blocking collectives  16.8 us
    unnamed x30, local copies, waits for them, and re-layouts  5.03 us
    reshape x3, local copies, waits for them, and re-layouts, split_heads(): return matrix.reshape(matrix.shape[0], heads, matrix.shape[1] // heads)  3.92 us
  transfers between devices with their start and end apart: 2, of which 1 were waited for; matrix products, arithmetic and copies ran while one was open for 11% of the time, Pallas kernels for 0%

commit v1 on v0

v1 whole, which is shorter than its diff:
```python
import functools

import jax
import jax.numpy as jnp
from jax import lax
from jax.experimental import pallas as pl
from jax.experimental.pallas import tpu as pltpu
from jax.sharding import PartitionSpec as P

HEADS = 8
LMAX = 192
EPSILON = 1e-05
COUNT = 256
WIDTH = 1024
HEAD_DIM = 128
ROWS = 96
RING = 8
POOL = ROWS * RING
HALF = ROWS // 2
XY = 32
NEAR = 16

F32 = jnp.float32
BF16 = jnp.bfloat16
I32 = jnp.int32
CONTRACT_LAST = (((1,), (1,)), ((), ()))
CONTRACT_FIRST = (((0,), (0,)), ((), ()))


def dot(a, b, dims=(((1,), (0,)), ((), ()))):
    return lax.dot_general(a, b, dims, preferred_element_type=F32)


def forward_kernel(
    lengths, q_ref, k_ref, v_ref, gate_ref, gain_ref,
    emb_ref, normed_ref, inv_ref, attend_ref, slope_ref, mixed, mask,
):
    scaling = HEAD_DIM ** (-0.5)
    row = lax.broadcasted_iota(I32, (COUNT, COUNT), 0)
    col = lax.broadcasted_iota(I32, (COUNT, COUNT), 1)
    first = jnp.zeros((COUNT, COUNT), I32)
    finish = jnp.int32(0)
    for i in range(lengths.shape[1]):
        finish = finish + lengths[0, i]
        first = jnp.where(row >= finish, finish, first)
    mask[...] = jnp.where((col >= first) & (col <= row), F32(1.0 / LMAX), F32(0.0))
    for h in range(HEADS):
        lanes = slice(h * HEAD_DIM, (h + 1) * HEAD_DIM)
        scores = dot(q_ref[:, lanes], k_ref[:, lanes], CONTRACT_LAST) * scaling
        squash = 0.5 * jnp.tanh(0.5 * scores) + 0.5
        keep = mask[...]
        act = scores * squash
        attend = (act * keep).astype(BF16)
        attend_ref[h] = attend
        slope_ref[h] = (squash + act * (1.0 - squash)) * (keep * scaling)
        mixed[:, lanes] = dot(attend, v_ref[:, lanes])
    gain = gain_ref[...]
    step = 64
    for i in range(COUNT // step):
        at = slice(i * step, (i + 1) * step)
        part = mixed[at, :]
        center = part - jnp.mean(part, axis=1, keepdims=True)
        inv = lax.rsqrt(jnp.mean(center * center, axis=1, keepdims=True) + EPSILON)
        normed = center * inv
        normed_ref[at, :] = normed
        inv_ref[at, :] = jnp.broadcast_to(inv, (step, HEAD_DIM))
        emb_ref[at, :] = (normed * gain * gate_ref[at, :].astype(F32)).astype(BF16)


def pool_kernel(
    place, lengths, emb_ref, normed_ref, inv_ref, gate_ref, gain_ref, target_ref, ids_ref,
    own, r1, r2, r3, l1, l2, l3, far_a, far_b,
    plus1, minus1, plus2h, minus2h, plus2, minus2, keep_ref, gate_grad_ref, dmixed_ref, part_ref,
    rows, logits, slopes, terms, back,
):
    z = place[0]

    def block(offset):
        return pl.multiple_of(lax.rem(z + offset + RING, RING) * ROWS, 16)

    rows[pl.ds(block(0), ROWS), :] = own[...]
    for offset, ref in ((-1, r1), (-2, r2), (-3, r3), (1, l1), (2, l2), (3, l3)):
        rows[pl.ds(block(offset), ROWS), :] = ref[...]
    rows[pl.ds(block(4), HALF), :] = far_a[...]
    rows[pl.ds(pl.multiple_of(block(4) + HALF, 16), HALF), :] = far_b[...]

    logits[...] = dot(emb_ref[...], rows[...], CONTRACT_LAST)
    step = 32
    ids = ids_ref[...]
    for i in range(COUNT // step):
        at = slice(i * step, (i + 1) * step)
        target = target_ref[at, :]
        column = lax.broadcasted_iota(I32, (step, POOL), 1)
        chosen = column == target
        own_id = jnp.sum(jnp.where(chosen, ids, F32(0)), axis=1, keepdims=True)
        token = lax.broadcasted_iota(I32, (step, 1), 0) + i * step
        usable = jnp.ones((step, 1), F32)
        finish = jnp.int32(0)
        for j in range(lengths.shape[1]):
            finish = finish + lengths[0, j]
            usable = jnp.where(token + 1 == finish, F32(0.0), usable)
        clash = (ids == own_id) & jnp.logical_not(chosen)
        masked = jnp.where(clash, F32(-1e30), logits[at, :])
        peak = jnp.max(masked, axis=1, keepdims=True)
        weight = jnp.where(clash, F32(0.0), jnp.exp(masked - peak))
        total = jnp.sum(weight, axis=1, keepdims=True)
        probs = weight * (1.0 / total)
        slopes[at, :] = (usable * jnp.where(chosen, probs - 1.0, probs)).astype(BF16)

    terms[...] = dot(slopes[...], emb_ref[...], CONTRACT_FIRST).astype(BF16)
    keep_ref[...] = terms[pl.ds(block(0), ROWS), :]
    plus1[0:ROWS, :] = terms[pl.ds(block(3), ROWS), :]
    plus1[ROWS : 2 * ROWS, :] = terms[pl.ds(block(1), ROWS), :]
    minus1[0:ROWS, :] = terms[pl.ds(block(-3), ROWS), :]
    minus1[ROWS : 2 * ROWS, :] = terms[pl.ds(block(-1), ROWS), :]
    plus2h[...] = terms[pl.ds(block(4), HALF), :]
    minus2h[...] = terms[pl.ds(pl.multiple_of(block(4) + HALF, 16), HALF), :]
    plus2[...] = terms[pl.ds(block(2), ROWS), :]
    minus2[...] = terms[pl.ds(block(-2), ROWS), :]

    back[...] = dot(slopes[...], rows[...])
    gain = gain_ref[...]
    sums = jnp.zeros((8, WIDTH), F32)
    step = 32
    for i in range(COUNT // step):
        at = slice(i * step, (i + 1) * step)
        normed = normed_ref[at, :]
        pulled = back[at, :]
        gate_grad_ref[at, :] = (pulled * (normed * gain)).astype(BF16)
        dscaled = pulled * gate_ref[at, :].astype(F32)
        product = dscaled * normed
        sums = sums + jnp.sum(product.reshape(step // 8, 8, WIDTH), axis=0)
        dnormed = dscaled * gain
        mean1 = jnp.mean(dnormed, axis=1, keepdims=True)
        mean2 = jnp.mean(product * gain, axis=1, keepdims=True)
        dmixed_ref[at, :] = ((dnormed - mean1 - normed * mean2) * inv_ref[at, 0:1]).astype(BF16)
    part_ref[...] = jnp.broadcast_to(jnp.sum(sums, axis=0, keepdims=True), (XY, WIDTH))


def backward_kernel(
    dmixed_ref, q_ref, k_ref, v_ref, attend_ref, slope_ref, dq_ref, dk_ref, dv_ref,
):
    for h in range(HEADS):
        lanes = slice(h * HEAD_DIM, (h + 1) * HEAD_DIM)
        dmixed = dmixed_ref[:, lanes]
        dattend = dot(dmixed, v_ref[:, lanes], CONTRACT_LAST)
        dscores = (dattend * slope_ref[h]).astype(BF16)
        dv_ref[:, lanes] = dot(attend_ref[h], dmixed, CONTRACT_FIRST).astype(BF16)
        dq_ref[:, lanes] = dot(dscores, k_ref[:, lanes]).astype(BF16)
        dk_ref[:, lanes] = dot(dscores, q_ref[:, lanes], CONTRACT_FIRST).astype(BF16)


VMEM = pl.BlockSpec(memory_space=pltpu.VMEM)
SMEM = pl.BlockSpec(memory_space=pltpu.SMEM)


def call(kernel, specs, outs, scratch, cost, limit=24):
    return pl.pallas_call(
        kernel,
        out_shape=[jax.ShapeDtypeStruct(shape, kind) for shape, kind in outs],
        in_specs=specs,
        out_specs=[VMEM] * len(outs),
        scratch_shapes=[pltpu.VMEM(shape, kind) for shape, kind in scratch],
        compiler_params=pltpu.CompilerParams(vmem_limit_bytes=limit * 1024 * 1024),
        cost_estimate=cost,
    )


def shift(value, by):
    return lax.ppermute(value, "pool", [(i, (i + by) % RING) for i in range(RING)])


def body(query_act, key_act, value_act, gate_act, lengths, targets, pool_rows, pool_ids, norm_gain):
    token = (COUNT, WIDTH)
    r2 = shift(pool_rows, 2)
    l2 = shift(pool_rows, -2)
    r1 = shift(pool_rows, 1)
    l1 = shift(pool_rows, -1)
    r3 = shift(r2, 1)
    l3 = shift(l2, -1)
    far_a = shift(r2[:HALF], 2)
    far_b = shift(l2[HALF:], -2)
    ids = lax.all_to_all(
        jnp.broadcast_to(pool_ids[None, :], (RING, ROWS)), "pool", 0, 0
    ).reshape(1, POOL).astype(F32)
    gain = norm_gain.reshape(1, WIDTH)
    place = lax.axis_index("pool").reshape(1).astype(I32)

    emb, normed, inv, attend, slope = call(
        forward_kernel,
        [SMEM] + [VMEM] * 5,
        [(token, BF16), (token, F32), ((COUNT, HEAD_DIM), F32),
         ((HEADS, COUNT, COUNT), BF16), ((HEADS, COUNT, COUNT), F32)],
        [(token, F32), ((COUNT, COUNT), F32)],
        pl.CostEstimate(flops=2 * 10**9, bytes_accessed=8 * 10**6, transcendentals=524288),
    )(lengths, query_act, key_act, value_act, gate_act, gain)

    chunk = (ROWS, WIDTH)
    half = (HALF, WIDTH)
    plus1, minus1, plus2h, minus2h, plus2, minus2, kept, gate_grad, dmixed, part = call(
        pool_kernel,
        [SMEM, SMEM] + [VMEM] * 16,
        [((2 * ROWS, WIDTH), BF16), ((2 * ROWS, WIDTH), BF16), (half, BF16), (half, BF16),
         (chunk, BF16), (chunk, BF16), (chunk, BF16), (token, BF16), (token, BF16),
         ((XY, WIDTH), F32)],
        [((POOL, WIDTH), BF16), ((COUNT, POOL), F32), ((COUNT, POOL), BF16),
         ((POOL, WIDTH), BF16), (token, F32)],
        pl.CostEstimate(flops=2 * 10**9, bytes_accessed=8 * 10**6, transcendentals=196608),
    )(place, lengths, emb, normed, inv, gate_act, gain, targets.reshape(COUNT, 1), ids,
      pool_rows, r1, r2, r3, l1, l2, l3, far_a, far_b)

    from_left = shift(plus1, 1)
    from_right = shift(minus1, -1)
    far_left = shift(plus2h, 2)
    far_right = shift(minus2h, -2)

    plane = [[x * 16 + y * 2 + c for x in range(4) for y in range(8)] for c in range(2)]
    spread = lax.all_to_all(part, "dp", 0, 0, axis_index_groups=plane)
    spread = jnp.broadcast_to(jnp.sum(spread, axis=0, keepdims=True), (NEAR, WIDTH))
    near = [[i * NEAR + j for j in range(NEAR)] for i in range(XY)]
    spread = lax.all_to_all(spread, ("dp", "pool"), 0, 0, axis_index_groups=near)
    gain_grad = jnp.sum(spread, axis=0)

    zeros = jnp.zeros(half, F32)
    plus2 = (
        plus2.astype(F32) + from_left[:ROWS].astype(F32)
        + jnp.concatenate([far_left.astype(F32), zeros])
    ).astype(BF16)
    minus2 = (
        minus2.astype(F32) + from_right[:ROWS].astype(F32)
        + jnp.concatenate([zeros, far_right.astype(F32)])
    ).astype(BF16)
    two_left = shift(plus2, 2)
    two_right = shift(minus2, -2)
    pool_grad = (
        kept.astype(F32) + from_left[ROWS:].astype(F32) + from_right[ROWS:].astype(F32)
        + two_left.astype(F32) + two_right.astype(F32)
    )

    query_grad, key_grad, value_grad = call(
        backward_kernel,
        [VMEM] * 6,
        [(token, BF16)] * 3,
        [],
        pl.CostEstimate(flops=2 * 10**9, bytes_accessed=8 * 10**6, transcendentals=0),
    )(dmixed, query_act, key_act, value_act, attend, slope)
    return (query_grad, key_grad, value_grad, gate_grad, pool_grad, gain_grad)


def solution(mesh):
    rows = P(("dp", "pool"), None)
    flat = P(("dp", "pool"))
    in_specs = (rows, rows, rows, rows, rows, flat, rows, flat, P())
    out_specs = (rows, rows, rows, rows, rows, P())
    return jax.shard_map(body, mesh=mesh, in_specs=in_specs, out_specs=out_specs, check_vma=False)
```

time: 183 us -> 124 us (0.68)
  blocking collectives: 118 us -> 0 us
  starting transfers between devices: 0.08 us -> 79 us
  waiting for transfers between devices: 21.6 us -> 6.19 us
  between operations: 14.9 us -> 0.99 us
  matrix products: 13.6 us -> 0 us
  local copies, waits for them, and re-layouts: 9.28 us -> 21.6 us
  Pallas kernels: 0 us -> 9.38 us
    psum x1 -> x0, blocking collectives: 101 us -> none  [body(): gain_grad = lax.psum(gain_part, ('dp', 'pool'))]
    ppermute x0 -> x14, starting transfers between devices: none -> 54.9 us  [shift(): lax.ppermute(value, 'pool', [(i, (i + by) % RING) for i in range(RING)])]
    all_to_all x0 -> x3, starting transfers between devices: none -> 24.1 us  [the longest x1 10.3 us: body(): lax.all_to_all(spread, ('dp', 'pool'), 0, 0, axis_index_groups=near)]
    all_gather x1 -> x0, waiting for transfers between devices: 20.9 us -> none  [body(): lax.all_gather(pool_rows, 'pool', axis=0, tiled=True)]
    unnamed x1 -> x0, blocking collectives: 16.8 us -> none
    dot_general x9 -> x0, matrix products: 13.6 us -> none  [the longest x1 2.85 us: body(): jnp.einsum('thd,shd->hts', dmixed_h, values_all, preferred_element_type=j...]
    unnamed x30 -> x56, local copies, waits for them, and re-layouts: 5.03 us -> 18.6 us
    pallas_call x0 -> x3, Pallas kernels: none -> 9.38 us  [the longest x1 4.15 us: body(): call(pool_kernel, [SMEM, SMEM] + [VMEM] * 16, [((2 * ROWS, WIDTH), BF16),...]
  transfers between devices with their start and end apart: 2 -> 17, of which waited for: 1 -> 3; matrix products, arithmetic and copies ran while one was open for 11% -> 5% of each run, Pallas kernels for 0% -> 4%
where the time goes in v1:
time: 124 us; the launch traced here: 123 us
  starting transfers between devices  79 us (64%)
  local copies, waits for them, and re-layouts  21.6 us (17%)
  Pallas kernels  9.38 us (8%)
  waiting for transfers between devices  6.19 us (5%)
  other arithmetic  5.68 us (5%)
    ppermute x14, starting transfers between devices, shift(): lax.ppermute(value, 'pool', [(i, (i + by) % RING) for i in range(RING)])  54.9 us
    unnamed x56, local copies, waits for them, and re-layouts  18.6 us
    all_to_all x1, starting transfers between devices, body(): lax.all_to_all(spread, ('dp', 'pool'), 0, 0, axis_index_groups=near)  10.3 us
    all_to_all x1, starting transfers between devices, body(): spread = lax.all_to_all(part, 'dp', 0, 0, axis_index_groups=plane)  9.8 us
    ppermute x14, waiting for transfers between devices, shift(): lax.ppermute(value, 'pool', [(i, (i + by) % RING) for i in range(RING)])  4.71 us
    pallas_call x1, Pallas kernels, body(): call(pool_kernel, [SMEM, SMEM] + [VMEM] * 16, [((2 * ROWS, WIDTH), BF16),...  4.15 us
    all_to_all x1, starting transfers between devices, body(): lax.all_to_all(jnp.broadcast_to(pool_ids[None, :], (RING, ROWS)), 'pool',...  3.94 us
    pallas_call x1, Pallas kernels, body(): call(backward_kernel, [VMEM] * 6, [(token, BF16)] * 3, [], pl.CostEstimat...  2.83 us
  transfers between devices with their start and end apart: 17, of which 3 were waited for; matrix products, arithmetic and copies ran while one was open for 5% of the time, Pallas kernels for 4%

profile of v1, /device:TPU:1, one launch (start us, length us, event | category | flops | bytes accessed | tf_op | source)
XLA Modules:
  0.0 122.8 jit_solution(13124433309785912970)
XLA Ops:
  0.6 6.6 %collective-permute-start.1 = (bf16[96,1024]{1,0:T(8,128)(2,1)}, bf16[96,1024]{1,0:T(8,128)(2,1)S(1)}, u32[]{:S(2)}, u32[]{:S(2)}) collective-permute-start(bf16[96,1024]{1,0:T(8,128)(2,1)} %own.1), channel_id=1, source_target_pairs={{0,2},{1,3},{2,4},{3,5},{4,6},{5,7},{6,0},{7,1},{8,10},{9,11},{10,... | collective-permute-start | bytes 589832 | tf_op jit(solution)/shard_map/ppermute | solution.py:170
  7.3 6.8 %collective-permute-start.4 = (bf16[96,1024]{1,0:T(8,128)(2,1)}, bf16[96,1024]{1,0:T(8,128)(2,1)S(1)}, u32[]{:S(2)}, u32[]{:S(2)}) collective-permute-start(bf16[96,1024]{1,0:T(8,128)(2,1)} %own.1), channel_id=1, source_target_pairs={{0,6},{1,7},{2,0},{3,1},{4,2},{5,3},{6,4},{7,5},{8,14},{9,15},{10,... | collective-permute-start | bytes 589832 | tf_op jit(solution)/shard_map/ppermute | solution.py:170
  14.1 4.3 %collective-permute-start.3 = (bf16[96,1024]{1,0:T(8,128)(2,1)}, bf16[96,1024]{1,0:T(8,128)(2,1)S(1)}, u32[]{:S(2)}, u32[]{:S(2)}) collective-permute-start(bf16[96,1024]{1,0:T(8,128)(2,1)} %own.1), channel_id=1, source_target_pairs={{0,7},{1,0},{2,1},{3,2},{4,3},{5,4},{6,5},{7,6},{8,15},{9,8},{10,9... | collective-permute-start | bytes 589832 | tf_op jit(solution)/shard_map/ppermute | solution.py:170
  18.3 1.9 %collective-permute-start = (bf16[96,1024]{1,0:T(8,128)(2,1)}, bf16[96,1024]{1,0:T(8,128)(2,1)S(1)}, u32[]{:S(2)}, u32[]{:S(2)}) collective-permute-start(bf16[96,1024]{1,0:T(8,128)(2,1)} %own.1), channel_id=1, source_target_pairs={{0,1},{1,2},{2,3},{3,4},{4,5},{5,6},{6,7},{7,0},{8,9},{9,10},{10,1... | collective-permute-start | bytes 589832 | tf_op jit(solution)/shard_map/ppermute | solution.py:170
  21.5 3.9 %all-to-all-start = ((s32[8,1,96]{2,1,0:T(1,128)}), s32[8,1,96]{2,1,0:T(1,128)S(1)}, u32[]{:S(2)}, u32[]{:S(2)}) async-start(s32[8,1,96]{2,1,0:T(1,128)} %broadcast_in_dim.4), calls=%async_computation | async-start | bytes 8192 | tf_op jit(solution)/shard_map/all_to_all | solution.py:183
  25.5 3.4 %collective-permute-start.2 = (bf16[96,1024]{1,0:T(8,128)(2,1)S(1)}, bf16[96,1024]{1,0:T(8,128)(2,1)S(1)}, u32[]{:S(2)}, u32[]{:S(2)}) collective-permute-start(bf16[96,1024]{1,0:T(8,128)(2,1)S(1)} %collective-permute-done.1.r2), channel_id=1, source_target_pairs={{0,1},{1,2},{2,3},{3,4},{4,5},{5,6},{6,7},{7,0},{8,9},{9,10},{10,1... | collective-permute-start | bytes 589832 | tf_op jit(solution)/shard_map/ppermute | solution.py:170
  28.8 3.1 %collective-permute-start.5 = (bf16[96,1024]{1,0:T(8,128)(2,1)S(1)}, bf16[96,1024]{1,0:T(8,128)(2,1)S(1)}, u32[]{:S(2)}, u32[]{:S(2)}) collective-permute-start(bf16[96,1024]{1,0:T(8,128)(2,1)S(1)} %collective-permute-done.4.l2), channel_id=1, source_target_pairs={{0,7},{1,0},{2,1},{3,2},{4,3},{5,4},{6,5},{7,6},{8,15},{9,8},{10,9... | collective-permute-start | bytes 589832 | tf_op jit(solution)/shard_map/ppermute | solution.py:170
  37.5 2.4 %shard_map.136 = (bf16[256,1024]{1,0:T(8,128)(2,1)S(1)}, f32[256,1024]{1,0:T(8,128)S(1)}, f32[256,128]{1,0:T(8,128)S(1)}, bf16[8,256,256]{2,1,0:T(8,128)(2,1)S(1)}, f32[8,256,256]{2,1,0:T(8,128)S(1)}) custom-call(s32[1,4]{1,0:T(1,128)S(1)} %copy-done.13, bf16[256,1024]{1,0:T(8,128)(2,1)S(1)} %copy-done.2, bf16[256,1024]{1,0:T(8,128)(2,1)S(1)} %copy-done.4, ...), custom_call_target="tpu_custom_call" | custom-call | flops 2000000000 | bytes 8000000 | tf_op jit(solution)/shard_map/pallas_call | solution.py:189
  44.9 3.0 %collective-permute-start.6 = (bf16[48,1024]{1,0:T(8,128)(2,1)S(1)}, bf16[48,1024]{1,0:T(8,128)(2,1)S(1)}, u32[]{:S(2)}, u32[]{:S(2)}) collective-permute-start(bf16[48,1024]{1,0:T(8,128)(2,1)S(1)} %slice.24), channel_id=1, source_target_pairs={{0,2},{1,3},{2,4},{3,5},{4,6},{5,7},{6,0},{7,1},{8,10},{9,11},{10,... | collective-permute-start | bytes 294920 | tf_op jit(solution)/shard_map/ppermute | solution.py:170
  48.0 4.4 %collective-permute-start.7 = (bf16[48,1024]{1,0:T(8,128)(2,1)S(1)}, bf16[48,1024]{1,0:T(8,128)(2,1)S(1)}, u32[]{:S(2)}, u32[]{:S(2)}) collective-permute-start(bf16[48,1024]{1,0:T(8,128)(2,1)S(1)} %slice.25), channel_id=1, source_target_pairs={{0,6},{1,7},{2,0},{3,1},{4,2},{5,3},{6,4},{7,5},{8,14},{9,15},{10,... | collective-permute-start | bytes 294920 | tf_op jit(solution)/shard_map/ppermute | solution.py:170
  53.4 3.8 %collective-permute-done.7.far_b = bf16[48,1024]{1,0:T(8,128)(2,1)S(1)} collective-permute-done((bf16[48,1024]{1,0:T(8,128)(2,1)S(1)}, bf16[48,1024]{1,0:T(8,128)(2,1)S(1)}, u32[]{:S(2)}, u32[]{:S(2)}) %collective-permute-start.7) | collective-permute-done | bytes 98336 | tf_op jit(solution)/shard_map/ppermute | solution.py:170
  61.9 4.2 %shard_map.137 = (bf16[192,1024]{1,0:T(8,128)(2,1)S(1)}, bf16[192,1024]{1,0:T(8,128)(2,1)S(1)}, bf16[48,1024]{1,0:T(8,128)(2,1)}, bf16[48,1024]{1,0:T(8,128)(2,1...) custom-call(s32[1]{0:T(128)} %bitcast.place, ...), custom_call_target="tpu_custom_call" | custom-call | flops 2000000000 | bytes 8000000 | tf_op jit(solution)/shard_map/pallas_call | solution.py:200
  66.8 2.1 %collective-permute-start.8 = (bf16[192,1024]{1,0:T(8,128)(2,1)S(1)}, bf16[192,1024]{1,0:T(8,128)(2,1)}, u32[]{:S(2)}, u32[]{:S(2)}) collective-permute-start(bf16[192,1024]{1,0:T(8,128)(2,1)S(1)} %get-tuple-element.35), channel_id=1, source_target_pairs={{0,1},{1,2},{2,3},{3,4},{4,5},{5,6},{6,7},{7,0},{8,9},{9,10},{10,1... | collective-permute-start | bytes 1179656 | tf_op jit(solution)/shard_map/ppermute | solution.py:170
  68.9 4.6 %collective-permute-start.9 = (bf16[192,1024]{1,0:T(8,128)(2,1)S(1)}, bf16[192,1024]{1,0:T(8,128)(2,1)}, u32[]{:S(2)}, u32[]{:S(2)}) collective-permute-start(bf16[192,1024]{1,0:T(8,128)(2,1)S(1)} %get-tuple-element.36), channel_id=1, source_target_pairs={{0,7},{1,0},{2,1},{3,2},{4,3},{5,4},{6,5},{7,6},{8,15},{9,8},{10,9... | collective-permute-start | bytes 1179656 | tf_op jit(solution)/shard_map/ppermute | solution.py:170
  73.5 4.4 %collective-permute-start.10 = (bf16[48,1024]{1,0:T(8,128)(2,1)}, bf16[48,1024]{1,0:T(8,128)(2,1)}, u32[]{:S(2)}, u32[]{:S(2)}) collective-permute-start(bf16[48,1024]{1,0:T(8,128)(2,1)} %get-tuple-element.38), channel_id=1, source_target_pairs={{0,2},{1,3},{2,4},{3,5},{4,6},{5,7},{6,0},{7,1},{8,10},{9,11},{10,... | collective-permute-start | bytes 294920 | tf_op jit(solution)/shard_map/ppermute | solution.py:170
  77.8 3.0 %collective-permute-start.12 = (bf16[48,1024]{1,0:T(8,128)(2,1)}, bf16[48,1024]{1,0:T(8,128)(2,1)}, u32[]{:S(2)}, u32[]{:S(2)}) collective-permute-start(bf16[48,1024]{1,0:T(8,128)(2,1)} %get-tuple-element.40), channel_id=1, source_target_pairs={{0,6},{1,7},{2,0},{3,1},{4,2},{5,3},{6,4},{7,5},{8,14},{9,15},{10,... | collective-permute-start | bytes 294920 | tf_op jit(solution)/shard_map/ppermute | solution.py:170
  81.7 9.8 %all-to-all-start.1 = ((f32[32,1,1024]{2,1,0:T(1,128)}), f32[32,1,1024]{2,1,0:T(1,128)}, u32[]{:S(2)}, u32[]{:S(2)}) async-start(f32[32,1,1024]{2,1,0:T(1,128)} %copy.21), calls=%async_computation.1 | async-start | bytes 262144 | tf_op jit(solution)/shard_map/all_to_all | solution.py:218
  92.6 3.1 %collective-permute-start.11 = (bf16[96,1024]{1,0:T(8,128)(2,1)S(1)}, bf16[96,1024]{1,0:T(8,128)(2,1)S(1)}, u32[]{:S(2)}, u32[]{:S(2)}) collective-permute-start(bf16[96,1024]{1,0:T(8,128)(2,1)S(1)} %add_convert_fusion.1), channel_id=1, source_target_pairs={{0,2},{1,3},{2,4},{3,5},{4,6},{5,7},{6,0},{7,1},{8,10},{9,11},{10,... | collective-permute-start | bytes 589832 | tf_op jit(solution)/shard_map/ppermute | solution.py:170
  96.8 4.2 %collective-permute-start.13 = (bf16[96,1024]{1,0:T(8,128)(2,1)S(1)}, bf16[96,1024]{1,0:T(8,128)(2,1)S(1)}, u32[]{:S(2)}, u32[]{:S(2)}) collective-permute-start(bf16[96,1024]{1,0:T(8,128)(2,1)S(1)} %add_convert_fusion), channel_id=1, source_target_pairs={{0,6},{1,7},{2,0},{3,1},{4,2},{5,3},{6,4},{7,5},{8,14},{9,15},{10,... | collective-permute-start | bytes 589832 | tf_op jit(solution)/shard_map/ppermute | solution.py:170
  102.7 10.3 %all-to-all-start.2 = ((f32[16,1,1024]{2,1,0:T(1,128)}), f32[16,1,1024]{2,1,0:T(1,128)S(1)}, u32[]{:S(2)}, u32[]{:S(2)}) async-start(f32[16,1,1024]{2,1,0:T(1,128)} %broadcast_in_dim.5), calls=%async_computation.2 | async-start | bytes 131072 | tf_op jit(solution)/shard_map/all_to_all | solution.py:221
  113.1 1.6 %copy-done.16 = f32[8,256,256]{2,1,0:T(8,128)S(1)} copy-done((f32[8,256,256]{2,1,0:T(8,128)S(1)}, f32[8,256,256]{2,1,0:T(8,128)}, u32[]{:S(2)}) %copy-start.16) | copy-done | bytes 2097176
  115.9 2.8 %shard_map.138 = (bf16[256,1024]{1,0:T(8,128)(2,1)}, bf16[256,1024]{1,0:T(8,128)(2,1)}, bf16[256,1024]{1,0:T(8,128)(2,1)}) custom-call(bf16[256,1024]{1,0:T(8,128)(2,1)S(1)} %copy-done.20, bf16[256,1024]{1,0:T(8,128)(2,1)S(1)} %copy-done.3, bf16[256,1024]{1,0:T(8,128)(2,1)S(1)} %copy-done.5, bf16[256,1024]{1,0:T(8,128)(2,1)S(1)} %copy-done.7, ...), custom_call_target="tpu_custom_call" | custom-call | flops 2000000000 | bytes 8000000 | tf_op jit(solution)/shard_map/pallas_call | solution.py:240
  118.8 1.5 %all-to-all-done.2 = f32[16,1,1024]{2,1,0:T(1,128)S(1)} async-done(((f32[16,1,1024]{2,1,0:T(1,128)}), f32[16,1,1024]{2,1,0:T(1,128)S(1)}, u32[]{:S(2)}, u32[]{:S(2)}) %all-to-all-start.2) | async-done | bytes 65568 | tf_op jit(solution)/shard_map/all_to_all | solution.py:221
  120.9 1.9 %convert_add_fusion = f32[96,1024]{1,0:T(8,128)} fusion(bf16[96,1024]{1,0:T(8,128)(2,1)S(1)} %collective-permute-done.13, bf16[96,1024]{1,0:T(8,128)(2,1)S(1)} %collective-permute-done.11, bf16[96,1024]{1,0:T(8,128)(2,1)S(1)} %get-tuple-element.34, bf16[192,1024]{1,0:T(8,128)(2,1)} %collective-permute-done.9, bf16[192,1024]{1,0:T(8,128)(2,1)} %collective-permute-done.8), kind=kLoop, calls=%fused_computation | loop fusion | flops 884736 | bytes 1376256 | tf_op jit(solution)/shard_map/add | solution.py:236
  (82 shorter events, 24.7 us)
Async XLA Ops:
  0.6 24.8 %collective-permute-start.1 = (bf16[96,1024]{1,0:T(8,128)(2,1)}, bf16[96,1024]{1,0:T(8,128)(2,1)S(1)}, u32[]{:S(2)}, u32[]{:S(2)}) collective-permute-start(bf16[96,1024]{1,0:T(8,128)(2,1)} %own.1), channel_id=1, source_target_pairs={{0,2},{1,3},{2,4},{3,5},{4,6},{5,7},{6,0},{7,1},{8,10},{9,11},{10,... | collective-permute-start | bytes 589832 | tf_op jit(solution)/shard_map/ppermute | solution.py:170
  7.3 21.6 %collective-permute-start.4 = (bf16[96,1024]{1,0:T(8,128)(2,1)}, bf16[96,1024]{1,0:T(8,128)(2,1)S(1)}, u32[]{:S(2)}, u32[]{:S(2)}) collective-permute-start(bf16[96,1024]{1,0:T(8,128)(2,1)} %own.1), channel_id=1, source_target_pairs={{0,6},{1,7},{2,0},{3,1},{4,2},{5,3},{6,4},{7,5},{8,14},{9,15},{10,... | collective-permute-start | bytes 589832 | tf_op jit(solution)/shard_map/ppermute | solution.py:170
  14.1 33.9 %collective-permute-start.3 = (bf16[96,1024]{1,0:T(8,128)(2,1)}, bf16[96,1024]{1,0:T(8,128)(2,1)S(1)}, u32[]{:S(2)}, u32[]{:S(2)}) collective-permute-start(bf16[96,1024]{1,0:T(8,128)(2,1)} %own.1), channel_id=1, source_target_pairs={{0,7},{1,0},{2,1},{3,2},{4,3},{5,4},{6,5},{7,6},{8,15},{9,8},{10,9... | collective-permute-start | bytes 589832 | tf_op jit(solution)/shard_map/ppermute | solution.py:170
  18.3 34.1 %collective-permute-start = (bf16[96,1024]{1,0:T(8,128)(2,1)}, bf16[96,1024]{1,0:T(8,128)(2,1)S(1)}, u32[]{:S(2)}, u32[]{:S(2)}) collective-permute-start(bf16[96,1024]{1,0:T(8,128)(2,1)} %own.1), channel_id=1, source_target_pairs={{0,1},{1,2},{2,3},{3,4},{4,5},{5,6},{6,7},{7,0},{8,9},{9,10},{10,1... | collective-permute-start | bytes 589832 | tf_op jit(solution)/shard_map/ppermute | solution.py:170
  21.5 30.8 %all-to-all-start = ((s32[8,1,96]{2,1,0:T(1,128)}), s32[8,1,96]{2,1,0:T(1,128)S(1)}, u32[]{:S(2)}, u32[]{:S(2)}) async-start(s32[8,1,96]{2,1,0:T(1,128)} %broadcast_in_dim.4), calls=%async_computation | async-start | bytes 8192 | tf_op jit(solution)/shard_map/all_to_all | solution.py:183
  25.5 32.3 %collective-permute-start.2 = (bf16[96,1024]{1,0:T(8,128)(2,1)S(1)}, bf16[96,1024]{1,0:T(8,128)(2,1)S(1)}, u32[]{:S(2)}, u32[]{:S(2)}) collective-permute-start(bf16[96,1024]{1,0:T(8,128)(2,1)S(1)} %collective-permute-done.1.r2), channel_id=1, source_target_pairs={{0,1},{1,2},{2,3},{3,4},{4,5},{5,6},{6,7},{7,0},{8,9},{9,10},{10,1... | collective-permute-start | bytes 589832 | tf_op jit(solution)/shard_map/ppermute | solution.py:170
  28.8 28.9 %collective-permute-start.5 = (bf16[96,1024]{1,0:T(8,128)(2,1)S(1)}, bf16[96,1024]{1,0:T(8,128)(2,1)S(1)}, u32[]{:S(2)}, u32[]{:S(2)}) collective-permute-start(bf16[96,1024]{1,0:T(8,128)(2,1)S(1)} %collective-permute-done.4.l2), channel_id=1, source_target_pairs={{0,7},{1,0},{2,1},{3,2},{4,3},{5,4},{6,5},{7,6},{8,15},{9,8},{10,9... | collective-permute-start | bytes 589832 | tf_op jit(solution)/shard_map/ppermute | solution.py:170
  37.5 20.3 %copy-start.8 = (bf16[96,1024]{1,0:T(8,128)(2,1)S(1)}, bf16[96,1024]{1,0:T(8,128)(2,1)}, u32[]{:S(2)}) copy-start(bf16[96,1024]{1,0:T(8,128)(2,1)} %own.1) | copy-start | bytes 589828
  37.5 20.3 %copy-start.12 = (f32[1024]{0:T(1024)S(1)}, f32[1024]{0:T(1024)}, u32[]{:S(2)}) copy-start(f32[1024]{0:T(1024)} %param.17) | copy-start | bytes 12292
  37.5 20.3 %copy-start.14 = (s32[1,4]{1,0:T(1,128)S(1)}, s32[1,4]{1,0:T(1,128)}, u32[]{:S(2)}) copy-start(s32[1,4]{1,0:T(1,128)} %lengths.3) | copy-start | bytes 52
  44.9 8.5 %collective-permute-start.6 = (bf16[48,1024]{1,0:T(8,128)(2,1)S(1)}, bf16[48,1024]{1,0:T(8,128)(2,1)S(1)}, u32[]{:S(2)}, u32[]{:S(2)}) collective-permute-start(bf16[48,1024]{1,0:T(8,128)(2,1)S(1)} %slice.24), channel_id=1, source_target_pairs={{0,2},{1,3},{2,4},{3,5},{4,6},{5,7},{6,0},{7,1},{8,10},{9,11},{10,... | collective-permute-start | bytes 294920 | tf_op jit(solution)/shard_map/ppermute | solution.py:170
  48.0 9.2 %collective-permute-start.7 = (bf16[48,1024]{1,0:T(8,128)(2,1)S(1)}, bf16[48,1024]{1,0:T(8,128)(2,1)S(1)}, u32[]{:S(2)}, u32[]{:S(2)}) collective-permute-start(bf16[48,1024]{1,0:T(8,128)(2,1)S(1)} %slice.25), channel_id=1, source_target_pairs={{0,6},{1,7},{2,0},{3,1},{4,2},{5,3},{6,4},{7,5},{8,14},{9,15},{10,... | collective-permute-start | bytes 294920 | tf_op jit(solution)/shard_map/ppermute | solution.py:170
  66.8 46.3 %copy-start.3 = (bf16[256,1024]{1,0:T(8,128)(2,1)S(1)}, bf16[256,1024]{1,0:T(8,128)(2,1)}, u32[]{:S(2)}) copy-start(bf16[256,1024]{1,0:T(8,128)(2,1)} %q_ref.3) | copy-start | bytes 1572868
  66.8 46.3 %copy-start.5 = (bf16[256,1024]{1,0:T(8,128)(2,1)S(1)}, bf16[256,1024]{1,0:T(8,128)(2,1)}, u32[]{:S(2)}) copy-start(bf16[256,1024]{1,0:T(8,128)(2,1)} %k_ref.3) | copy-start | bytes 1572868
  66.8 46.3 %copy-start.7 = (bf16[256,1024]{1,0:T(8,128)(2,1)S(1)}, bf16[256,1024]{1,0:T(8,128)(2,1)}, u32[]{:S(2)}) copy-start(bf16[256,1024]{1,0:T(8,128)(2,1)} %v_ref.3) | copy-start | bytes 1572868
  66.8 46.3 %copy-start.20 = (bf16[256,1024]{1,0:T(8,128)(2,1)S(1)}, bf16[256,1024]{1,0:T(8,128)(2,1)}, u32[]{:S(2)}) copy-start(bf16[256,1024]{1,0:T(8,128)(2,1)} %copy-done.19) | copy-start | bytes 1572868
  66.8 24.7 %collective-permute-start.8 = (bf16[192,1024]{1,0:T(8,128)(2,1)S(1)}, bf16[192,1024]{1,0:T(8,128)(2,1)}, u32[]{:S(2)}, u32[]{:S(2)}) collective-permute-start(bf16[192,1024]{1,0:T(8,128)(2,1)S(1)} %get-tuple-element.35), channel_id=1, source_target_pairs={{0,1},{1,2},{2,3},{3,4},{4,5},{5,6},{6,7},{7,0},{8,9},{9,10},{10,1... | collective-permute-start | bytes 1179656 | tf_op jit(solution)/shard_map/ppermute | solution.py:170
  68.9 26.8 %collective-permute-start.9 = (bf16[192,1024]{1,0:T(8,128)(2,1)S(1)}, bf16[192,1024]{1,0:T(8,128)(2,1)}, u32[]{:S(2)}, u32[]{:S(2)}) collective-permute-start(bf16[192,1024]{1,0:T(8,128)(2,1)S(1)} %get-tuple-element.36), channel_id=1, source_target_pairs={{0,7},{1,0},{2,1},{3,2},{4,3},{5,4},{6,5},{7,6},{8,15},{9,8},{10,9... | collective-permute-start | bytes 1179656 | tf_op jit(solution)/shard_map/ppermute | solution.py:170
  73.5 18.0 %collective-permute-start.10 = (bf16[48,1024]{1,0:T(8,128)(2,1)}, bf16[48,1024]{1,0:T(8,128)(2,1)}, u32[]{:S(2)}, u32[]{:S(2)}) collective-permute-start(bf16[48,1024]{1,0:T(8,128)(2,1)} %get-tuple-element.38), channel_id=1, source_target_pairs={{0,2},{1,3},{2,4},{3,5},{4,6},{5,7},{6,0},{7,1},{8,10},{9,11},{10,... | collective-permute-start | bytes 294920 | tf_op jit(solution)/shard_map/ppermute | solution.py:170
  77.8 17.9 %collective-permute-start.12 = (bf16[48,1024]{1,0:T(8,128)(2,1)}, bf16[48,1024]{1,0:T(8,128)(2,1)}, u32[]{:S(2)}, u32[]{:S(2)}) collective-permute-start(bf16[48,1024]{1,0:T(8,128)(2,1)} %get-tuple-element.40), channel_id=1, source_target_pairs={{0,6},{1,7},{2,0},{3,1},{4,2},{5,3},{6,4},{7,5},{8,14},{9,15},{10,... | collective-permute-start | bytes 294920 | tf_op jit(solution)/shard_map/ppermute | solution.py:170
  81.7 19.4 %all-to-all-start.1 = ((f32[32,1,1024]{2,1,0:T(1,128)}), f32[32,1,1024]{2,1,0:T(1,128)}, u32[]{:S(2)}, u32[]{:S(2)}) async-start(f32[32,1,1024]{2,1,0:T(1,128)} %copy.21), calls=%async_computation.1 | async-start | bytes 262144 | tf_op jit(solution)/shard_map/all_to_all | solution.py:218
  92.6 28.3 %collective-permute-start.11 = (bf16[96,1024]{1,0:T(8,128)(2,1)S(1)}, bf16[96,1024]{1,0:T(8,128)(2,1)S(1)}, u32[]{:S(2)}, u32[]{:S(2)}) collective-permute-start(bf16[96,1024]{1,0:T(8,128)(2,1)S(1)} %add_convert_fusion.1), channel_id=1, source_target_pairs={{0,2},{1,3},{2,4},{3,5},{4,6},{5,7},{6,0},{7,1},{8,10},{9,11},{10,... | collective-permute-start | bytes 589832 | tf_op jit(solution)/shard_map/ppermute | solution.py:170
  96.8 24.1 %collective-permute-start.13 = (bf16[96,1024]{1,0:T(8,128)(2,1)S(1)}, bf16[96,1024]{1,0:T(8,128)(2,1)S(1)}, u32[]{:S(2)}, u32[]{:S(2)}) collective-permute-start(bf16[96,1024]{1,0:T(8,128)(2,1)S(1)} %add_convert_fusion), channel_id=1, source_target_pairs={{0,6},{1,7},{2,0},{3,1},{4,2},{5,3},{6,4},{7,5},{8,14},{9,15},{10,... | collective-permute-start | bytes 589832 | tf_op jit(solution)/shard_map/ppermute | solution.py:170
  102.7 17.5 %all-to-all-start.2 = ((f32[16,1,1024]{2,1,0:T(1,128)}), f32[16,1,1024]{2,1,0:T(1,128)S(1)}, u32[]{:S(2)}, u32[]{:S(2)}) async-start(f32[16,1,1024]{2,1,0:T(1,128)} %broadcast_in_dim.5), calls=%async_computation.2 | async-start | bytes 131072 | tf_op jit(solution)/shard_map/all_to_all | solution.py:221
  (21 other events, 46.2 us)

commit v2 on v1

v2 whole, which is shorter than its diff:
```python
import jax
import jax.numpy as jnp
from jax import lax
from jax.experimental import pallas as pl
from jax.experimental.pallas import tpu as pltpu
from jax.sharding import PartitionSpec as P

HEADS = 8
LMAX = 192
EPSILON = 1e-05
COUNT = 256
WIDTH = 1024
HEAD_DIM = 128
ROWS = 96
RING = 8
POOL = ROWS * RING
LIMIT = 56 * 1024 * 1024
XY = 32
NEAR = 16

F32 = jnp.float32
BF16 = jnp.bfloat16
I32 = jnp.int32
CONTRACT_LAST = (((1,), (1,)), ((), ()))
CONTRACT_FIRST = (((0,), (0,)), ((), ()))


def dot(a, b, dims=(((1,), (0,)), ((), ()))):
    return lax.dot_general(a, b, dims, preferred_element_type=F32)


def step_kernel(
    place, lengths, q_hbm, k_hbm, v_hbm, gate_hbm, gain_ref, target_ref, ids_ref,
    own, r1, r2, r3, l1, l2, l3, four,
    dq_hbm, dk_hbm, dv_hbm, gate_grad_hbm, part_ref,
    plus1, minus1, plus4, plus2, minus2, kept,
    q, k, v, gate, rows, attend, slope, mask, normed, inv, emb, logits, slopes, terms, back,
    dmixed, gate_grad, dq, dk, dv, came, went,
):
    z = place[0]

    def start_of(offset):
        return pl.multiple_of(lax.rem(z + offset + RING, RING) * ROWS, 16)

    def load(src, dst, i):
        copy = pltpu.make_async_copy(src, dst, came.at[i])
        copy.start()
        return copy

    stores = []

    def store(src, dst):
        copy = pltpu.make_async_copy(src, dst, went.at[len(stores)])
        copy.start()
        stores.append(copy)

    inputs = [load(*pair, i) for i, pair in enumerate(((q_hbm, q), (k_hbm, k), (v_hbm, v), (gate_hbm, gate)))]
    blocks = [
        load(ref, rows.at[pl.ds(start_of(offset), ROWS), :], 4 + i)
        for i, (offset, ref) in enumerate(
            ((0, own), (-1, r1), (-2, r2), (-3, r3), (1, l1), (2, l2), (3, l3), (4, four))
        )
    ]

    scaling = HEAD_DIM ** (-0.5)
    row = lax.broadcasted_iota(I32, (COUNT, COUNT), 0)
    col = lax.broadcasted_iota(I32, (COUNT, COUNT), 1)
    first = jnp.zeros((COUNT, COUNT), I32)
    finish = jnp.int32(0)
    for i in range(lengths.shape[1]):
        finish = finish + lengths[0, i]
        first = jnp.where(row >= finish, finish, first)
    mask[...] = jnp.where((col >= first) & (col <= row), F32(1.0 / LMAX), F32(0.0))
    for copy in inputs[:3]:
        copy.wait()
    for h in range(HEADS):
        lanes = slice(h * HEAD_DIM, (h + 1) * HEAD_DIM)
        scores = dot(q[:, lanes], k[:, lanes], CONTRACT_LAST) * scaling
        squash = 0.5 * jnp.tanh(0.5 * scores) + 0.5
        keep = mask[...]
        act = scores * squash
        weights = (act * keep).astype(BF16)
        attend[h] = weights
        slope[h] = (squash + act * (1.0 - squash)) * (keep * scaling)
        normed[:, lanes] = dot(weights, v[:, lanes])
    inputs[3].wait()
    gain = gain_ref[...]
    step = 32
    for i in range(COUNT // step):
        at = slice(i * step, (i + 1) * step)
        part = normed[at, :]
        center = part - jnp.mean(part, axis=1, keepdims=True)
        scale = lax.rsqrt(jnp.mean(center * center, axis=1, keepdims=True) + EPSILON)
        unit = center * scale
        normed[at, :] = unit
        inv[at, :] = jnp.broadcast_to(scale, (step, HEAD_DIM))
        emb[at, :] = (unit * gain * gate[at, :].astype(F32)).astype(BF16)

    for copy in blocks:
        copy.wait()
    logits[...] = dot(emb[...], rows[...], CONTRACT_LAST)
    ids = ids_ref[...]
    for i in range(COUNT // step):
        at = slice(i * step, (i + 1) * step)
        target = target_ref[at, :]
        column = lax.broadcasted_iota(I32, (step, POOL), 1)
        chosen = column == target
        own_id = jnp.sum(jnp.where(chosen, ids, F32(0)), axis=1, keepdims=True)
        token = lax.broadcasted_iota(I32, (step, 1), 0) + i * step
        usable = jnp.ones((step, 1), F32)
        finish = jnp.int32(0)
        for j in range(lengths.shape[1]):
            finish = finish + lengths[0, j]
            usable = jnp.where(token + 1 == finish, F32(0.0), usable)
        clash = (ids == own_id) & jnp.logical_not(chosen)
        masked = jnp.where(clash, F32(-1e30), logits[at, :])
        peak = jnp.max(masked, axis=1, keepdims=True)
        weight = jnp.where(clash, F32(0.0), jnp.exp(masked - peak))
        total = jnp.sum(weight, axis=1, keepdims=True)
        probs = weight * (1.0 / total)
        slopes[at, :] = (usable * jnp.where(chosen, probs - 1.0, probs)).astype(BF16)

    terms[...] = dot(slopes[...], emb[...], CONTRACT_FIRST).astype(BF16)
    for offset, ref in (
        (3, plus1.at[0:ROWS]), (1, plus1.at[ROWS : 2 * ROWS]),
        (-3, minus1.at[0:ROWS]), (-1, minus1.at[ROWS : 2 * ROWS]),
        (4, plus4), (2, plus2), (-2, minus2), (0, kept),
    ):
        store(terms.at[pl.ds(start_of(offset), ROWS), :], ref)

    back[...] = dot(slopes[...], rows[...])
    sums = jnp.zeros((8, WIDTH), F32)
    for i in range(COUNT // step):
        at = slice(i * step, (i + 1) * step)
        unit = normed[at, :]
        pulled = back[at, :]
        gate_grad[at, :] = (pulled * (unit * gain)).astype(BF16)
        dscaled = pulled * gate[at, :].astype(F32)
        product = dscaled * unit
        sums = sums + jnp.sum(product.reshape(step // 8, 8, WIDTH), axis=0)
        dnormed = dscaled * gain
        mean1 = jnp.mean(dnormed, axis=1, keepdims=True)
        mean2 = jnp.mean(product * gain, axis=1, keepdims=True)
        dmixed[at, :] = ((dnormed - mean1 - unit * mean2) * inv[at, 0:1]).astype(BF16)
    store(gate_grad, gate_grad_hbm)
    part = jnp.sum(sums, axis=0, keepdims=True)
    for i in range(XY):
        part_ref[i] = part

    for h in range(HEADS):
        lanes = slice(h * HEAD_DIM, (h + 1) * HEAD_DIM)
        part = dmixed[:, lanes]
        dattend = dot(part, v[:, lanes], CONTRACT_LAST)
        dscores = (dattend * slope[h]).astype(BF16)
        dv[:, lanes] = dot(attend[h], part, CONTRACT_FIRST).astype(BF16)
        dq[:, lanes] = dot(dscores, k[:, lanes]).astype(BF16)
        dk[:, lanes] = dot(dscores, q[:, lanes], CONTRACT_FIRST).astype(BF16)
        if h % 4 == 3:
            wide = slice((h - 3) * HEAD_DIM, (h + 1) * HEAD_DIM)
            for src, dst in ((dv, dv_hbm), (dq, dq_hbm), (dk, dk_hbm)):
                store(src.at[:, wide], dst.at[:, wide])
    for copy in stores:
        copy.wait()


VMEM = pl.BlockSpec(memory_space=pltpu.VMEM)
SMEM = pl.BlockSpec(memory_space=pltpu.SMEM)
ANY = pl.BlockSpec(memory_space=pl.ANY)


def shift(value, by):
    return lax.ppermute(value, "pool", [(i, (i + by) % RING) for i in range(RING)])


TOKEN = (COUNT, WIDTH)
CHUNK = (ROWS, WIDTH)
PAIR = (2 * ROWS, WIDTH)
SQUARES = (HEADS, COUNT, COUNT)
TABLE = (POOL, WIDTH)
OUTS = [
    (TOKEN, BF16, ANY), (TOKEN, BF16, ANY), (TOKEN, BF16, ANY), (TOKEN, BF16, ANY),
    ((XY, 1, WIDTH), F32, VMEM), (PAIR, BF16, ANY), (PAIR, BF16, ANY),
    (CHUNK, BF16, ANY), (CHUNK, BF16, ANY), (CHUNK, BF16, ANY), (CHUNK, BF16, ANY),
]
SCRATCH = [
    (TOKEN, BF16), (TOKEN, BF16), (TOKEN, BF16), (TOKEN, BF16), (TABLE, BF16),
    (SQUARES, BF16), (SQUARES, F32), ((COUNT, COUNT), F32), (TOKEN, F32), ((COUNT, HEAD_DIM), F32),
    (TOKEN, BF16), ((COUNT, POOL), F32), ((COUNT, POOL), BF16), (TABLE, BF16), (TOKEN, F32),
    (TOKEN, BF16), (TOKEN, BF16), (TOKEN, BF16), (TOKEN, BF16), (TOKEN, BF16),
]


def body(query_act, key_act, value_act, gate_act, lengths, targets, pool_rows, pool_ids, norm_gain):
    r2 = shift(pool_rows, 2)
    l2 = shift(pool_rows, -2)
    four = shift(pool_rows, 4)
    r1 = shift(pool_rows, 1)
    l1 = shift(pool_rows, -1)
    r3 = shift(r2, 1)
    l3 = shift(l2, -1)
    ids = lax.all_to_all(
        jnp.broadcast_to(pool_ids[None, None, :], (RING, 1, ROWS)), "pool", 0, 0, tiled=True
    ).reshape(1, POOL).astype(F32)
    place = lax.axis_index("pool").reshape(1).astype(I32)

    dq, dk, dv, gate_grad, part, plus1, minus1, plus4, plus2, minus2, kept = pl.pallas_call(
        step_kernel,
        out_shape=[jax.ShapeDtypeStruct(shape, kind) for shape, kind, _ in OUTS],
        in_specs=[SMEM, SMEM] + [ANY] * 4 + [VMEM] * 3 + [ANY] * 8,
        out_specs=[spec for _, _, spec in OUTS],
        scratch_shapes=[pltpu.VMEM(shape, kind) for shape, kind in SCRATCH]
        + [pltpu.SemaphoreType.DMA((12,)), pltpu.SemaphoreType.DMA((15,))],
        compiler_params=pltpu.CompilerParams(vmem_limit_bytes=LIMIT),
        cost_estimate=pl.CostEstimate(flops=2 * 10**9, bytes_accessed=8 * 10**6, transcendentals=720896),
    )(place, lengths, query_act, key_act, value_act, gate_act, norm_gain.reshape(1, WIDTH),
      targets.reshape(COUNT, 1), ids, pool_rows, r1, r2, r3, l1, l2, l3, four)

    from_left = shift(plus1, 1)
    from_right = shift(minus1, -1)
    from_far = shift(plus4, 4)

    plane = [[x * 16 + y * 2 + c for x in range(4) for y in range(8)] for c in range(2)]
    spread = lax.all_to_all(part, "dp", 0, 0, axis_index_groups=plane, tiled=True)
    spread = jnp.broadcast_to(jnp.sum(spread, axis=0, keepdims=True), (NEAR, 1, WIDTH))
    near = [[i * NEAR + j for j in range(NEAR)] for i in range(XY)]
    spread = lax.all_to_all(spread, ("dp", "pool"), 0, 0, axis_index_groups=near, tiled=True)
    gain_grad = jnp.sum(spread, axis=0).reshape(WIDTH)

    plus2 = (plus2.astype(F32) + from_left[:ROWS].astype(F32)).astype(BF16)
    minus2 = (minus2.astype(F32) + from_right[:ROWS].astype(F32)).astype(BF16)
    two_left = shift(plus2, 2)
    two_right = shift(minus2, -2)
    pool_grad = (
        kept.astype(F32) + from_left[ROWS:].astype(F32) + from_right[ROWS:].astype(F32)
        + from_far.astype(F32) + two_left.astype(F32) + two_right.astype(F32)
    )
    return (dq, dk, dv, gate_grad, pool_grad, gain_grad)


def solution(mesh):
    rows = P(("dp", "pool"), None)
    flat = P(("dp", "pool"))
    in_specs = (rows, rows, rows, rows, rows, flat, rows, flat, P())
    out_specs = (rows, rows, rows, rows, rows, P())
    return jax.shard_map(body, mesh=mesh, in_specs=in_specs, out_specs=out_specs, check_vma=False)
```

time: 124 us -> 105 us (0.85)
  local copies, waits for them, and re-layouts: 21.6 us -> 4.32 us
  blocking collectives: 0 us -> 16.1 us
  starting transfers between devices: 79 us -> 65.5 us
  other arithmetic: 5.68 us -> 1.79 us
    unnamed x56 -> x22, local copies, waits for them, and re-layouts: 18.6 us -> 1.59 us
    all_to_all x0 -> x1, blocking collectives: none -> 16.1 us  [body(): lax.all_to_all(spread, ('dp', 'pool'), 0, 0, axis_index_groups=near, tile...]
    all_to_all x3 -> x2, starting transfers between devices: 24.1 us -> 16.6 us  [the longest x1 9.68 us: body(): lax.all_to_all(part, 'dp', 0, 0, axis_index_groups=plane, tiled=True)]
    ppermute x14 -> x12, starting transfers between devices: 54.9 us -> 48.9 us  [shift(): lax.ppermute(value, 'pool', [(i, (i + by) % RING) for i in range(RING)])]
    ppermute x14 -> x12, waiting for transfers between devices: 4.71 us -> 0.03 us  [shift(): lax.ppermute(value, 'pool', [(i, (i + by) % RING) for i in range(RING)])]
    all_to_all x3 -> x2, waiting for transfers between devices: 1.49 us -> 4.98 us  [the longest x1 4.97 us: body(): lax.all_to_all(jnp.broadcast_to(pool_ids[None, None, :], (RING, 1, ROWS))...]
    convert_element_type x3, other arithmetic: 2.13 us -> 0.12 us  [the longest x1 0.05 us: body(): minus2 = (minus2.astype(F32) + from_right[:ROWS].astype(F32)).astype(BF16)]
    pallas_call x3 -> x1, Pallas kernels: 9.38 us -> 10.2 us  [body(): pl.pallas_call(step_kernel, out_shape=[jax.ShapeDtypeStruct(shape, kind)...]
  transfers between devices with their start and end apart: 17 -> 14, of which waited for: 3 -> 1; matrix products, arithmetic and copies ran while one was open for 5% -> 3% of each run, Pallas kernels for 4% -> 0%
where the time goes in v2:
time: 105 us; the launch traced here: 104 us
  starting transfers between devices  65.5 us (62%)
  blocking collectives  16.1 us (15%)
  Pallas kernels  10.2 us (10%)
  waiting for transfers between devices  5.01 us (5%)
  local copies, waits for them, and re-layouts  4.32 us (4%)
  other arithmetic  1.79 us (2%)
    ppermute x12, starting transfers between devices, shift(): lax.ppermute(value, 'pool', [(i, (i + by) % RING) for i in range(RING)])  48.9 us
    all_to_all x1, blocking collectives, body(): lax.all_to_all(spread, ('dp', 'pool'), 0, 0, axis_index_groups=near, tile...  16.1 us
    pallas_call x1, Pallas kernels, body(): pl.pallas_call(step_kernel, out_shape=[jax.ShapeDtypeStruct(shape, kind)...  10.2 us
    all_to_all x1, starting transfers between devices, body(): lax.all_to_all(part, 'dp', 0, 0, axis_index_groups=plane, tiled=True)  9.68 us
    all_to_all x1, starting transfers between devices, body(): lax.all_to_all(jnp.broadcast_to(pool_ids[None, None, :], (RING, 1, ROWS))...  6.91 us
    all_to_all x1, waiting for transfers between devices, body(): lax.all_to_all(jnp.broadcast_to(pool_ids[None, None, :], (RING, 1, ROWS))...  4.97 us
  transfers between devices with their start and end apart: 14, of which 1 were waited for; matrix products, arithmetic and copies ran while one was open for 3% of the time, Pallas kernels for 0%

profile of v2, /device:TPU:1, one launch (start us, length us, event | category | flops | bytes accessed | tf_op | source)
XLA Modules:
  0.0 103.9 jit_solution(9506097628758481028)
XLA Ops:
  0.6 11.5 %collective-permute-start.4 = (bf16[96,1024]{1,0:T(8,128)(2,1)}, bf16[96,1024]{1,0:T(8,128)(2,1)S(1)}, u32[]{:S(2)}, u32[]{:S(2)}) collective-permute-start(bf16[96,1024]{1,0:T(8,128)(2,1)} %own.1), channel_id=1, source_target_pairs={{0,6},{1,7},{2,0},{3,1},{4,2},{5,3},{6,4},{7,5},{8,14},{9,15},{10,... | collective-permute-start | bytes 589832 | tf_op jit(solution)/shard_map/ppermute | solution.py:172
  12.1 1.9 %collective-permute-start.1 = (bf16[96,1024]{1,0:T(8,128)(2,1)}, bf16[96,1024]{1,0:T(8,128)(2,1)S(1)}, u32[]{:S(2)}, u32[]{:S(2)}) collective-permute-start(bf16[96,1024]{1,0:T(8,128)(2,1)} %own.1), channel_id=1, source_target_pairs={{0,2},{1,3},{2,4},{3,5},{4,6},{5,7},{6,0},{7,1},{8,10},{9,11},{10,... | collective-permute-start | bytes 589832 | tf_op jit(solution)/shard_map/ppermute | solution.py:172
  14.1 5.5 %collective-permute-start.3 = (bf16[96,1024]{1,0:T(8,128)(2,1)}, bf16[96,1024]{1,0:T(8,128)(2,1)S(1)}, u32[]{:S(2)}, u32[]{:S(2)}) collective-permute-start(bf16[96,1024]{1,0:T(8,128)(2,1)} %own.1), channel_id=1, source_target_pairs={{0,7},{1,0},{2,1},{3,2},{4,3},{5,4},{6,5},{7,6},{8,15},{9,8},{10,9... | collective-permute-start | bytes 589832 | tf_op jit(solution)/shard_map/ppermute | solution.py:172
  19.6 1.9 %collective-permute-start = (bf16[96,1024]{1,0:T(8,128)(2,1)}, bf16[96,1024]{1,0:T(8,128)(2,1)S(1)}, u32[]{:S(2)}, u32[]{:S(2)}) collective-permute-start(bf16[96,1024]{1,0:T(8,128)(2,1)} %own.1), channel_id=1, source_target_pairs={{0,1},{1,2},{2,3},{3,4},{4,5},{5,6},{6,7},{7,0},{8,9},{9,10},{10,1... | collective-permute-start | bytes 589832 | tf_op jit(solution)/shard_map/ppermute | solution.py:172
  21.5 2.1 %collective-permute-start.6 = (bf16[96,1024]{1,0:T(8,128)(2,1)}, bf16[96,1024]{1,0:T(8,128)(2,1)S(1)}, u32[]{:S(2)}, u32[]{:S(2)}) collective-permute-start(bf16[96,1024]{1,0:T(8,128)(2,1)} %own.1), channel_id=1, source_target_pairs={{0,4},{1,5},{2,6},{3,7},{4,0},{5,1},{6,2},{7,3},{8,12},{9,13},{10,... | collective-permute-start | bytes 589832 | tf_op jit(solution)/shard_map/ppermute | solution.py:172
  23.6 4.4 %collective-permute-start.5 = (bf16[96,1024]{1,0:T(8,128)(2,1)S(1)}, bf16[96,1024]{1,0:T(8,128)(2,1)S(1)}, u32[]{:S(2)}, u32[]{:S(2)}) collective-permute-start(bf16[96,1024]{1,0:T(8,128)(2,1)S(1)} %collective-permute-done.4.l2), channel_id=1, source_target_pairs={{0,7},{1,0},{2,1},{3,2},{4,3},{5,4},{6,5},{7,6},{8,15},{9,8},{10,9... | collective-permute-start | bytes 589832 | tf_op jit(solution)/shard_map/ppermute | solution.py:172
  28.0 1.9 %collective-permute-start.2 = (bf16[96,1024]{1,0:T(8,128)(2,1)S(1)}, bf16[96,1024]{1,0:T(8,128)(2,1)S(1)}, u32[]{:S(2)}, u32[]{:S(2)}) collective-permute-start(bf16[96,1024]{1,0:T(8,128)(2,1)S(1)} %collective-permute-done.1.r2), channel_id=1, source_target_pairs={{0,1},{1,2},{2,3},{3,4},{4,5},{5,6},{6,7},{7,0},{8,9},{9,10},{10,1... | collective-permute-start | bytes 589832 | tf_op jit(solution)/shard_map/ppermute | solution.py:172
  30.0 1.3 %broadcast_in_dim.4 = s32[8,1,96]{2,1,0:T(1,128)} broadcast(s32[96]{0:T(128)} %param.16), dimensions={2} | broadcast | bytes 3456 | tf_op jit(solution)/shard_map/broadcast_in_dim | solution.py:202
  31.2 6.9 %all-to-all-start = ((s32[8,1,96]{2,1,0:T(1,128)}), s32[8,1,96]{2,1,0:T(1,128)S(1)}, u32[]{:S(2)}, u32[]{:S(2)}) async-start(s32[8,1,96]{2,1,0:T(1,128)} %broadcast_in_dim.4), calls=%async_computation | async-start | bytes 8192 | tf_op jit(solution)/shard_map/all_to_all | solution.py:201
  38.1 0.7 copy-done.3
  38.8 0.8 copy.18.target_ref
  39.6 5.0 %all-to-all-done = s32[8,1,96]{2,1,0:T(1,128)S(1)} async-done(((s32[8,1,96]{2,1,0:T(1,128)}), s32[8,1,96]{2,1,0:T(1,128)S(1)}, u32[]{:S(2)}, u32[]{:S(2)}) %all-to-all-start) | async-done | bytes 3104 | tf_op jit(solution)/shard_map/all_to_all | solution.py:201
  44.6 0.7 convert_element_type.42.ids_ref
  45.3 0.6 copy-done.6
  46.2 10.2 %shard_map.136 = (bf16[256,1024]{1,0:T(8,128)(2,1)}, bf16[256,1024]{1,0:T(8,128)(2,1)}, bf16[256,1024]{1,0:T(8,128)(2,1)}, bf16[256,1024]{1,0:T(8,128)(2,1)}, f3...) custom-call(s32[1]{0:T(128)} %bitcast.place, ...), custom_call_target="tpu_custom_call" | custom-call | flops 2000000000 | bytes 8000000 | tf_op jit(solution)/shard_map/pallas_call | solution.py:206
  56.5 2.5 %collective-permute-start.7 = (bf16[192,1024]{1,0:T(8,128)(2,1)}, bf16[192,1024]{1,0:T(8,128)(2,1)S(1)}, u32[]{:S(2)}, u32[]{:S(2)}) collective-permute-start(bf16[192,1024]{1,0:T(8,128)(2,1)} %get-tuple-element.22), channel_id=1, source_target_pairs={{0,1},{1,2},{2,3},{3,4},{4,5},{5,6},{6,7},{7,0},{8,9},{9,10},{10,1... | collective-permute-start | bytes 1179656 | tf_op jit(solution)/shard_map/ppermute | solution.py:172
  58.9 4.2 %collective-permute-start.8 = (bf16[192,1024]{1,0:T(8,128)(2,1)}, bf16[192,1024]{1,0:T(8,128)(2,1)S(1)}, u32[]{:S(2)}, u32[]{:S(2)}) collective-permute-start(bf16[192,1024]{1,0:T(8,128)(2,1)} %get-tuple-element.23), channel_id=1, source_target_pairs={{0,7},{1,0},{2,1},{3,2},{4,3},{5,4},{6,5},{7,6},{8,15},{9,8},{10,9... | collective-permute-start | bytes 1179656 | tf_op jit(solution)/shard_map/ppermute | solution.py:172
  63.1 9.7 %all-to-all-start.1 = ((f32[32,1,1024]{2,1,0:T(1,128)}), f32[32,1,1024]{2,1,0:T(1,128)S(1)}, u32[]{:S(2)}, u32[]{:S(2)}) async-start(f32[32,1,1024]{2,1,0:T(1,128)} %get-tuple-element.27), calls=%async_computation.1 | async-start | bytes 262144 | tf_op jit(solution)/shard_map/all_to_all | solution.py:223
  72.8 5.4 %collective-permute-start.9 = (bf16[96,1024]{1,0:T(8,128)(2,1)}, bf16[96,1024]{1,0:T(8,128)(2,1)S(1)}, u32[]{:S(2)}, u32[]{:S(2)}) collective-permute-start(bf16[96,1024]{1,0:T(8,128)(2,1)} %get-tuple-element.24), channel_id=1, source_target_pairs={{0,4},{1,5},{2,6},{3,7},{4,0},{5,1},{6,2},{7,3},{8,12},{9,13},{10,... | collective-permute-start | bytes 589832 | tf_op jit(solution)/shard_map/ppermute | solution.py:172
  78.2 2.1 %collective-permute-start.10 = (bf16[96,1024]{1,0:T(8,128)(2,1)S(1)}, bf16[96,1024]{1,0:T(8,128)(2,1)S(1)}, u32[]{:S(2)}, u32[]{:S(2)}) collective-permute-start(bf16[96,1024]{1,0:T(8,128)(2,1)S(1)} %add_convert_fusion.1), channel_id=1, source_target_pairs={{0,2},{1,3},{2,4},{3,5},{4,6},{5,7},{6,0},{7,1},{8,10},{9,11},{10,... | collective-permute-start | bytes 589832 | tf_op jit(solution)/shard_map/ppermute | solution.py:172
  80.4 5.6 %collective-permute-start.11 = (bf16[96,1024]{1,0:T(8,128)(2,1)S(1)}, bf16[96,1024]{1,0:T(8,128)(2,1)S(1)}, u32[]{:S(2)}, u32[]{:S(2)}) collective-permute-start(bf16[96,1024]{1,0:T(8,128)(2,1)S(1)} %add_convert_fusion), channel_id=1, source_target_pairs={{0,6},{1,7},{2,0},{3,1},{4,2},{5,3},{6,4},{7,5},{8,14},{9,15},{10,... | collective-permute-start | bytes 589832 | tf_op jit(solution)/shard_map/ppermute | solution.py:172
  86.2 16.1 %all_to_all.15 = f32[16,1,1024]{2,1,0:T(1,128)S(1)} all-to-all(f32[16,1,1024]{2,1,0:T(1,128)S(1)} %broadcast_in_dim.5), channel_id=1, replica_groups={{0,1,2,3,4,5,6,7,8,9,10,11,12,13,14,15},{16,17,18,19,20,21,22,23,24,25,..., dimensions={0} | all-to-all | bytes 131072 | tf_op jit(solution)/shard_map/all_to_all | solution.py:226
  102.3 0.6 reduce_sum.19
  103.0 0.9 convert_add_fusion
  (38 shorter events, 0.6 us)
Async XLA Ops:
  0.6 23.0 %collective-permute-start.4 = (bf16[96,1024]{1,0:T(8,128)(2,1)}, bf16[96,1024]{1,0:T(8,128)(2,1)S(1)}, u32[]{:S(2)}, u32[]{:S(2)}) collective-permute-start(bf16[96,1024]{1,0:T(8,128)(2,1)} %own.1), channel_id=1, source_target_pairs={{0,6},{1,7},{2,0},{3,1},{4,2},{5,3},{6,4},{7,5},{8,14},{9,15},{10,... | collective-permute-start | bytes 589832 | tf_op jit(solution)/shard_map/ppermute | solution.py:172
  12.1 15.9 %collective-permute-start.1 = (bf16[96,1024]{1,0:T(8,128)(2,1)}, bf16[96,1024]{1,0:T(8,128)(2,1)S(1)}, u32[]{:S(2)}, u32[]{:S(2)}) collective-permute-start(bf16[96,1024]{1,0:T(8,128)(2,1)} %own.1), channel_id=1, source_target_pairs={{0,2},{1,3},{2,4},{3,5},{4,6},{5,7},{6,0},{7,1},{8,10},{9,11},{10,... | collective-permute-start | bytes 589832 | tf_op jit(solution)/shard_map/ppermute | solution.py:172
  14.1 31.2 %collective-permute-start.3 = (bf16[96,1024]{1,0:T(8,128)(2,1)}, bf16[96,1024]{1,0:T(8,128)(2,1)S(1)}, u32[]{:S(2)}, u32[]{:S(2)}) collective-permute-start(bf16[96,1024]{1,0:T(8,128)(2,1)} %own.1), channel_id=1, source_target_pairs={{0,7},{1,0},{2,1},{3,2},{4,3},{5,4},{6,5},{7,6},{8,15},{9,8},{10,9... | collective-permute-start | bytes 589832 | tf_op jit(solution)/shard_map/ppermute | solution.py:172
  19.6 25.7 %collective-permute-start = (bf16[96,1024]{1,0:T(8,128)(2,1)}, bf16[96,1024]{1,0:T(8,128)(2,1)S(1)}, u32[]{:S(2)}, u32[]{:S(2)}) collective-permute-start(bf16[96,1024]{1,0:T(8,128)(2,1)} %own.1), channel_id=1, source_target_pairs={{0,1},{1,2},{2,3},{3,4},{4,5},{5,6},{6,7},{7,0},{8,9},{9,10},{10,1... | collective-permute-start | bytes 589832 | tf_op jit(solution)/shard_map/ppermute | solution.py:172
  21.5 23.8 %collective-permute-start.6 = (bf16[96,1024]{1,0:T(8,128)(2,1)}, bf16[96,1024]{1,0:T(8,128)(2,1)S(1)}, u32[]{:S(2)}, u32[]{:S(2)}) collective-permute-start(bf16[96,1024]{1,0:T(8,128)(2,1)} %own.1), channel_id=1, source_target_pairs={{0,4},{1,5},{2,6},{3,7},{4,0},{5,1},{6,2},{7,3},{8,12},{9,13},{10,... | collective-permute-start | bytes 589832 | tf_op jit(solution)/shard_map/ppermute | solution.py:172
  23.6 21.7 %copy-start.4 = (bf16[96,1024]{1,0:T(8,128)(2,1)}, bf16[96,1024]{1,0:T(8,128)(2,1)S(1)}, u32[]{:S(2)}) copy-start(bf16[96,1024]{1,0:T(8,128)(2,1)S(1)} %collective-permute-done.4.l2) | copy-start | bytes 589828
  23.6 21.7 %collective-permute-start.5 = (bf16[96,1024]{1,0:T(8,128)(2,1)S(1)}, bf16[96,1024]{1,0:T(8,128)(2,1)S(1)}, u32[]{:S(2)}, u32[]{:S(2)}) collective-permute-start(bf16[96,1024]{1,0:T(8,128)(2,1)S(1)} %collective-permute-done.4.l2), channel_id=1, source_target_pairs={{0,7},{1,0},{2,1},{3,2},{4,3},{5,4},{6,5},{7,6},{8,15},{9,8},{10,9... | collective-permute-start | bytes 589832 | tf_op jit(solution)/shard_map/ppermute | solution.py:172
  28.0 17.3 %copy-start.5 = (bf16[96,1024]{1,0:T(8,128)(2,1)}, bf16[96,1024]{1,0:T(8,128)(2,1)S(1)}, u32[]{:S(2)}) copy-start(bf16[96,1024]{1,0:T(8,128)(2,1)S(1)} %collective-permute-done.1.r2) | copy-start | bytes 589828
  28.0 17.3 %collective-permute-start.2 = (bf16[96,1024]{1,0:T(8,128)(2,1)S(1)}, bf16[96,1024]{1,0:T(8,128)(2,1)S(1)}, u32[]{:S(2)}, u32[]{:S(2)}) collective-permute-start(bf16[96,1024]{1,0:T(8,128)(2,1)S(1)} %collective-permute-done.1.r2), channel_id=1, source_target_pairs={{0,1},{1,2},{2,3},{3,4},{4,5},{5,6},{6,7},{7,0},{8,9},{9,10},{10,1... | collective-permute-start | bytes 589832 | tf_op jit(solution)/shard_map/ppermute | solution.py:172
  31.2 13.4 %all-to-all-start = ((s32[8,1,96]{2,1,0:T(1,128)}), s32[8,1,96]{2,1,0:T(1,128)S(1)}, u32[]{:S(2)}, u32[]{:S(2)}) async-start(s32[8,1,96]{2,1,0:T(1,128)} %broadcast_in_dim.4), calls=%async_computation | async-start | bytes 8192 | tf_op jit(solution)/shard_map/all_to_all | solution.py:201
  45.2 0.7 copy-start.6
  45.3 0.8 copy-start.7
  45.3 0.8 copy-start.8
  45.3 0.9 copy-start.9
  45.3 0.9 copy-start.10
  56.5 21.7 %copy-start.2 = (bf16[96,1024]{1,0:T(8,128)(2,1)S(1)}, bf16[96,1024]{1,0:T(8,128)(2,1)}, u32[]{:S(2)}) copy-start(bf16[96,1024]{1,0:T(8,128)(2,1)} %get-tuple-element.25) | copy-start | bytes 589828
  56.5 21.7 %collective-permute-start.7 = (bf16[192,1024]{1,0:T(8,128)(2,1)}, bf16[192,1024]{1,0:T(8,128)(2,1)S(1)}, u32[]{:S(2)}, u32[]{:S(2)}) collective-permute-start(bf16[192,1024]{1,0:T(8,128)(2,1)} %get-tuple-element.22), channel_id=1, source_target_pairs={{0,1},{1,2},{2,3},{3,4},{4,5},{5,6},{6,7},{7,0},{8,9},{9,10},{10,1... | collective-permute-start | bytes 1179656 | tf_op jit(solution)/shard_map/ppermute | solution.py:172
  58.9 21.4 %collective-permute-start.8 = (bf16[192,1024]{1,0:T(8,128)(2,1)}, bf16[192,1024]{1,0:T(8,128)(2,1)S(1)}, u32[]{:S(2)}, u32[]{:S(2)}) collective-permute-start(bf16[192,1024]{1,0:T(8,128)(2,1)} %get-tuple-element.23), channel_id=1, source_target_pairs={{0,7},{1,0},{2,1},{3,2},{4,3},{5,4},{6,5},{7,6},{8,15},{9,8},{10,9... | collective-permute-start | bytes 1179656 | tf_op jit(solution)/shard_map/ppermute | solution.py:172
  63.1 22.9 %all-to-all-start.1 = ((f32[32,1,1024]{2,1,0:T(1,128)}), f32[32,1,1024]{2,1,0:T(1,128)S(1)}, u32[]{:S(2)}, u32[]{:S(2)}) async-start(f32[32,1,1024]{2,1,0:T(1,128)} %get-tuple-element.27), calls=%async_computation.1 | async-start | bytes 262144 | tf_op jit(solution)/shard_map/all_to_all | solution.py:223
  72.8 30.2 %collective-permute-start.9 = (bf16[96,1024]{1,0:T(8,128)(2,1)}, bf16[96,1024]{1,0:T(8,128)(2,1)S(1)}, u32[]{:S(2)}, u32[]{:S(2)}) collective-permute-start(bf16[96,1024]{1,0:T(8,128)(2,1)} %get-tuple-element.24), channel_id=1, source_target_pairs={{0,4},{1,5},{2,6},{3,7},{4,0},{5,1},{6,2},{7,3},{8,12},{9,13},{10,... | collective-permute-start | bytes 589832 | tf_op jit(solution)/shard_map/ppermute | solution.py:172
  78.2 2.1 %copy-start.1 = (bf16[96,1024]{1,0:T(8,128)(2,1)S(1)}, bf16[96,1024]{1,0:T(8,128)(2,1)}, u32[]{:S(2)}) copy-start(bf16[96,1024]{1,0:T(8,128)(2,1)} %get-tuple-element.26) | copy-start | bytes 589828
  78.2 24.7 %collective-permute-start.10 = (bf16[96,1024]{1,0:T(8,128)(2,1)S(1)}, bf16[96,1024]{1,0:T(8,128)(2,1)S(1)}, u32[]{:S(2)}, u32[]{:S(2)}) collective-permute-start(bf16[96,1024]{1,0:T(8,128)(2,1)S(1)} %add_convert_fusion.1), channel_id=1, source_target_pairs={{0,2},{1,3},{2,4},{3,5},{4,6},{5,7},{6,0},{7,1},{8,10},{9,11},{10,... | collective-permute-start | bytes 589832 | tf_op jit(solution)/shard_map/ppermute | solution.py:172
  80.4 22.6 %copy-start = (bf16[96,1024]{1,0:T(8,128)(2,1)S(1)}, bf16[96,1024]{1,0:T(8,128)(2,1)}, u32[]{:S(2)}) copy-start(bf16[96,1024]{1,0:T(8,128)(2,1)} %get-tuple-element.21) | copy-start | bytes 589828
  80.4 22.6 %collective-permute-start.11 = (bf16[96,1024]{1,0:T(8,128)(2,1)S(1)}, bf16[96,1024]{1,0:T(8,128)(2,1)S(1)}, u32[]{:S(2)}, u32[]{:S(2)}) collective-permute-start(bf16[96,1024]{1,0:T(8,128)(2,1)S(1)} %add_convert_fusion), channel_id=1, source_target_pairs={{0,6},{1,7},{2,0},{3,1},{4,2},{5,3},{6,4},{7,5},{8,14},{9,15},{10,... | collective-permute-start | bytes 589832 | tf_op jit(solution)/shard_map/ppermute | solution.py:172
  (1 other events, 0.7 us)

commit v3 on v2

v3 whole, which is shorter than its diff:
```python
import jax
import jax.numpy as jnp
from jax import lax
from jax.experimental import pallas as pl
from jax.experimental.pallas import tpu as pltpu
from jax.sharding import PartitionSpec as P

HEADS = 8
LMAX = 192
EPSILON = 1e-05
COUNT = 256
WIDTH = 1024
HEAD_DIM = 128
ROWS = 96
RING = 8
POOL = ROWS * RING
LIMIT = 56 * 1024 * 1024
EXTRA = 128
BASE = 64
XY = 32
NEAR = 16

F32 = jnp.float32
BF16 = jnp.bfloat16
I32 = jnp.int32
CONTRACT_LAST = (((1,), (1,)), ((), ()))
CONTRACT_FIRST = (((0,), (0,)), ((), ()))


def dot(a, b, dims=(((1,), (0,)), ((), ()))):
    return lax.dot_general(a, b, dims, preferred_element_type=F32)


def forward_kernel(
    lengths, q_hbm, k_hbm, v_hbm, gate_hbm, gain_ref, target_ref,
    emb_hbm, normed_hbm, aux_hbm, attend_hbm, slope_hbm,
    q, k, v, gate, emb, normed, aux, attend, slope, mask, came, went,
):
    loads = [
        pltpu.make_async_copy(src, dst, came.at[i])
        for i, (src, dst) in enumerate(((q_hbm, q), (k_hbm, k), (v_hbm, v), (gate_hbm, gate)))
    ]
    for load in loads:
        load.start()
    stores = []

    def store(src, dst):
        copy = pltpu.make_async_copy(src, dst, went.at[len(stores)])
        copy.start()
        stores.append(copy)

    scaling = HEAD_DIM ** (-0.5)
    row = lax.broadcasted_iota(I32, (COUNT, COUNT), 0)
    col = lax.broadcasted_iota(I32, (COUNT, COUNT), 1)
    first = jnp.zeros((COUNT, COUNT), I32)
    finish = jnp.int32(0)
    for i in range(lengths.shape[1]):
        finish = finish + lengths[0, i]
        first = jnp.where(row >= finish, finish, first)
    mask[...] = jnp.where((col >= first) & (col <= row), F32(1.0 / LMAX), F32(0.0))
    for load in loads[:3]:
        load.wait()
    for h in range(HEADS):
        lanes = slice(h * HEAD_DIM, (h + 1) * HEAD_DIM)
        scores = dot(q[:, lanes], k[:, lanes], CONTRACT_LAST) * scaling
        squash = 0.5 * jnp.tanh(0.5 * scores) + 0.5
        keep = mask[...]
        act = scores * squash
        weights = (act * keep).astype(BF16)
        attend[h] = weights
        slope[h] = (squash + act * (1.0 - squash)) * (keep * scaling)
        if h % 2 == 1:
            store(attend.at[h - 1 : h + 1], attend_hbm.at[h - 1 : h + 1])
            store(slope.at[h - 1 : h + 1], slope_hbm.at[h - 1 : h + 1])
        normed[:, lanes] = dot(weights, v[:, lanes])
    loads[3].wait()
    gain = gain_ref[...]
    step = 32
    for i in range(COUNT // step):
        at = slice(i * step, (i + 1) * step)
        part = normed[at, :]
        center = part - jnp.mean(part, axis=1, keepdims=True)
        scale = lax.rsqrt(jnp.mean(center * center, axis=1, keepdims=True) + EPSILON)
        unit = center * scale
        normed[at, :] = unit
        emb[at, :] = (unit * gain * gate[at, :].astype(F32)).astype(BF16)
        lane = lax.broadcasted_iota(I32, (step, HEAD_DIM), 1)
        token = lax.broadcasted_iota(I32, (step, HEAD_DIM), 0) + i * step
        usable = jnp.ones((step, HEAD_DIM), F32)
        finish = jnp.int32(0)
        for j in range(lengths.shape[1]):
            finish = finish + lengths[0, j]
            usable = jnp.where(token + 1 == finish, F32(0.0), usable)
        same = lax.broadcasted_iota(I32, (step, COUNT), 0) + i * step == lax.broadcasted_iota(I32, (step, COUNT), 1)
        target = jnp.sum(jnp.where(same, target_ref[...].astype(F32), F32(0.0)), axis=1, keepdims=True)
        aux[at, :] = jnp.where(lane == 0, scale, jnp.where(lane == 1, usable, target))
    store(emb, emb_hbm)
    store(normed, normed_hbm)
    store(aux, aux_hbm)
    for copy in stores:
        copy.wait()


def step_kernel(
    place, emb_hbm, normed_hbm, aux_hbm, attend_hbm, slope_hbm, q_hbm, k_hbm, v_hbm, gate_hbm, gain_ref,
    own, r1, r2, r3, r4, l1, l2, l3,
    dq_hbm, dk_hbm, dv_hbm, gate_grad_hbm, part_ref,
    plus1, minus1, plus4, plus2, minus2, kept,
    emb, rows, aux, normed, gate, q, k, v, attend, slope, logits, slopes, terms, back,
    dmixed, gate_grad, dq, dk, dv, came, went,
):
    z = place[0]
    ahead = place[1]

    def start_of(offset):
        return pl.multiple_of(lax.rem(z + ahead * offset + RING, RING) * ROWS, 16)

    stores = []

    def store(src, dst):
        copy = pltpu.make_async_copy(src, dst, went.at[len(stores)])
        copy.start()
        stores.append(copy)

    pairs = [(emb_hbm, emb)]
    for offset, ref in ((0, own), (-1, r1), (-2, r2), (-3, r3), (-4, r4), (1, l1), (2, l2), (3, l3)):
        pairs.append((ref, rows.at[pl.ds(start_of(offset), ROWS), :]))
    pairs += [(aux_hbm, aux), (normed_hbm, normed), (gate_hbm, gate)]
    pairs += [(v_hbm, v), (slope_hbm, slope), (attend_hbm, attend), (k_hbm, k), (q_hbm, q)]
    loads = [pltpu.make_async_copy(src, dst, came.at[i]) for i, (src, dst) in enumerate(pairs)]
    for load in loads:
        load.start()
    for load in loads[:10]:
        load.wait()

    logits[...] = dot(emb[...], rows[:, 0:WIDTH], CONTRACT_LAST)
    lane = lax.broadcasted_iota(I32, (8, EXTRA), 1)
    digits = jnp.where(lane == 0, F32(BASE), jnp.where(lane == 1, F32(1.0), F32(0.0))).astype(BF16)
    ids = dot(digits, rows[:, WIDTH : WIDTH + EXTRA], CONTRACT_LAST)[0:1, :]
    step = 32
    for i in range(COUNT // step):
        at = slice(i * step, (i + 1) * step)
        column = lax.broadcasted_iota(I32, (step, POOL), 1).astype(F32)
        chosen = column == aux[at, 2:3]
        own_id = jnp.sum(jnp.where(chosen, ids, F32(0.0)), axis=1, keepdims=True)
        clash = (ids == own_id) & jnp.logical_not(chosen)
        masked = jnp.where(clash, F32(-1e30), logits[at, :])
        peak = jnp.max(masked, axis=1, keepdims=True)
        weight = jnp.where(clash, F32(0.0), jnp.exp(masked - peak))
        total = jnp.sum(weight, axis=1, keepdims=True)
        probs = weight * (1.0 / total)
        slopes[at, :] = (aux[at, 1:2] * jnp.where(chosen, probs - 1.0, probs)).astype(BF16)

    terms[...] = dot(slopes[...], emb[...], CONTRACT_FIRST).astype(BF16)
    for offset, ref in (
        (3, plus1.at[0:ROWS]), (1, plus1.at[ROWS : 2 * ROWS]),
        (-3, minus1.at[0:ROWS]), (-1, minus1.at[ROWS : 2 * ROWS]),
        (4, plus4), (2, plus2), (-2, minus2), (0, kept),
    ):
        store(terms.at[pl.ds(start_of(offset), ROWS), :], ref)

    back[...] = dot(slopes[...], rows[:, 0:WIDTH])
    for load in loads[10:12]:
        load.wait()
    gain = gain_ref[...]
    sums = jnp.zeros((8, WIDTH), F32)
    for i in range(COUNT // step):
        at = slice(i * step, (i + 1) * step)
        unit = normed[at, :]
        pulled = back[at, :]
        gate_grad[at, :] = (pulled * (unit * gain)).astype(BF16)
        dscaled = pulled * gate[at, :].astype(F32)
        product = dscaled * unit
        sums = sums + jnp.sum(product.reshape(step // 8, 8, WIDTH), axis=0)
        dnormed = dscaled * gain
        mean1 = jnp.mean(dnormed, axis=1, keepdims=True)
        mean2 = jnp.mean(product * gain, axis=1, keepdims=True)
        dmixed[at, :] = ((dnormed - mean1 - unit * mean2) * aux[at, 0:1]).astype(BF16)
    store(gate_grad, gate_grad_hbm)
    part = jnp.sum(sums, axis=0, keepdims=True)
    for i in range(XY):
        part_ref[i] = part

    for load in loads[12:]:
        load.wait()
    for h in range(HEADS):
        lanes = slice(h * HEAD_DIM, (h + 1) * HEAD_DIM)
        part = dmixed[:, lanes]
        dattend = dot(part, v[:, lanes], CONTRACT_LAST)
        dscores = (dattend * slope[h]).astype(BF16)
        dv[:, lanes] = dot(attend[h], part, CONTRACT_FIRST).astype(BF16)
        dq[:, lanes] = dot(dscores, k[:, lanes]).astype(BF16)
        dk[:, lanes] = dot(dscores, q[:, lanes], CONTRACT_FIRST).astype(BF16)
        if h % 2 == 1:
            wide = slice((h - 1) * HEAD_DIM, (h + 1) * HEAD_DIM)
            for src, dst in ((dv, dv_hbm), (dq, dq_hbm), (dk, dk_hbm)):
                store(src.at[:, wide], dst.at[:, wide])
    for copy in stores:
        copy.wait()


VMEM = pl.BlockSpec(memory_space=pltpu.VMEM)
SMEM = pl.BlockSpec(memory_space=pltpu.SMEM)
ANY = pl.BlockSpec(memory_space=pl.ANY)


def call(kernel, specs, outs, scratch, copies, cost):
    return pl.pallas_call(
        kernel,
        out_shape=[jax.ShapeDtypeStruct(shape, kind) for shape, kind, _ in outs],
        in_specs=specs,
        out_specs=[spec for _, _, spec in outs],
        scratch_shapes=[pltpu.VMEM(shape, kind) for shape, kind in scratch]
        + [pltpu.SemaphoreType.DMA((count,)) for count in copies],
        compiler_params=pltpu.CompilerParams(vmem_limit_bytes=LIMIT),
        cost_estimate=pl.CostEstimate(flops=cost, bytes_accessed=8 * 10**6, transcendentals=524288),
    )


def shift(value, by):
    pairs = []
    for line in range(2 * XY):
        ahead = by if line % 2 == 0 else -by
        pairs += [(line * RING + i, line * RING + (i + ahead) % RING) for i in range(RING)]
    return lax.ppermute(value, ("dp", "pool"), pairs)


TOKEN = (COUNT, WIDTH)
CHUNK = (ROWS, WIDTH)
PAIR = (2 * ROWS, WIDTH)
SQUARES = (HEADS, COUNT, COUNT)
LANES = (COUNT, HEAD_DIM)
TABLE = (POOL, WIDTH)


def body(query_act, key_act, value_act, gate_act, lengths, targets, pool_rows, pool_ids, norm_gain):
    lane = lax.broadcasted_iota(I32, (ROWS, EXTRA), 1)
    column = pool_ids[:, None]
    digits = jnp.where(lane == 0, column // BASE, jnp.where(lane == 1, column % BASE, 0))
    mine = jnp.concatenate([pool_rows, digits.astype(BF16)], axis=1)
    r2 = shift(mine, 2)
    l2 = shift(mine, -2)
    r1 = shift(mine, 1)
    l1 = shift(mine, -1)
    r4 = shift(r2, 2)
    r3 = shift(r2, 1)
    l3 = shift(l2, -1)
    core = lax.rem(lax.axis_index("dp"), 2)
    place = jnp.stack([lax.axis_index("pool"), 1 - 2 * core]).astype(I32)
    gain = norm_gain.reshape(1, WIDTH)

    emb, normed, aux, attend, slope = call(
        forward_kernel,
        [SMEM] + [ANY] * 4 + [VMEM] * 2,
        [(TOKEN, BF16, ANY), (TOKEN, F32, ANY), (LANES, F32, ANY), (SQUARES, BF16, ANY), (SQUARES, F32, ANY)],
        [(TOKEN, BF16)] * 5 + [(TOKEN, F32), (LANES, F32), (SQUARES, BF16), (SQUARES, F32), ((COUNT, COUNT), F32)],
        (4, HEADS + 3),
        10**9,
    )(lengths, query_act, key_act, value_act, gate_act, gain, targets.reshape(1, COUNT))

    dq, dk, dv, gate_grad, part, plus1, minus1, plus4, plus2, minus2, kept = call(
        step_kernel,
        [SMEM] + [ANY] * 9 + [VMEM] + [ANY] * 8,
        [(TOKEN, BF16, ANY)] * 4
        + [((XY, 1, WIDTH), F32, VMEM), (PAIR, BF16, ANY), (PAIR, BF16, ANY)]
        + [(CHUNK, BF16, ANY)] * 4,
        [(TOKEN, BF16), ((POOL, WIDTH + EXTRA), BF16), (LANES, F32), (TOKEN, F32)]
        + [(TOKEN, BF16)] * 4
        + [(SQUARES, BF16), (SQUARES, F32), ((COUNT, POOL), F32), ((COUNT, POOL), BF16), (TABLE, BF16), (TOKEN, F32)]
        + [(TOKEN, BF16)] * 5,
        (17, 21),
        2 * 10**9,
    )(place, emb, normed, aux, attend, slope, query_act, key_act, value_act, gate_act, gain,
      mine, r1, r2, r3, r4, l1, l2, l3)

    from_left = shift(plus1, 1)
    from_right = shift(minus1, -1)
    from_far = shift(plus4, 2)
    from_left, from_right, from_far = lax.optimization_barrier((from_left, from_right, from_far))
    plus2 = (plus2.astype(F32) + from_left[:ROWS].astype(F32) + from_far.astype(F32)).astype(BF16)
    minus2 = (minus2.astype(F32) + from_right[:ROWS].astype(F32)).astype(BF16)
    two_left = shift(plus2, 2)
    two_right = shift(minus2, -2)

    plane = [[x * 16 + y * 2 + c for x in range(4) for y in range(8)] for c in range(2)]
    spread = lax.all_to_all(part, "dp", 0, 0, axis_index_groups=plane, tiled=True)
    spread = jnp.broadcast_to(jnp.sum(spread, axis=0, keepdims=True), (NEAR, 1, WIDTH))
    near = [[i * NEAR + j for j in range(NEAR)] for i in range(XY)]
    spread = lax.all_to_all(spread, ("dp", "pool"), 0, 0, axis_index_groups=near, tiled=True)
    gain_grad = jnp.sum(spread, axis=0).reshape(WIDTH)

    pool_grad = (
        kept.astype(F32) + from_left[ROWS:].astype(F32) + from_right[ROWS:].astype(F32)
        + two_left.astype(F32) + two_right.astype(F32)
    )
    return (dq, dk, dv, gate_grad, pool_grad, gain_grad)


def solution(mesh):
    rows = P(("dp", "pool"), None)
    flat = P(("dp", "pool"))
    in_specs = (rows, rows, rows, rows, rows, flat, rows, flat, P())
    out_specs = (rows, rows, rows, rows, rows, P())
    return jax.shard_map(body, mesh=mesh, in_specs=in_specs, out_specs=out_specs, check_vma=False)
```

time: 105 us -> 96.8 us (0.922)
  starting transfers between devices: 65.5 us -> 56.9 us
  other arithmetic: 1.79 us -> 5.98 us
  Pallas kernels: 10.2 us -> 14 us
  local copies, waits for them, and re-layouts: 4.32 us -> 0.77 us
  waiting for transfers between devices: 5.01 us -> 2.53 us
    all_to_all x1 -> x0, starting transfers between devices: 6.91 us -> none  [body(): lax.all_to_all(jnp.broadcast_to(pool_ids[None, None, :], (RING, 1, ROWS))...]
    all_to_all x1 -> x0, waiting for transfers between devices: 4.97 us -> none  [body(): lax.all_to_all(jnp.broadcast_to(pool_ids[None, None, :], (RING, 1, ROWS))...]
    pallas_call x1 -> x2, Pallas kernels: 10.2 us -> 14 us  [the longest x1 8.58 us: body(): call(step_kernel, [SMEM] + [ANY] * 9 + [VMEM] + [ANY] * 8, [(TOKEN, BF16,...]
    ppermute x12, waiting for transfers between devices: 0.03 us -> 2.53 us  [shift(): return lax.ppermute(value, ('dp', 'pool'), pairs)]
    ppermute x12, starting transfers between devices: 48.9 us -> 47.1 us  [shift(): return lax.ppermute(value, ('dp', 'pool'), pairs)]
    broadcast_in_dim x1 -> x0, local copies, waits for them, and re-layouts: 1.25 us -> none  [body(): jnp.broadcast_to(pool_ids[None, None, :], (RING, 1, ROWS))]
    all_to_all x1, blocking collectives: 16.1 us -> 15.1 us  [body(): lax.all_to_all(spread, ('dp', 'pool'), 0, 0, axis_index_groups=near, tile...]
  transfers between devices with their start and end apart: 14 -> 13, of which waited for: 1 -> 3; matrix products, arithmetic and copies ran while one was open for 3% -> 4% of each run, Pallas kernels for 0% -> 6%
where the time goes in v3:
time: 96.8 us; the launch traced here: 96.1 us
  starting transfers between devices  56.9 us (59%)
  blocking collectives  15.1 us (16%)
  Pallas kernels  14 us (14%)
  other arithmetic  5.98 us (6%)
  waiting for transfers between devices  2.53 us (3%)
    ppermute x12, starting transfers between devices, shift(): return lax.ppermute(value, ('dp', 'pool'), pairs)  47.1 us
    all_to_all x1, blocking collectives, body(): lax.all_to_all(spread, ('dp', 'pool'), 0, 0, axis_index_groups=near, tile...  15.1 us
    all_to_all x1, starting transfers between devices, body(): lax.all_to_all(part, 'dp', 0, 0, axis_index_groups=plane, tiled=True)  9.7 us
    pallas_call x1, Pallas kernels, body(): call(step_kernel, [SMEM] + [ANY] * 9 + [VMEM] + [ANY] * 8, [(TOKEN, BF16,...  8.58 us
    pallas_call x1, Pallas kernels, body(): call(forward_kernel, [SMEM] + [ANY] * 4 + [VMEM] * 2, [(TOKEN, BF16, ANY)...  5.42 us
    ppermute x12, waiting for transfers between devices, shift(): return lax.ppermute(value, ('dp', 'pool'), pairs)  2.53 us
  transfers between devices with their start and end apart: 13, of which 3 were waited for; matrix products, arithmetic and copies ran while one was open for 4% of the time, Pallas kernels for 6%

profile of v3, /device:TPU:1, one launch (start us, length us, event | category | flops | bytes accessed | tf_op | source)
XLA Modules:
  0.0 96.1 jit_solution(7388639334078865093)
XLA Ops:
  0.6 0.7 and_select_fusion.1
  1.4 0.9 pad_maximum_fusion.own
  2.4 6.6 %collective-permute-start.5 = (bf16[96,1152]{1,0:T(8,128)(2,1)S(1)}, bf16[96,1152]{1,0:T(8,128)(2,1)S(1)}, u32[]{:S(2)}, u32[]{:S(2)}) collective-permute-start(bf16[96,1152]{1,0:T(8,128)(2,1)S(1)} %pad_maximum_fusion.own), channel_id=1, source_target_pairs={{0,6},{1,7},{2,0},{3,1},{4,2},{5,3},{6,4},{7,5},{8,10},{9,11},{10,... | collective-permute-start | bytes 663560 | tf_op jit(solution)/shard_map/ppermute | solution.py:225
  9.0 6.8 %collective-permute-start.1 = (bf16[96,1152]{1,0:T(8,128)(2,1)S(1)}, bf16[96,1152]{1,0:T(8,128)(2,1)S(1)}, u32[]{:S(2)}, u32[]{:S(2)}) collective-permute-start(bf16[96,1152]{1,0:T(8,128)(2,1)S(1)} %pad_maximum_fusion.own), channel_id=1, source_target_pairs={{0,2},{1,3},{2,4},{3,5},{4,6},{5,7},{6,0},{7,1},{8,14},{9,15},{10,... | collective-permute-start | bytes 663560 | tf_op jit(solution)/shard_map/ppermute | solution.py:225
  15.8 3.1 %collective-permute-start.4 = (bf16[96,1152]{1,0:T(8,128)(2,1)S(1)}, bf16[96,1152]{1,0:T(8,128)(2,1)S(1)}, u32[]{:S(2)}, u32[]{:S(2)}) collective-permute-start(bf16[96,1152]{1,0:T(8,128)(2,1)S(1)} %pad_maximum_fusion.own), channel_id=1, source_target_pairs={{0,7},{1,0},{2,1},{3,2},{4,3},{5,4},{6,5},{7,6},{8,9},{9,10},{10,1... | collective-permute-start | bytes 663560 | tf_op jit(solution)/shard_map/ppermute | solution.py:225
  18.9 3.4 %collective-permute-start = (bf16[96,1152]{1,0:T(8,128)(2,1)S(1)}, bf16[96,1152]{1,0:T(8,128)(2,1)S(1)}, u32[]{:S(2)}, u32[]{:S(2)}) collective-permute-start(bf16[96,1152]{1,0:T(8,128)(2,1)S(1)} %pad_maximum_fusion.own), channel_id=1, source_target_pairs={{0,1},{1,2},{2,3},{3,4},{4,5},{5,6},{6,7},{7,0},{8,15},{9,8},{10,9... | collective-permute-start | bytes 663560 | tf_op jit(solution)/shard_map/ppermute | solution.py:225
  22.3 1.9 %collective-permute-start.6 = (bf16[96,1152]{1,0:T(8,128)(2,1)S(1)}, bf16[96,1152]{1,0:T(8,128)(2,1)S(1)}, u32[]{:S(2)}, u32[]{:S(2)}) collective-permute-start(bf16[96,1152]{1,0:T(8,128)(2,1)S(1)} %collective-permute-done.5.l2), channel_id=1, source_target_pairs={{0,7},{1,0},{2,1},{3,2},{4,3},{5,4},{6,5},{7,6},{8,9},{9,10},{10,1... | collective-permute-start | bytes 663560 | tf_op jit(solution)/shard_map/ppermute | solution.py:225
  24.2 1.5 %collective-permute-done.1.r2 = bf16[96,1152]{1,0:T(8,128)(2,1)S(1)} collective-permute-done((bf16[96,1152]{1,0:T(8,128)(2,1)S(1)}, bf16[96,1152]{1,0:T(8,128)(2,1)S(1)}, u32[]{:S(2)}, u32[]{:S(2)}) %collective-permute-start.1) | collective-permute-done | bytes 221216 | tf_op jit(solution)/shard_map/ppermute | solution.py:225
  25.7 5.9 %collective-permute-start.3 = (bf16[96,1152]{1,0:T(8,128)(2,1)S(1)}, bf16[96,1152]{1,0:T(8,128)(2,1)S(1)}, u32[]{:S(2)}, u32[]{:S(2)}) collective-permute-start(bf16[96,1152]{1,0:T(8,128)(2,1)S(1)} %collective-permute-done.1.r2), channel_id=1, source_target_pairs={{0,2},{1,3},{2,4},{3,5},{4,6},{5,7},{6,0},{7,1},{8,14},{9,15},{10,... | collective-permute-start | bytes 663560 | tf_op jit(solution)/shard_map/ppermute | solution.py:225
  31.6 1.9 %collective-permute-start.2 = (bf16[96,1152]{1,0:T(8,128)(2,1)S(1)}, bf16[96,1152]{1,0:T(8,128)(2,1)S(1)}, u32[]{:S(2)}, u32[]{:S(2)}) collective-permute-start(bf16[96,1152]{1,0:T(8,128)(2,1)S(1)} %collective-permute-done.1.r2), channel_id=1, source_target_pairs={{0,1},{1,2},{2,3},{3,4},{4,5},{5,6},{6,7},{7,0},{8,15},{9,8},{10,9... | collective-permute-start | bytes 663560 | tf_op jit(solution)/shard_map/ppermute | solution.py:225
  33.6 5.4 %shard_map.136 = (bf16[256,1024]{1,0:T(8,128)(2,1)}, f32[256,1024]{1,0:T(8,128)}, f32[256,128]{1,0:T(8,128)}, bf16[8,256,256]{2,1,0:T(8,128)(2,1)}, f32[8,256,256]{2,1,0:T(8,128)}) custom-call(s32[1,4]{1,0:T(1,128)} %lengths.1, bf16[256,1024]{1,0:T(8,128)(2,1)} %q_hbm.3, bf16[256,1024]{1,0:T(8,128)(2,1)} %k_hbm.3, bf16[256,1024]{1,0:T(8,128)(2,1)} %v_hbm.3, ...), custom_call_target="tpu_custom_call" | custom-call | flops 1000000000 | bytes 8000000 | tf_op jit(solution)/shard_map/pallas_call | solution.py:252
  39.0 0.7 pad_add_fusion.place
  40.7 8.6 %shard_map.137 = (bf16[256,1024]{1,0:T(8,128)(2,1)}, bf16[256,1024]{1,0:T(8,128)(2,1)}, bf16[256,1024]{1,0:T(8,128)(2,1)}, bf16[256,1024]{1,0:T(8,128)(2,1)}, f3...) custom-call(s32[2]{0:T(128)} %pad_add_fusion.place, ...), custom_call_target="tpu_custom_call" | custom-call | flops 2000000000 | bytes 8000000 | tf_op jit(solution)/shard_map/pallas_call | solution.py:261
  49.3 5.1 %collective-permute-start.7 = (bf16[192,1024]{1,0:T(8,128)(2,1)}, bf16[192,1024]{1,0:T(8,128)(2,1)S(1)}, u32[]{:S(2)}, u32[]{:S(2)}) collective-permute-start(bf16[192,1024]{1,0:T(8,128)(2,1)} %get-tuple-element.35), channel_id=1, source_target_pairs={{0,1},{1,2},{2,3},{3,4},{4,5},{5,6},{6,7},{7,0},{8,15},{9,8},{10,9... | collective-permute-start | bytes 1179656 | tf_op jit(solution)/shard_map/ppermute | solution.py:225
  54.4 1.9 %collective-permute-start.8 = (bf16[192,1024]{1,0:T(8,128)(2,1)}, bf16[192,1024]{1,0:T(8,128)(2,1)S(1)}, u32[]{:S(2)}, u32[]{:S(2)}) collective-permute-start(bf16[192,1024]{1,0:T(8,128)(2,1)} %get-tuple-element.36), channel_id=1, source_target_pairs={{0,7},{1,0},{2,1},{3,2},{4,3},{5,4},{6,5},{7,6},{8,9},{9,10},{10,1... | collective-permute-start | bytes 1179656 | tf_op jit(solution)/shard_map/ppermute | solution.py:225
  56.4 3.1 %collective-permute-start.9 = (bf16[96,1024]{1,0:T(8,128)(2,1)}, bf16[96,1024]{1,0:T(8,128)(2,1)S(1)}, u32[]{:S(2)}, u32[]{:S(2)}) collective-permute-start(bf16[96,1024]{1,0:T(8,128)(2,1)} %get-tuple-element.37), channel_id=1, source_target_pairs={{0,2},{1,3},{2,4},{3,5},{4,6},{5,7},{6,0},{7,1},{8,14},{9,15},{10,... | collective-permute-start | bytes 589832 | tf_op jit(solution)/shard_map/ppermute | solution.py:225
  59.5 9.7 %all-to-all-start = ((f32[32,1,1024]{2,1,0:T(1,128)}), f32[32,1,1024]{2,1,0:T(1,128)S(1)}, u32[]{:S(2)}, u32[]{:S(2)}) async-start(f32[32,1,1024]{2,1,0:T(1,128)} %get-tuple-element.43), calls=%async_computation | async-start | bytes 262144 | tf_op jit(solution)/shard_map/all_to_all | solution.py:286
  69.2 0.8 collective-permute-done.8
  69.9 1.0 %add_convert_fusion = bf16[96,1024]{1,0:T(8,128)(2,1)S(1)} fusion(bf16[96,1024]{1,0:T(8,128)(2,1)} %get-tuple-element.42, bf16[192,1024]{1,0:T(8,128)(2,1)S(1)} %collective-permute-done.8), kind=kLoop, calls=%fused_computation.1 | loop fusion | flops 393216 | bytes 589824 | tf_op jit(solution)/shard_map/convert_element_type | solution.py:281
  70.9 2.4 %collective-permute-start.11 = (bf16[96,1024]{1,0:T(8,128)(2,1)S(1)}, bf16[96,1024]{1,0:T(8,128)(2,1)S(1)}, u32[]{:S(2)}, u32[]{:S(2)}) collective-permute-start(bf16[96,1024]{1,0:T(8,128)(2,1)S(1)} %add_convert_fusion), channel_id=1, source_target_pairs={{0,6},{1,7},{2,0},{3,1},{4,2},{5,3},{6,4},{7,5},{8,10},{9,11},{10,... | collective-permute-start | bytes 589832 | tf_op jit(solution)/shard_map/ppermute | solution.py:225
  73.3 1.0 %add_convert_fusion.1 = bf16[96,1024]{1,0:T(8,128)(2,1)S(1)} fusion(bf16[96,1024]{1,0:T(8,128)(2,1)S(1)} %collective-permute-done.9, bf16[96,1024]{1,0:T(8,128)(2,1)} %get-tuple-element.40, bf16[192,1024]{1,0:T(8,128)(2,1)S(1)} %collective-permute-done.7), kind=kLoop, calls=%fused_computation.2 | loop fusion | flops 589824 | bytes 786432 | tf_op jit(solution)/shard_map/convert_element_type | solution.py:280
  74.3 5.0 %collective-permute-start.10 = (bf16[96,1024]{1,0:T(8,128)(2,1)S(1)}, bf16[96,1024]{1,0:T(8,128)(2,1)S(1)}, u32[]{:S(2)}, u32[]{:S(2)}) collective-permute-start(bf16[96,1024]{1,0:T(8,128)(2,1)S(1)} %add_convert_fusion.1), channel_id=1, source_target_pairs={{0,2},{1,3},{2,4},{3,5},{4,6},{5,7},{6,0},{7,1},{8,14},{9,15},{10,... | collective-permute-start | bytes 589832 | tf_op jit(solution)/shard_map/ppermute | solution.py:225
  79.5 15.1 %all_to_all.10 = f32[16,1,1024]{2,1,0:T(1,128)S(1)} all-to-all(f32[16,1,1024]{2,1,0:T(1,128)S(1)} %broadcast_in_dim.27), channel_id=1, replica_groups={{0,1,2,3,4,5,6,7,8,9,10,11,12,13,14,15},{16,17,18,19,20,21,22,23,24,25,..., dimensions={0} | all-to-all | bytes 131072 | tf_op jit(solution)/shard_map/all_to_all | solution.py:289
  95.2 0.9 convert_add_fusion
  (34 shorter events, 1.9 us)
Async XLA Ops:
  2.4 37.7 %copy-start = (bf16[96,1152]{1,0:T(8,128)(2,1)}, bf16[96,1152]{1,0:T(8,128)(2,1)S(1)}, u32[]{:S(2)}) copy-start(bf16[96,1152]{1,0:T(8,128)(2,1)S(1)} %pad_maximum_fusion.own) | copy-start | bytes 663556
  2.4 19.9 %collective-permute-start.5 = (bf16[96,1152]{1,0:T(8,128)(2,1)S(1)}, bf16[96,1152]{1,0:T(8,128)(2,1)S(1)}, u32[]{:S(2)}, u32[]{:S(2)}) collective-permute-start(bf16[96,1152]{1,0:T(8,128)(2,1)S(1)} %pad_maximum_fusion.own), channel_id=1, source_target_pairs={{0,6},{1,7},{2,0},{3,1},{4,2},{5,3},{6,4},{7,5},{8,10},{9,11},{10,... | collective-permute-start | bytes 663560 | tf_op jit(solution)/shard_map/ppermute | solution.py:225
  9.0 16.7 %collective-permute-start.1 = (bf16[96,1152]{1,0:T(8,128)(2,1)S(1)}, bf16[96,1152]{1,0:T(8,128)(2,1)S(1)}, u32[]{:S(2)}, u32[]{:S(2)}) collective-permute-start(bf16[96,1152]{1,0:T(8,128)(2,1)S(1)} %pad_maximum_fusion.own), channel_id=1, source_target_pairs={{0,2},{1,3},{2,4},{3,5},{4,6},{5,7},{6,0},{7,1},{8,14},{9,15},{10,... | collective-permute-start | bytes 663560 | tf_op jit(solution)/shard_map/ppermute | solution.py:225
  15.8 23.9 %collective-permute-start.4 = (bf16[96,1152]{1,0:T(8,128)(2,1)S(1)}, bf16[96,1152]{1,0:T(8,128)(2,1)S(1)}, u32[]{:S(2)}, u32[]{:S(2)}) collective-permute-start(bf16[96,1152]{1,0:T(8,128)(2,1)S(1)} %pad_maximum_fusion.own), channel_id=1, source_target_pairs={{0,7},{1,0},{2,1},{3,2},{4,3},{5,4},{6,5},{7,6},{8,9},{9,10},{10,1... | collective-permute-start | bytes 663560 | tf_op jit(solution)/shard_map/ppermute | solution.py:225
  18.9 20.8 %collective-permute-start = (bf16[96,1152]{1,0:T(8,128)(2,1)S(1)}, bf16[96,1152]{1,0:T(8,128)(2,1)S(1)}, u32[]{:S(2)}, u32[]{:S(2)}) collective-permute-start(bf16[96,1152]{1,0:T(8,128)(2,1)S(1)} %pad_maximum_fusion.own), channel_id=1, source_target_pairs={{0,1},{1,2},{2,3},{3,4},{4,5},{5,6},{6,7},{7,0},{8,15},{9,8},{10,9... | collective-permute-start | bytes 663560 | tf_op jit(solution)/shard_map/ppermute | solution.py:225
  22.3 17.7 %copy-start.1 = (bf16[96,1152]{1,0:T(8,128)(2,1)}, bf16[96,1152]{1,0:T(8,128)(2,1)S(1)}, u32[]{:S(2)}) copy-start(bf16[96,1152]{1,0:T(8,128)(2,1)S(1)} %collective-permute-done.5.l2) | copy-start | bytes 663556
  22.3 17.4 %collective-permute-start.6 = (bf16[96,1152]{1,0:T(8,128)(2,1)S(1)}, bf16[96,1152]{1,0:T(8,128)(2,1)S(1)}, u32[]{:S(2)}, u32[]{:S(2)}) collective-permute-start(bf16[96,1152]{1,0:T(8,128)(2,1)S(1)} %collective-permute-done.5.l2), channel_id=1, source_target_pairs={{0,7},{1,0},{2,1},{3,2},{4,3},{5,4},{6,5},{7,6},{8,9},{9,10},{10,1... | collective-permute-start | bytes 663560 | tf_op jit(solution)/shard_map/ppermute | solution.py:225
  25.7 14.3 %copy-start.2 = (bf16[96,1152]{1,0:T(8,128)(2,1)}, bf16[96,1152]{1,0:T(8,128)(2,1)S(1)}, u32[]{:S(2)}) copy-start(bf16[96,1152]{1,0:T(8,128)(2,1)S(1)} %collective-permute-done.1.r2) | copy-start | bytes 663556
  25.7 14.0 %collective-permute-start.3 = (bf16[96,1152]{1,0:T(8,128)(2,1)S(1)}, bf16[96,1152]{1,0:T(8,128)(2,1)S(1)}, u32[]{:S(2)}, u32[]{:S(2)}) collective-permute-start(bf16[96,1152]{1,0:T(8,128)(2,1)S(1)} %collective-permute-done.1.r2), channel_id=1, source_target_pairs={{0,2},{1,3},{2,4},{3,5},{4,6},{5,7},{6,0},{7,1},{8,14},{9,15},{10,... | collective-permute-start | bytes 663560 | tf_op jit(solution)/shard_map/ppermute | solution.py:225
  31.6 8.4 %collective-permute-start.2 = (bf16[96,1152]{1,0:T(8,128)(2,1)S(1)}, bf16[96,1152]{1,0:T(8,128)(2,1)S(1)}, u32[]{:S(2)}, u32[]{:S(2)}) collective-permute-start(bf16[96,1152]{1,0:T(8,128)(2,1)S(1)} %collective-permute-done.1.r2), channel_id=1, source_target_pairs={{0,1},{1,2},{2,3},{3,4},{4,5},{5,6},{6,7},{7,0},{8,15},{9,8},{10,9... | collective-permute-start | bytes 663560 | tf_op jit(solution)/shard_map/ppermute | solution.py:225
  39.7 0.7 copy-start.3
  39.7 0.8 copy-start.4
  39.7 0.8 copy-start.5
  39.7 0.9 copy-start.6
  40.0 0.7 copy-start.7
  49.3 45.9 %copy-start.8 = (bf16[96,1024]{1,0:T(8,128)(2,1)S(1)}, bf16[96,1024]{1,0:T(8,128)(2,1)}, u32[]{:S(2)}) copy-start(bf16[96,1024]{1,0:T(8,128)(2,1)} %get-tuple-element.34) | copy-start | bytes 589828
  49.3 19.8 %collective-permute-start.7 = (bf16[192,1024]{1,0:T(8,128)(2,1)}, bf16[192,1024]{1,0:T(8,128)(2,1)S(1)}, u32[]{:S(2)}, u32[]{:S(2)}) collective-permute-start(bf16[192,1024]{1,0:T(8,128)(2,1)} %get-tuple-element.35), channel_id=1, source_target_pairs={{0,1},{1,2},{2,3},{3,4},{4,5},{5,6},{6,7},{7,0},{8,15},{9,8},{10,9... | collective-permute-start | bytes 1179656 | tf_op jit(solution)/shard_map/ppermute | solution.py:225
  54.4 15.5 %collective-permute-start.8 = (bf16[192,1024]{1,0:T(8,128)(2,1)}, bf16[192,1024]{1,0:T(8,128)(2,1)S(1)}, u32[]{:S(2)}, u32[]{:S(2)}) collective-permute-start(bf16[192,1024]{1,0:T(8,128)(2,1)} %get-tuple-element.36), channel_id=1, source_target_pairs={{0,7},{1,0},{2,1},{3,2},{4,3},{5,4},{6,5},{7,6},{8,9},{9,10},{10,1... | collective-permute-start | bytes 1179656 | tf_op jit(solution)/shard_map/ppermute | solution.py:225
  56.4 12.8 %collective-permute-start.9 = (bf16[96,1024]{1,0:T(8,128)(2,1)}, bf16[96,1024]{1,0:T(8,128)(2,1)S(1)}, u32[]{:S(2)}, u32[]{:S(2)}) collective-permute-start(bf16[96,1024]{1,0:T(8,128)(2,1)} %get-tuple-element.37), channel_id=1, source_target_pairs={{0,2},{1,3},{2,4},{3,5},{4,6},{5,7},{6,0},{7,1},{8,14},{9,15},{10,... | collective-permute-start | bytes 589832 | tf_op jit(solution)/shard_map/ppermute | solution.py:225
  59.5 19.9 %all-to-all-start = ((f32[32,1,1024]{2,1,0:T(1,128)}), f32[32,1,1024]{2,1,0:T(1,128)S(1)}, u32[]{:S(2)}, u32[]{:S(2)}) async-start(f32[32,1,1024]{2,1,0:T(1,128)} %get-tuple-element.43), calls=%async_computation | async-start | bytes 262144 | tf_op jit(solution)/shard_map/all_to_all | solution.py:286
  70.9 24.3 %collective-permute-start.11 = (bf16[96,1024]{1,0:T(8,128)(2,1)S(1)}, bf16[96,1024]{1,0:T(8,128)(2,1)S(1)}, u32[]{:S(2)}, u32[]{:S(2)}) collective-permute-start(bf16[96,1024]{1,0:T(8,128)(2,1)S(1)} %add_convert_fusion), channel_id=1, source_target_pairs={{0,6},{1,7},{2,0},{3,1},{4,2},{5,3},{6,4},{7,5},{8,10},{9,11},{10,... | collective-permute-start | bytes 589832 | tf_op jit(solution)/shard_map/ppermute | solution.py:225
  74.3 20.9 %collective-permute-start.10 = (bf16[96,1024]{1,0:T(8,128)(2,1)S(1)}, bf16[96,1024]{1,0:T(8,128)(2,1)S(1)}, u32[]{:S(2)}, u32[]{:S(2)}) collective-permute-start(bf16[96,1024]{1,0:T(8,128)(2,1)S(1)} %add_convert_fusion.1), channel_id=1, source_target_pairs={{0,2},{1,3},{2,4},{3,5},{4,6},{5,7},{6,0},{7,1},{8,14},{9,15},{10,... | collective-permute-start | bytes 589832 | tf_op jit(solution)/shard_map/ppermute | solution.py:225

commit v4 on v3

--- a/solution.py
+++ b/solution.py
@@ -36,10 +36,13 @@
     emb_hbm, normed_hbm, aux_hbm, attend_hbm, slope_hbm,
     q, k, v, gate, emb, normed, aux, attend, slope, mask, came, went,
 ):
-    loads = [
-        pltpu.make_async_copy(src, dst, came.at[i])
-        for i, (src, dst) in enumerate(((q_hbm, q), (k_hbm, k), (v_hbm, v), (gate_hbm, gate)))
-    ]
+    halves = (slice(0, WIDTH // 2), slice(WIDTH // 2, WIDTH))
+    pairs = [
+        (src.at[:, half], dst.at[:, half])
+        for half in halves
+        for src, dst in ((q_hbm, q), (k_hbm, k), (v_hbm, v))
+    ] + [(gate_hbm, gate)]
+    loads = [pltpu.make_async_copy(src, dst, came.at[i]) for i, (src, dst) in enumerate(pairs)]
     for load in loads:
         load.start()
     stores = []
@@ -58,9 +61,10 @@
         finish = finish + lengths[0, i]
         first = jnp.where(row >= finish, finish, first)
     mask[...] = jnp.where((col >= first) & (col <= row), F32(1.0 / LMAX), F32(0.0))
-    for load in loads[:3]:
-        load.wait()
     for h in range(HEADS):
+        if h % 4 == 0:
+            for load in loads[h // 4 * 3 : h // 4 * 3 + 3]:
+                load.wait()
         lanes = slice(h * HEAD_DIM, (h + 1) * HEAD_DIM)
         scores = dot(q[:, lanes], k[:, lanes], CONTRACT_LAST) * scaling
         squash = 0.5 * jnp.tanh(0.5 * scores) + 0.5
@@ -73,7 +77,7 @@
             store(attend.at[h - 1 : h + 1], attend_hbm.at[h - 1 : h + 1])
             store(slope.at[h - 1 : h + 1], slope_hbm.at[h - 1 : h + 1])
         normed[:, lanes] = dot(weights, v[:, lanes])
-    loads[3].wait()
+    loads[6].wait()
     gain = gain_ref[...]
     step = 32
     for i in range(COUNT // step):
@@ -94,23 +98,24 @@
         same = lax.broadcasted_iota(I32, (step, COUNT), 0) + i * step == lax.broadcasted_iota(I32, (step, COUNT), 1)
         target = jnp.sum(jnp.where(same, target_ref[...].astype(F32), F32(0.0)), axis=1, keepdims=True)
         aux[at, :] = jnp.where(lane == 0, scale, jnp.where(lane == 1, usable, target))
-    store(emb, emb_hbm)
-    store(normed, normed_hbm)
+        if i % 4 == 3:
+            half = slice((i - 3) * step, (i + 1) * step)
+            store(normed.at[half], normed_hbm.at[half])
+            store(emb.at[half], emb_hbm.at[half])
     store(aux, aux_hbm)
     for copy in stores:
         copy.wait()
 
 
 def step_kernel(
-    place, emb_hbm, normed_hbm, aux_hbm, attend_hbm, slope_hbm, q_hbm, k_hbm, v_hbm, gate_hbm, gain_ref,
-    own, r1, r2, r3, r4, l1, l2, l3,
-    dq_hbm, dk_hbm, dv_hbm, gate_grad_hbm, part_ref,
+    place, line, emb_hbm, normed_hbm, aux_hbm, gate_hbm, gain_ref,
+    own, r1, r2, r3, l1, l2, l3, l4,
+    gate_grad_hbm, dmixed_hbm, part_ref,
     plus1, minus1, plus4, plus2, minus2, kept,
-    emb, rows, aux, normed, gate, q, k, v, attend, slope, logits, slopes, terms, back,
-    dmixed, gate_grad, dq, dk, dv, came, went,
+    emb, rows, aux, normed, gate, logits, slopes, terms, back, dmixed, gate_grad, came, went,
 ):
     z = place[0]
-    ahead = place[1]
+    ahead = 1 - 2 * lax.rem(line[0], 2)
 
     def start_of(offset):
         return pl.multiple_of(lax.rem(z + ahead * offset + RING, RING) * ROWS, 16)
@@ -123,10 +128,9 @@
         stores.append(copy)
 
     pairs = [(emb_hbm, emb)]
-    for offset, ref in ((0, own), (-1, r1), (-2, r2), (-3, r3), (-4, r4), (1, l1), (2, l2), (3, l3)):
+    for offset, ref in ((0, own), (-1, r1), (-2, r2), (-3, r3), (1, l1), (2, l2), (3, l3), (4, l4)):
         pairs.append((ref, rows.at[pl.ds(start_of(offset), ROWS), :]))
     pairs += [(aux_hbm, aux), (normed_hbm, normed), (gate_hbm, gate)]
-    pairs += [(v_hbm, v), (slope_hbm, slope), (attend_hbm, attend), (k_hbm, k), (q_hbm, q)]
     loads = [pltpu.make_async_copy(src, dst, came.at[i]) for i, (src, dst) in enumerate(pairs)]
     for load in loads:
         load.start()
@@ -176,14 +180,35 @@
         mean1 = jnp.mean(dnormed, axis=1, keepdims=True)
         mean2 = jnp.mean(product * gain, axis=1, keepdims=True)
         dmixed[at, :] = ((dnormed - mean1 - unit * mean2) * aux[at, 0:1]).astype(BF16)
+    store(dmixed, dmixed_hbm)
     store(gate_grad, gate_grad_hbm)
     part = jnp.sum(sums, axis=0, keepdims=True)
     for i in range(XY):
         part_ref[i] = part
 
-    for load in loads[12:]:
-        load.wait()
+    for copy in stores:
+        copy.wait()
+
+
+def backward_kernel(
+    dmixed_hbm, q_hbm, k_hbm, v_hbm, attend_hbm, slope_hbm, dq_hbm, dk_hbm, dv_hbm,
+    dmixed, q, k, v, attend, slope, dq, dk, dv, came, went,
+):
+    pairs = []
+    for half in range(2):
+        lanes = slice(half * WIDTH // 2, (half + 1) * WIDTH // 2)
+        heads = slice(half * HEADS // 2, (half + 1) * HEADS // 2)
+        pairs += [(src.at[:, lanes], dst.at[:, lanes]) for src, dst in ((dmixed_hbm, dmixed), (v_hbm, v))]
+        pairs += [(src.at[heads], dst.at[heads]) for src, dst in ((slope_hbm, slope), (attend_hbm, attend))]
+        pairs += [(src.at[:, lanes], dst.at[:, lanes]) for src, dst in ((k_hbm, k), (q_hbm, q))]
+    loads = [pltpu.make_async_copy(src, dst, came.at[i]) for i, (src, dst) in enumerate(pairs)]
+    for load in loads:
+        load.start()
+    stores = []
     for h in range(HEADS):
+        if h % 4 == 0:
+            for load in loads[h // 4 * 6 : h // 4 * 6 + 6]:
+                load.wait()
         lanes = slice(h * HEAD_DIM, (h + 1) * HEAD_DIM)
         part = dmixed[:, lanes]
         dattend = dot(part, v[:, lanes], CONTRACT_LAST)
@@ -194,7 +219,9 @@
         if h % 2 == 1:
             wide = slice((h - 1) * HEAD_DIM, (h + 1) * HEAD_DIM)
             for src, dst in ((dv, dv_hbm), (dq, dq_hbm), (dk, dk_hbm)):
-                store(src.at[:, wide], dst.at[:, wide])
+                copy = pltpu.make_async_copy(src.at[:, wide], dst.at[:, wide], went.at[len(stores)])
+                copy.start()
+                stores.append(copy)
     for copy in stores:
         copy.wait()
 
@@ -204,7 +231,7 @@
 ANY = pl.BlockSpec(memory_space=pl.ANY)
 
 
-def call(kernel, specs, outs, scratch, copies, cost):
+def call(kernel, specs, outs, scratch, copies, cost, limit=LIMIT):
     return pl.pallas_call(
         kernel,
         out_shape=[jax.ShapeDtypeStruct(shape, kind) for shape, kind, _ in outs],
@@ -212,7 +239,7 @@
         out_specs=[spec for _, _, spec in outs],
         scratch_shapes=[pltpu.VMEM(shape, kind) for shape, kind in scratch]
         + [pltpu.SemaphoreType.DMA((count,)) for count in copies],
-        compiler_params=pltpu.CompilerParams(vmem_limit_bytes=LIMIT),
+        compiler_params=pltpu.CompilerParams(vmem_limit_bytes=limit),
         cost_estimate=pl.CostEstimate(flops=cost, bytes_accessed=8 * 10**6, transcendentals=524288),
     )
 
@@ -242,11 +269,11 @@
     l2 = shift(mine, -2)
     r1 = shift(mine, 1)
     l1 = shift(mine, -1)
-    r4 = shift(r2, 2)
+    l4 = shift(l2, -2)
     r3 = shift(r2, 1)
     l3 = shift(l2, -1)
-    core = lax.rem(lax.axis_index("dp"), 2)
-    place = jnp.stack([lax.axis_index("pool"), 1 - 2 * core]).astype(I32)
+    place = lax.axis_index("pool").reshape(1).astype(I32)
+    line = lax.axis_index("dp").reshape(1).astype(I32)
     gain = norm_gain.reshape(1, WIDTH)
 
     emb, normed, aux, attend, slope = call(
@@ -254,24 +281,22 @@
         [SMEM] + [ANY] * 4 + [VMEM] * 2,
         [(TOKEN, BF16, ANY), (TOKEN, F32, ANY), (LANES, F32, ANY), (SQUARES, BF16, ANY), (SQUARES, F32, ANY)],
         [(TOKEN, BF16)] * 5 + [(TOKEN, F32), (LANES, F32), (SQUARES, BF16), (SQUARES, F32), ((COUNT, COUNT), F32)],
-        (4, HEADS + 3),
+        (7, HEADS + 5),
         10**9,
     )(lengths, query_act, key_act, value_act, gate_act, gain, targets.reshape(1, COUNT))
 
-    dq, dk, dv, gate_grad, part, plus1, minus1, plus4, plus2, minus2, kept = call(
+    gate_grad, dmixed, part, plus1, minus1, plus4, plus2, minus2, kept = call(
         step_kernel,
-        [SMEM] + [ANY] * 9 + [VMEM] + [ANY] * 8,
-        [(TOKEN, BF16, ANY)] * 4
+        [SMEM, SMEM] + [ANY] * 4 + [VMEM] + [ANY] * 8,
+        [(TOKEN, BF16, ANY)] * 2
         + [((XY, 1, WIDTH), F32, VMEM), (PAIR, BF16, ANY), (PAIR, BF16, ANY)]
         + [(CHUNK, BF16, ANY)] * 4,
-        [(TOKEN, BF16), ((POOL, WIDTH + EXTRA), BF16), (LANES, F32), (TOKEN, F32)]
-        + [(TOKEN, BF16)] * 4
-        + [(SQUARES, BF16), (SQUARES, F32), ((COUNT, POOL), F32), ((COUNT, POOL), BF16), (TABLE, BF16), (TOKEN, F32)]
-        + [(TOKEN, BF16)] * 5,
-        (17, 21),
+        [(TOKEN, BF16), ((POOL, WIDTH + EXTRA), BF16), (LANES, F32), (TOKEN, F32), (TOKEN, BF16)]
+        + [((COUNT, POOL), F32), ((COUNT, POOL), BF16), (TABLE, BF16), (TOKEN, F32)]
+        + [(TOKEN, BF16)] * 2,
+        (12, 10),
         2 * 10**9,
-    )(place, emb, normed, aux, attend, slope, query_act, key_act, value_act, gate_act, gain,
-      mine, r1, r2, r3, r4, l1, l2, l3)
+    )(place, line, emb, normed, aux, gate_act, gain, mine, r1, r2, r3, l1, l2, l3, l4)
 
     from_left = shift(plus1, 1)
     from_right = shift(minus1, -1)
@@ -293,6 +318,14 @@
         kept.astype(F32) + from_left[ROWS:].astype(F32) + from_right[ROWS:].astype(F32)
         + two_left.astype(F32) + two_right.astype(F32)
     )
+    dq, dk, dv = call(
+        backward_kernel,
+        [ANY] * 6,
+        [(TOKEN, BF16, ANY)] * 3,
+        [(TOKEN, BF16)] * 4 + [(SQUARES, BF16), (SQUARES, F32)] + [(TOKEN, BF16)] * 3,
+        (12, 12),
+        2 * 10**9,
+    )(dmixed, query_act, key_act, value_act, attend, slope)
     return (dq, dk, dv, gate_grad, pool_grad, gain_grad)
 
 

time: 96.8 us -> 95.3 us (0.985)
  blocking collectives: 15.1 us -> 0 us
  starting transfers between devices: 56.9 us -> 64.6 us
  waiting for transfers between devices: 2.53 us -> 5.51 us
  Pallas kernels: 14 us -> 16.9 us
    all_to_all x1 -> x0, blocking collectives: 15.1 us -> none  [body(): lax.all_to_all(spread, ('dp', 'pool'), 0, 0, axis_index_groups=near, tile...]
    all_to_all x0 -> x1, starting transfers between devices: none -> 10.2 us  [body(): lax.all_to_all(spread, ('dp', 'pool'), 0, 0, axis_index_groups=near, tile...]
    pallas_call x1 -> x2, Pallas kernels: 8.58 us -> 11.6 us  [the longest x1 6.95 us: body(): call(step_kernel, [SMEM, SMEM] + [ANY] * 4 + [VMEM] + [ANY] * 8, [(TOKEN,...]
    all_to_all x0 -> x1, waiting for transfers between devices: none -> 2.53 us  [body(): lax.all_to_all(spread, ('dp', 'pool'), 0, 0, axis_index_groups=near, tile...]
    ppermute x12, starting transfers between devices: 47.1 us -> 44.7 us  [shift(): return lax.ppermute(value, ('dp', 'pool'), pairs)]
  transfers between devices with their start and end apart: 13 -> 14, of which waited for: 3 -> 4; matrix products, arithmetic and copies ran while one was open for 4% -> 4% of each run, Pallas kernels for 6% -> 10%
where the time goes in v4:
time: 95.3 us; the launch traced here: 94.6 us
  starting transfers between devices  64.6 us (68%)
  Pallas kernels  16.9 us (18%)
  waiting for transfers between devices  5.51 us (6%)
  other arithmetic  5.32 us (6%)
  local copies, waits for them, and re-layouts  1.34 us (1%)
    ppermute x12, starting transfers between devices, shift(): return lax.ppermute(value, ('dp', 'pool'), pairs)  44.7 us
    all_to_all x1, starting transfers between devices, body(): lax.all_to_all(spread, ('dp', 'pool'), 0, 0, axis_index_groups=near, tile...  10.2 us
    all_to_all x1, starting transfers between devices, body(): lax.all_to_all(part, 'dp', 0, 0, axis_index_groups=plane, tiled=True)  9.68 us
    pallas_call x1, Pallas kernels, body(): call(step_kernel, [SMEM, SMEM] + [ANY] * 4 + [VMEM] + [ANY] * 8, [(TOKEN,...  6.95 us
    pallas_call x1, Pallas kernels, body(): call(forward_kernel, [SMEM] + [ANY] * 4 + [VMEM] * 2, [(TOKEN, BF16, ANY)...  5.29 us
    pallas_call x1, Pallas kernels, body(): call(backward_kernel, [ANY] * 6, [(TOKEN, BF16, ANY)] * 3, [(TOKEN, BF16)...  4.62 us
    ppermute x12, waiting for transfers between devices, shift(): return lax.ppermute(value, ('dp', 'pool'), pairs)  2.97 us
    all_to_all x1, waiting for transfers between devices, body(): lax.all_to_all(spread, ('dp', 'pool'), 0, 0, axis_index_groups=near, tile...  2.53 us
  transfers between devices with their start and end apart: 14, of which 4 were waited for; matrix products, arithmetic and copies ran while one was open for 4% of the time, Pallas kernels for 10%

profile of v4, /device:TPU:1, one launch (start us, length us, event | category | flops | bytes accessed | tf_op | source)
XLA Modules:
  0.0 94.6 jit_solution(12086522627277378751)
XLA Ops:
  1.4 0.9 %pad_maximum_fusion.own = bf16[96,1152]{1,0:T(8,128)(2,1)S(1)} fusion(bf16[96,128]{1,0:T(8,128)(2,1)S(1)} %select_convert_fusion, bf16[96,1024]{1,0:T(8,128)(2,1)} %param.15), kind=kLoop, calls=%fused_computation.3 | loop fusion | flops 442368 | bytes 442368 | tf_op jit(solution)/shard_map/concatenate | solution.py:267
  2.4 6.6 %collective-permute-start.4 = (bf16[96,1152]{1,0:T(8,128)(2,1)S(1)}, bf16[96,1152]{1,0:T(8,128)(2,1)S(1)}, u32[]{:S(2)}, u32[]{:S(2)}) collective-permute-start(bf16[96,1152]{1,0:T(8,128)(2,1)S(1)} %pad_maximum_fusion.own), channel_id=1, source_target_pairs={{0,6},{1,7},{2,0},{3,1},{4,2},{5,3},{6,4},{7,5},{8,10},{9,11},{10,... | collective-permute-start | bytes 663560 | tf_op jit(solution)/shard_map/ppermute | solution.py:252
  9.0 6.8 %collective-permute-start.1 = (bf16[96,1152]{1,0:T(8,128)(2,1)S(1)}, bf16[96,1152]{1,0:T(8,128)(2,1)S(1)}, u32[]{:S(2)}, u32[]{:S(2)}) collective-permute-start(bf16[96,1152]{1,0:T(8,128)(2,1)S(1)} %pad_maximum_fusion.own), channel_id=1, source_target_pairs={{0,2},{1,3},{2,4},{3,5},{4,6},{5,7},{6,0},{7,1},{8,14},{9,15},{10,... | collective-permute-start | bytes 663560 | tf_op jit(solution)/shard_map/ppermute | solution.py:252
  15.8 3.1 %collective-permute-start.3 = (bf16[96,1152]{1,0:T(8,128)(2,1)S(1)}, bf16[96,1152]{1,0:T(8,128)(2,1)S(1)}, u32[]{:S(2)}, u32[]{:S(2)}) collective-permute-start(bf16[96,1152]{1,0:T(8,128)(2,1)S(1)} %pad_maximum_fusion.own), channel_id=1, source_target_pairs={{0,7},{1,0},{2,1},{3,2},{4,3},{5,4},{6,5},{7,6},{8,9},{9,10},{10,1... | collective-permute-start | bytes 663560 | tf_op jit(solution)/shard_map/ppermute | solution.py:252
  18.9 3.4 %collective-permute-start = (bf16[96,1152]{1,0:T(8,128)(2,1)S(1)}, bf16[96,1152]{1,0:T(8,128)(2,1)S(1)}, u32[]{:S(2)}, u32[]{:S(2)}) collective-permute-start(bf16[96,1152]{1,0:T(8,128)(2,1)S(1)} %pad_maximum_fusion.own), channel_id=1, source_target_pairs={{0,1},{1,2},{2,3},{3,4},{4,5},{5,6},{6,7},{7,0},{8,15},{9,8},{10,9... | collective-permute-start | bytes 663560 | tf_op jit(solution)/shard_map/ppermute | solution.py:252
  22.3 1.9 %collective-permute-start.6 = (bf16[96,1152]{1,0:T(8,128)(2,1)S(1)}, bf16[96,1152]{1,0:T(8,128)(2,1)S(1)}, u32[]{:S(2)}, u32[]{:S(2)}) collective-permute-start(bf16[96,1152]{1,0:T(8,128)(2,1)S(1)} %collective-permute-done.4.l2), channel_id=1, source_target_pairs={{0,6},{1,7},{2,0},{3,1},{4,2},{5,3},{6,4},{7,5},{8,10},{9,11},{10,... | collective-permute-start | bytes 663560 | tf_op jit(solution)/shard_map/ppermute | solution.py:252
  24.3 3.3 %collective-permute-start.5 = (bf16[96,1152]{1,0:T(8,128)(2,1)S(1)}, bf16[96,1152]{1,0:T(8,128)(2,1)S(1)}, u32[]{:S(2)}, u32[]{:S(2)}) collective-permute-start(bf16[96,1152]{1,0:T(8,128)(2,1)S(1)} %collective-permute-done.4.l2), channel_id=1, source_target_pairs={{0,7},{1,0},{2,1},{3,2},{4,3},{5,4},{6,5},{7,6},{8,9},{9,10},{10,1... | collective-permute-start | bytes 663560 | tf_op jit(solution)/shard_map/ppermute | solution.py:252
  27.6 3.2 %collective-permute-start.2 = (bf16[96,1152]{1,0:T(8,128)(2,1)S(1)}, bf16[96,1152]{1,0:T(8,128)(2,1)S(1)}, u32[]{:S(2)}, u32[]{:S(2)}) collective-permute-start(bf16[96,1152]{1,0:T(8,128)(2,1)S(1)} %collective-permute-done.1.r2), channel_id=1, source_target_pairs={{0,1},{1,2},{2,3},{3,4},{4,5},{5,6},{6,7},{7,0},{8,15},{9,8},{10,9... | collective-permute-start | bytes 663560 | tf_op jit(solution)/shard_map/ppermute | solution.py:252
  30.8 5.3 %shard_map.136 = (bf16[256,1024]{1,0:T(8,128)(2,1)}, f32[256,1024]{1,0:T(8,128)}, f32[256,128]{1,0:T(8,128)}, bf16[8,256,256]{2,1,0:T(8,128)(2,1)}, f32[8,256,256]{2,1,0:T(8,128)}) custom-call(s32[1,4]{1,0:T(1,128)} %lengths.1, bf16[256,1024]{1,0:T(8,128)(2,1)} %q_hbm.3, bf16[256,1024]{1,0:T(8,128)(2,1)} %k_hbm.3, bf16[256,1024]{1,0:T(8,128)(2,1)} %v_hbm.3, ...), custom_call_target="tpu_custom_call" | custom-call | flops 1000000000 | bytes 8000000 | tf_op jit(solution)/shard_map/pallas_call | solution.py:279
  36.6 1.3 %collective-permute-done.5.l3 = bf16[96,1152]{1,0:T(8,128)(2,1)S(1)} collective-permute-done((bf16[96,1152]{1,0:T(8,128)(2,1)S(1)}, bf16[96,1152]{1,0:T(8,128)(2,1)S(1)}, u32[]{:S(2)}, u32[]{:S(2)}) %collective-permute-start.5) | collective-permute-done | bytes 221216 | tf_op jit(solution)/shard_map/ppermute | solution.py:252
  37.9 1.2 %collective-permute-done.2.r3 = bf16[96,1152]{1,0:T(8,128)(2,1)S(1)} collective-permute-done((bf16[96,1152]{1,0:T(8,128)(2,1)S(1)}, bf16[96,1152]{1,0:T(8,128)(2,1)S(1)}, u32[]{:S(2)}, u32[]{:S(2)}) %collective-permute-start.2) | collective-permute-done | bytes 221216 | tf_op jit(solution)/shard_map/ppermute | solution.py:252
  39.8 7.0 %shard_map.137 = (bf16[256,1024]{1,0:T(8,128)(2,1)}, bf16[256,1024]{1,0:T(8,128)(2,1)}, f32[32,1,1024]{2,1,0:T(1,128)}, bf16[192,1024]{1,0:T(8,128)(2,1)}, bf16[...) custom-call(s32[1]{0:T(128)} %bitcast.place, ...), custom_call_target="tpu_custom_call" | custom-call | flops 2000000000 | bytes 8000000 | tf_op jit(solution)/shard_map/pallas_call | solution.py:288
  46.7 4.0 %collective-permute-start.7 = (bf16[192,1024]{1,0:T(8,128)(2,1)}, bf16[192,1024]{1,0:T(8,128)(2,1)S(1)}, u32[]{:S(2)}, u32[]{:S(2)}) collective-permute-start(bf16[192,1024]{1,0:T(8,128)(2,1)} %get-tuple-element.37), channel_id=1, source_target_pairs={{0,1},{1,2},{2,3},{3,4},{4,5},{5,6},{6,7},{7,0},{8,15},{9,8},{10,9... | collective-permute-start | bytes 1179656 | tf_op jit(solution)/shard_map/ppermute | solution.py:252
  50.7 1.9 %collective-permute-start.8 = (bf16[192,1024]{1,0:T(8,128)(2,1)}, bf16[192,1024]{1,0:T(8,128)(2,1)S(1)}, u32[]{:S(2)}, u32[]{:S(2)}) collective-permute-start(bf16[192,1024]{1,0:T(8,128)(2,1)} %get-tuple-element.38), channel_id=1, source_target_pairs={{0,7},{1,0},{2,1},{3,2},{4,3},{5,4},{6,5},{7,6},{8,9},{9,10},{10,1... | collective-permute-start | bytes 1179656 | tf_op jit(solution)/shard_map/ppermute | solution.py:252
  52.7 3.1 %collective-permute-start.9 = (bf16[96,1024]{1,0:T(8,128)(2,1)}, bf16[96,1024]{1,0:T(8,128)(2,1)S(1)}, u32[]{:S(2)}, u32[]{:S(2)}) collective-permute-start(bf16[96,1024]{1,0:T(8,128)(2,1)} %get-tuple-element.39), channel_id=1, source_target_pairs={{0,2},{1,3},{2,4},{3,5},{4,6},{5,7},{6,0},{7,1},{8,14},{9,15},{10,... | collective-permute-start | bytes 589832 | tf_op jit(solution)/shard_map/ppermute | solution.py:252
  55.8 9.7 %all-to-all-start = ((f32[32,1,1024]{2,1,0:T(1,128)}), f32[32,1,1024]{2,1,0:T(1,128)S(1)}, u32[]{:S(2)}, u32[]{:S(2)}) async-start(f32[32,1,1024]{2,1,0:T(1,128)} %get-tuple-element.45), calls=%async_computation | async-start | bytes 262144 | tf_op jit(solution)/shard_map/all_to_all | solution.py:311
  65.5 1.0 %add_convert_fusion = bf16[96,1024]{1,0:T(8,128)(2,1)S(1)} fusion(bf16[96,1024]{1,0:T(8,128)(2,1)} %get-tuple-element.44, bf16[192,1024]{1,0:T(8,128)(2,1)S(1)} %collective-permute-done.8), kind=kLoop, calls=%fused_computation.1 | loop fusion | flops 393216 | bytes 589824 | tf_op jit(solution)/shard_map/convert_element_type | solution.py:306
  66.5 3.1 %collective-permute-start.11 = (bf16[96,1024]{1,0:T(8,128)(2,1)S(1)}, bf16[96,1024]{1,0:T(8,128)(2,1)S(1)}, u32[]{:S(2)}, u32[]{:S(2)}) collective-permute-start(bf16[96,1024]{1,0:T(8,128)(2,1)S(1)} %add_convert_fusion), channel_id=1, source_target_pairs={{0,6},{1,7},{2,0},{3,1},{4,2},{5,3},{6,4},{7,5},{8,10},{9,11},{10,... | collective-permute-start | bytes 589832 | tf_op jit(solution)/shard_map/ppermute | solution.py:252
  69.6 1.0 %add_convert_fusion.1 = bf16[96,1024]{1,0:T(8,128)(2,1)S(1)} fusion(bf16[96,1024]{1,0:T(8,128)(2,1)S(1)} %collective-permute-done.9, bf16[96,1024]{1,0:T(8,128)(2,1)} %get-tuple-element.42, bf16[192,1024]{1,0:T(8,128)(2,1)S(1)} %collective-permute-done.7), kind=kLoop, calls=%fused_computation.2 | loop fusion | flops 589824 | bytes 786432 | tf_op jit(solution)/shard_map/convert_element_type | solution.py:305
  70.6 4.3 %collective-permute-start.10 = (bf16[96,1024]{1,0:T(8,128)(2,1)S(1)}, bf16[96,1024]{1,0:T(8,128)(2,1)S(1)}, u32[]{:S(2)}, u32[]{:S(2)}) collective-permute-start(bf16[96,1024]{1,0:T(8,128)(2,1)S(1)} %add_convert_fusion.1), channel_id=1, source_target_pairs={{0,2},{1,3},{2,4},{3,5},{4,6},{5,7},{6,0},{7,1},{8,14},{9,15},{10,... | collective-permute-start | bytes 589832 | tf_op jit(solution)/shard_map/ppermute | solution.py:252
  75.7 10.2 %all-to-all-start.1 = ((f32[16,1,1024]{2,1,0:T(1,128)}), f32[16,1,1024]{2,1,0:T(1,128)S(1)}, u32[]{:S(2)}, u32[]{:S(2)}) async-start(f32[16,1,1024]{2,1,0:T(1,128)} %broadcast_in_dim.27), calls=%async_computation.1 | async-start | bytes 131072 | tf_op jit(solution)/shard_map/all_to_all | solution.py:314
  85.9 4.6 %shard_map.138 = (bf16[256,1024]{1,0:T(8,128)(2,1)}, bf16[256,1024]{1,0:T(8,128)(2,1)}, bf16[256,1024]{1,0:T(8,128)(2,1)}) custom-call(bf16[256,1024]{1,0:T(8,128)(2,1)} %get-tuple-element.29.dmixed_hbm, bf16[256,1024]{1,0:T(8,128)(2,1)} %q_hbm.3, bf16[256,1024]{1,0:T(8,128)(2,1)} %k_hbm.3, bf16[256,1024]{1,0:T(8,128)(2,1)} %v_hbm.3, ...), custom_call_target="tpu_custom_call" | custom-call | flops 2000000000 | bytes 8000000 | tf_op jit(solution)/shard_map/pallas_call | solution.py:321
  90.5 2.5 %all-to-all-done.1 = f32[16,1,1024]{2,1,0:T(1,128)S(1)} async-done(((f32[16,1,1024]{2,1,0:T(1,128)}), f32[16,1,1024]{2,1,0:T(1,128)S(1)}, u32[]{:S(2)}, u32[]{:S(2)}) %all-to-all-start.1) | async-done | bytes 65568 | tf_op jit(solution)/shard_map/all_to_all | solution.py:314
  93.7 0.9 convert_add_fusion
  (35 shorter events, 3.3 us)
Async XLA Ops:
  2.4 36.7 %copy-start = (bf16[96,1152]{1,0:T(8,128)(2,1)}, bf16[96,1152]{1,0:T(8,128)(2,1)S(1)}, u32[]{:S(2)}) copy-start(bf16[96,1152]{1,0:T(8,128)(2,1)S(1)} %pad_maximum_fusion.own) | copy-start | bytes 663556
  2.4 19.9 %collective-permute-start.4 = (bf16[96,1152]{1,0:T(8,128)(2,1)S(1)}, bf16[96,1152]{1,0:T(8,128)(2,1)S(1)}, u32[]{:S(2)}, u32[]{:S(2)}) collective-permute-start(bf16[96,1152]{1,0:T(8,128)(2,1)S(1)} %pad_maximum_fusion.own), channel_id=1, source_target_pairs={{0,6},{1,7},{2,0},{3,1},{4,2},{5,3},{6,4},{7,5},{8,10},{9,11},{10,... | collective-permute-start | bytes 663560 | tf_op jit(solution)/shard_map/ppermute | solution.py:252
  9.0 18.6 %collective-permute-start.1 = (bf16[96,1152]{1,0:T(8,128)(2,1)S(1)}, bf16[96,1152]{1,0:T(8,128)(2,1)S(1)}, u32[]{:S(2)}, u32[]{:S(2)}) collective-permute-start(bf16[96,1152]{1,0:T(8,128)(2,1)S(1)} %pad_maximum_fusion.own), channel_id=1, source_target_pairs={{0,2},{1,3},{2,4},{3,5},{4,6},{5,7},{6,0},{7,1},{8,14},{9,15},{10,... | collective-permute-start | bytes 663560 | tf_op jit(solution)/shard_map/ppermute | solution.py:252
  15.8 20.3 %collective-permute-start.3 = (bf16[96,1152]{1,0:T(8,128)(2,1)S(1)}, bf16[96,1152]{1,0:T(8,128)(2,1)S(1)}, u32[]{:S(2)}, u32[]{:S(2)}) collective-permute-start(bf16[96,1152]{1,0:T(8,128)(2,1)S(1)} %pad_maximum_fusion.own), channel_id=1, source_target_pairs={{0,7},{1,0},{2,1},{3,2},{4,3},{5,4},{6,5},{7,6},{8,9},{9,10},{10,1... | collective-permute-start | bytes 663560 | tf_op jit(solution)/shard_map/ppermute | solution.py:252
  18.9 17.2 %collective-permute-start = (bf16[96,1152]{1,0:T(8,128)(2,1)S(1)}, bf16[96,1152]{1,0:T(8,128)(2,1)S(1)}, u32[]{:S(2)}, u32[]{:S(2)}) collective-permute-start(bf16[96,1152]{1,0:T(8,128)(2,1)S(1)} %pad_maximum_fusion.own), channel_id=1, source_target_pairs={{0,1},{1,2},{2,3},{3,4},{4,5},{5,6},{6,7},{7,0},{8,15},{9,8},{10,9... | collective-permute-start | bytes 663560 | tf_op jit(solution)/shard_map/ppermute | solution.py:252
  22.3 16.8 %copy-start.2 = (bf16[96,1152]{1,0:T(8,128)(2,1)}, bf16[96,1152]{1,0:T(8,128)(2,1)S(1)}, u32[]{:S(2)}) copy-start(bf16[96,1152]{1,0:T(8,128)(2,1)S(1)} %collective-permute-done.4.l2) | copy-start | bytes 663556
  22.3 14.3 %collective-permute-start.6 = (bf16[96,1152]{1,0:T(8,128)(2,1)S(1)}, bf16[96,1152]{1,0:T(8,128)(2,1)S(1)}, u32[]{:S(2)}, u32[]{:S(2)}) collective-permute-start(bf16[96,1152]{1,0:T(8,128)(2,1)S(1)} %collective-permute-done.4.l2), channel_id=1, source_target_pairs={{0,6},{1,7},{2,0},{3,1},{4,2},{5,3},{6,4},{7,5},{8,10},{9,11},{10,... | collective-permute-start | bytes 663560 | tf_op jit(solution)/shard_map/ppermute | solution.py:252
  24.3 13.7 %collective-permute-start.5 = (bf16[96,1152]{1,0:T(8,128)(2,1)S(1)}, bf16[96,1152]{1,0:T(8,128)(2,1)S(1)}, u32[]{:S(2)}, u32[]{:S(2)}) collective-permute-start(bf16[96,1152]{1,0:T(8,128)(2,1)S(1)} %collective-permute-done.4.l2), channel_id=1, source_target_pairs={{0,7},{1,0},{2,1},{3,2},{4,3},{5,4},{6,5},{7,6},{8,9},{9,10},{10,1... | collective-permute-start | bytes 663560 | tf_op jit(solution)/shard_map/ppermute | solution.py:252
  27.6 11.5 %copy-start.3 = (bf16[96,1152]{1,0:T(8,128)(2,1)}, bf16[96,1152]{1,0:T(8,128)(2,1)S(1)}, u32[]{:S(2)}) copy-start(bf16[96,1152]{1,0:T(8,128)(2,1)S(1)} %collective-permute-done.1.r2) | copy-start | bytes 663556
  27.6 11.5 %collective-permute-start.2 = (bf16[96,1152]{1,0:T(8,128)(2,1)S(1)}, bf16[96,1152]{1,0:T(8,128)(2,1)S(1)}, u32[]{:S(2)}, u32[]{:S(2)}) collective-permute-start(bf16[96,1152]{1,0:T(8,128)(2,1)S(1)} %collective-permute-done.1.r2), channel_id=1, source_target_pairs={{0,1},{1,2},{2,3},{3,4},{4,5},{5,6},{6,7},{7,0},{8,15},{9,8},{10,9... | collective-permute-start | bytes 663560 | tf_op jit(solution)/shard_map/ppermute | solution.py:252
  36.1 3.0 %copy-start.4 = (bf16[96,1152]{1,0:T(8,128)(2,1)}, bf16[96,1152]{1,0:T(8,128)(2,1)S(1)}, u32[]{:S(2)}) copy-start(bf16[96,1152]{1,0:T(8,128)(2,1)S(1)} %collective-permute-done.3.l1) | copy-start | bytes 663556
  36.1 3.0 %copy-start.5 = (bf16[96,1152]{1,0:T(8,128)(2,1)}, bf16[96,1152]{1,0:T(8,128)(2,1)S(1)}, u32[]{:S(2)}) copy-start(bf16[96,1152]{1,0:T(8,128)(2,1)S(1)} %collective-permute-done.r1) | copy-start | bytes 663556
  36.6 2.5 %copy-start.6 = (bf16[96,1152]{1,0:T(8,128)(2,1)}, bf16[96,1152]{1,0:T(8,128)(2,1)S(1)}, u32[]{:S(2)}) copy-start(bf16[96,1152]{1,0:T(8,128)(2,1)S(1)} %collective-permute-done.6.l4) | copy-start | bytes 663556
  37.9 1.2 %copy-start.7 = (bf16[96,1152]{1,0:T(8,128)(2,1)}, bf16[96,1152]{1,0:T(8,128)(2,1)S(1)}, u32[]{:S(2)}) copy-start(bf16[96,1152]{1,0:T(8,128)(2,1)S(1)} %collective-permute-done.5.l3) | copy-start | bytes 663556
  39.1 0.7 copy-start.8
  46.7 18.7 %collective-permute-start.7 = (bf16[192,1024]{1,0:T(8,128)(2,1)}, bf16[192,1024]{1,0:T(8,128)(2,1)S(1)}, u32[]{:S(2)}, u32[]{:S(2)}) collective-permute-start(bf16[192,1024]{1,0:T(8,128)(2,1)} %get-tuple-element.37), channel_id=1, source_target_pairs={{0,1},{1,2},{2,3},{3,4},{4,5},{5,6},{6,7},{7,0},{8,15},{9,8},{10,9... | collective-permute-start | bytes 1179656 | tf_op jit(solution)/shard_map/ppermute | solution.py:252
  50.7 14.7 %collective-permute-start.8 = (bf16[192,1024]{1,0:T(8,128)(2,1)}, bf16[192,1024]{1,0:T(8,128)(2,1)S(1)}, u32[]{:S(2)}, u32[]{:S(2)}) collective-permute-start(bf16[192,1024]{1,0:T(8,128)(2,1)} %get-tuple-element.38), channel_id=1, source_target_pairs={{0,7},{1,0},{2,1},{3,2},{4,3},{5,4},{6,5},{7,6},{8,9},{9,10},{10,1... | collective-permute-start | bytes 1179656 | tf_op jit(solution)/shard_map/ppermute | solution.py:252
  52.7 12.8 %collective-permute-start.9 = (bf16[96,1024]{1,0:T(8,128)(2,1)}, bf16[96,1024]{1,0:T(8,128)(2,1)S(1)}, u32[]{:S(2)}, u32[]{:S(2)}) collective-permute-start(bf16[96,1024]{1,0:T(8,128)(2,1)} %get-tuple-element.39), channel_id=1, source_target_pairs={{0,2},{1,3},{2,4},{3,5},{4,6},{5,7},{6,0},{7,1},{8,14},{9,15},{10,... | collective-permute-start | bytes 589832 | tf_op jit(solution)/shard_map/ppermute | solution.py:252
  55.8 19.1 %all-to-all-start = ((f32[32,1,1024]{2,1,0:T(1,128)}), f32[32,1,1024]{2,1,0:T(1,128)S(1)}, u32[]{:S(2)}, u32[]{:S(2)}) async-start(f32[32,1,1024]{2,1,0:T(1,128)} %get-tuple-element.45), calls=%async_computation | async-start | bytes 262144 | tf_op jit(solution)/shard_map/all_to_all | solution.py:311
  66.5 27.2 %collective-permute-start.11 = (bf16[96,1024]{1,0:T(8,128)(2,1)S(1)}, bf16[96,1024]{1,0:T(8,128)(2,1)S(1)}, u32[]{:S(2)}, u32[]{:S(2)}) collective-permute-start(bf16[96,1024]{1,0:T(8,128)(2,1)S(1)} %add_convert_fusion), channel_id=1, source_target_pairs={{0,6},{1,7},{2,0},{3,1},{4,2},{5,3},{6,4},{7,5},{8,10},{9,11},{10,... | collective-permute-start | bytes 589832 | tf_op jit(solution)/shard_map/ppermute | solution.py:252
  70.6 23.1 %collective-permute-start.10 = (bf16[96,1024]{1,0:T(8,128)(2,1)S(1)}, bf16[96,1024]{1,0:T(8,128)(2,1)S(1)}, u32[]{:S(2)}, u32[]{:S(2)}) collective-permute-start(bf16[96,1024]{1,0:T(8,128)(2,1)S(1)} %add_convert_fusion.1), channel_id=1, source_target_pairs={{0,2},{1,3},{2,4},{3,5},{4,6},{5,7},{6,0},{7,1},{8,14},{9,15},{10,... | collective-permute-start | bytes 589832 | tf_op jit(solution)/shard_map/ppermute | solution.py:252
  75.7 17.4 %all-to-all-start.1 = ((f32[16,1,1024]{2,1,0:T(1,128)}), f32[16,1,1024]{2,1,0:T(1,128)S(1)}, u32[]{:S(2)}, u32[]{:S(2)}) async-start(f32[16,1,1024]{2,1,0:T(1,128)} %broadcast_in_dim.27), calls=%async_computation.1 | async-start | bytes 131072 | tf_op jit(solution)/shard_map/all_to_all | solution.py:314
  85.9 7.8 %copy-start.1 = (bf16[96,1024]{1,0:T(8,128)(2,1)S(1)}, bf16[96,1024]{1,0:T(8,128)(2,1)}, u32[]{:S(2)}) copy-start(bf16[96,1024]{1,0:T(8,128)(2,1)} %get-tuple-element.36) | copy-start | bytes 589828

commit v5 on v4

--- a/solution.py
+++ b/solution.py
@@ -310,14 +310,15 @@
     plane = [[x * 16 + y * 2 + c for x in range(4) for y in range(8)] for c in range(2)]
     spread = lax.all_to_all(part, "dp", 0, 0, axis_index_groups=plane, tiled=True)
     spread = jnp.broadcast_to(jnp.sum(spread, axis=0, keepdims=True), (NEAR, 1, WIDTH))
+    spread, dmixed = lax.optimization_barrier((spread, dmixed))
     near = [[i * NEAR + j for j in range(NEAR)] for i in range(XY)]
     spread = lax.all_to_all(spread, ("dp", "pool"), 0, 0, axis_index_groups=near, tiled=True)
-    gain_grad = jnp.sum(spread, axis=0).reshape(WIDTH)
-
     pool_grad = (
         kept.astype(F32) + from_left[ROWS:].astype(F32) + from_right[ROWS:].astype(F32)
         + two_left.astype(F32) + two_right.astype(F32)
     )
+    spread, pool_grad = lax.optimization_barrier((spread, pool_grad))
+    gain_grad = jnp.sum(spread, axis=0).reshape(WIDTH)
     dq, dk, dv = call(
         backward_kernel,
         [ANY] * 6,

time: 95.3 us -> 94.4 us (level)
  transfers between devices with their start and end apart: 14 -> 14, of which waited for: 4 -> 4; matrix products, arithmetic and copies ran while one was open for 4% -> 4% of each run, Pallas kernels for 10% -> 11%
where the time goes in v5:
time: 94.4 us; the launch traced here: 93.7 us
  starting transfers between devices  64.6 us (68%)
  Pallas kernels  16.9 us (18%)
  other arithmetic  5.32 us (6%)
  waiting for transfers between devices  4.58 us (5%)
  local copies, waits for them, and re-layouts  1.35 us (1%)
  between operations  0.97 us (1%)
    ppermute x12, starting transfers between devices, shift(): return lax.ppermute(value, ('dp', 'pool'), pairs)  44.7 us
    all_to_all x1, starting transfers between devices, body(): lax.all_to_all(spread, ('dp', 'pool'), 0, 0, axis_index_groups=near, tile...  10.2 us
    all_to_all x1, starting transfers between devices, body(): lax.all_to_all(part, 'dp', 0, 0, axis_index_groups=plane, tiled=True)  9.68 us
    pallas_call x1, Pallas kernels, body(): call(step_kernel, [SMEM, SMEM] + [ANY] * 4 + [VMEM] + [ANY] * 8, [(TOKEN,...  6.95 us
    pallas_call x1, Pallas kernels, body(): call(forward_kernel, [SMEM] + [ANY] * 4 + [VMEM] * 2, [(TOKEN, BF16, ANY)...  5.29 us
    pallas_call x1, Pallas kernels, body(): call(backward_kernel, [ANY] * 6, [(TOKEN, BF16, ANY)] * 3, [(TOKEN, BF16)...  4.62 us
    ppermute x12, waiting for transfers between devices, shift(): return lax.ppermute(value, ('dp', 'pool'), pairs)  2.97 us
  transfers between devices with their start and end apart: 14, of which 4 were waited for; matrix products, arithmetic and copies ran while one was open for 4% of the time, Pallas kernels for 11%

profile of v5, /device:TPU:1, one launch (start us, length us, event | category | flops | bytes accessed | tf_op | source)
XLA Modules:
  0.0 93.7 jit_solution(14872516443602693931)
XLA Ops:
  1.4 0.9 %pad_maximum_fusion.own = bf16[96,1152]{1,0:T(8,128)(2,1)S(1)} fusion(bf16[96,128]{1,0:T(8,128)(2,1)S(1)} %select_convert_fusion, bf16[96,1024]{1,0:T(8,128)(2,1)} %param.15), kind=kLoop, calls=%fused_computation.3 | loop fusion | flops 442368 | bytes 442368 | tf_op jit(solution)/shard_map/concatenate | solution.py:267
  2.4 6.6 %collective-permute-start.4 = (bf16[96,1152]{1,0:T(8,128)(2,1)S(1)}, bf16[96,1152]{1,0:T(8,128)(2,1)S(1)}, u32[]{:S(2)}, u32[]{:S(2)}) collective-permute-start(bf16[96,1152]{1,0:T(8,128)(2,1)S(1)} %pad_maximum_fusion.own), channel_id=1, source_target_pairs={{0,6},{1,7},{2,0},{3,1},{4,2},{5,3},{6,4},{7,5},{8,10},{9,11},{10,... | collective-permute-start | bytes 663560 | tf_op jit(solution)/shard_map/ppermute | solution.py:252
  9.0 6.8 %collective-permute-start.1 = (bf16[96,1152]{1,0:T(8,128)(2,1)S(1)}, bf16[96,1152]{1,0:T(8,128)(2,1)S(1)}, u32[]{:S(2)}, u32[]{:S(2)}) collective-permute-start(bf16[96,1152]{1,0:T(8,128)(2,1)S(1)} %pad_maximum_fusion.own), channel_id=1, source_target_pairs={{0,2},{1,3},{2,4},{3,5},{4,6},{5,7},{6,0},{7,1},{8,14},{9,15},{10,... | collective-permute-start | bytes 663560 | tf_op jit(solution)/shard_map/ppermute | solution.py:252
  15.8 3.1 %collective-permute-start.3 = (bf16[96,1152]{1,0:T(8,128)(2,1)S(1)}, bf16[96,1152]{1,0:T(8,128)(2,1)S(1)}, u32[]{:S(2)}, u32[]{:S(2)}) collective-permute-start(bf16[96,1152]{1,0:T(8,128)(2,1)S(1)} %pad_maximum_fusion.own), channel_id=1, source_target_pairs={{0,7},{1,0},{2,1},{3,2},{4,3},{5,4},{6,5},{7,6},{8,9},{9,10},{10,1... | collective-permute-start | bytes 663560 | tf_op jit(solution)/shard_map/ppermute | solution.py:252
  18.9 3.4 %collective-permute-start = (bf16[96,1152]{1,0:T(8,128)(2,1)S(1)}, bf16[96,1152]{1,0:T(8,128)(2,1)S(1)}, u32[]{:S(2)}, u32[]{:S(2)}) collective-permute-start(bf16[96,1152]{1,0:T(8,128)(2,1)S(1)} %pad_maximum_fusion.own), channel_id=1, source_target_pairs={{0,1},{1,2},{2,3},{3,4},{4,5},{5,6},{6,7},{7,0},{8,15},{9,8},{10,9... | collective-permute-start | bytes 663560 | tf_op jit(solution)/shard_map/ppermute | solution.py:252
  22.3 1.9 %collective-permute-start.6 = (bf16[96,1152]{1,0:T(8,128)(2,1)S(1)}, bf16[96,1152]{1,0:T(8,128)(2,1)S(1)}, u32[]{:S(2)}, u32[]{:S(2)}) collective-permute-start(bf16[96,1152]{1,0:T(8,128)(2,1)S(1)} %collective-permute-done.4.l2), channel_id=1, source_target_pairs={{0,6},{1,7},{2,0},{3,1},{4,2},{5,3},{6,4},{7,5},{8,10},{9,11},{10,... | collective-permute-start | bytes 663560 | tf_op jit(solution)/shard_map/ppermute | solution.py:252
  24.3 3.3 %collective-permute-start.5 = (bf16[96,1152]{1,0:T(8,128)(2,1)S(1)}, bf16[96,1152]{1,0:T(8,128)(2,1)S(1)}, u32[]{:S(2)}, u32[]{:S(2)}) collective-permute-start(bf16[96,1152]{1,0:T(8,128)(2,1)S(1)} %collective-permute-done.4.l2), channel_id=1, source_target_pairs={{0,7},{1,0},{2,1},{3,2},{4,3},{5,4},{6,5},{7,6},{8,9},{9,10},{10,1... | collective-permute-start | bytes 663560 | tf_op jit(solution)/shard_map/ppermute | solution.py:252
  27.6 3.2 %collective-permute-start.2 = (bf16[96,1152]{1,0:T(8,128)(2,1)S(1)}, bf16[96,1152]{1,0:T(8,128)(2,1)S(1)}, u32[]{:S(2)}, u32[]{:S(2)}) collective-permute-start(bf16[96,1152]{1,0:T(8,128)(2,1)S(1)} %collective-permute-done.1.r2), channel_id=1, source_target_pairs={{0,1},{1,2},{2,3},{3,4},{4,5},{5,6},{6,7},{7,0},{8,15},{9,8},{10,9... | collective-permute-start | bytes 663560 | tf_op jit(solution)/shard_map/ppermute | solution.py:252
  30.8 5.3 %shard_map.136 = (bf16[256,1024]{1,0:T(8,128)(2,1)}, f32[256,1024]{1,0:T(8,128)}, f32[256,128]{1,0:T(8,128)}, bf16[8,256,256]{2,1,0:T(8,128)(2,1)}, f32[8,256,256]{2,1,0:T(8,128)}) custom-call(s32[1,4]{1,0:T(1,128)} %lengths.1, bf16[256,1024]{1,0:T(8,128)(2,1)} %q_hbm.3, bf16[256,1024]{1,0:T(8,128)(2,1)} %k_hbm.3, bf16[256,1024]{1,0:T(8,128)(2,1)} %v_hbm.3, ...), custom_call_target="tpu_custom_call" | custom-call | flops 1000000000 | bytes 8000000 | tf_op jit(solution)/shard_map/pallas_call | solution.py:279
  36.6 1.3 %collective-permute-done.5.l3 = bf16[96,1152]{1,0:T(8,128)(2,1)S(1)} collective-permute-done((bf16[96,1152]{1,0:T(8,128)(2,1)S(1)}, bf16[96,1152]{1,0:T(8,128)(2,1)S(1)}, u32[]{:S(2)}, u32[]{:S(2)}) %collective-permute-start.5) | collective-permute-done | bytes 221216 | tf_op jit(solution)/shard_map/ppermute | solution.py:252
  37.9 1.2 %collective-permute-done.2.r3 = bf16[96,1152]{1,0:T(8,128)(2,1)S(1)} collective-permute-done((bf16[96,1152]{1,0:T(8,128)(2,1)S(1)}, bf16[96,1152]{1,0:T(8,128)(2,1)S(1)}, u32[]{:S(2)}, u32[]{:S(2)}) %collective-permute-start.2) | collective-permute-done | bytes 221216 | tf_op jit(solution)/shard_map/ppermute | solution.py:252
  39.8 7.0 %shard_map.137 = (bf16[256,1024]{1,0:T(8,128)(2,1)}, bf16[256,1024]{1,0:T(8,128)(2,1)}, f32[32,1,1024]{2,1,0:T(1,128)}, bf16[192,1024]{1,0:T(8,128)(2,1)}, bf16[...) custom-call(s32[1]{0:T(128)} %bitcast.place, ...), custom_call_target="tpu_custom_call" | custom-call | flops 2000000000 | bytes 8000000 | tf_op jit(solution)/shard_map/pallas_call | solution.py:288
  46.7 4.0 %collective-permute-start.7 = (bf16[192,1024]{1,0:T(8,128)(2,1)}, bf16[192,1024]{1,0:T(8,128)(2,1)S(1)}, u32[]{:S(2)}, u32[]{:S(2)}) collective-permute-start(bf16[192,1024]{1,0:T(8,128)(2,1)} %get-tuple-element.44), channel_id=1, source_target_pairs={{0,1},{1,2},{2,3},{3,4},{4,5},{5,6},{6,7},{7,0},{8,15},{9,8},{10,9... | collective-permute-start | bytes 1179656 | tf_op jit(solution)/shard_map/ppermute | solution.py:252
  50.7 1.9 %collective-permute-start.8 = (bf16[192,1024]{1,0:T(8,128)(2,1)}, bf16[192,1024]{1,0:T(8,128)(2,1)S(1)}, u32[]{:S(2)}, u32[]{:S(2)}) collective-permute-start(bf16[192,1024]{1,0:T(8,128)(2,1)} %get-tuple-element.45), channel_id=1, source_target_pairs={{0,7},{1,0},{2,1},{3,2},{4,3},{5,4},{6,5},{7,6},{8,9},{9,10},{10,1... | collective-permute-start | bytes 1179656 | tf_op jit(solution)/shard_map/ppermute | solution.py:252
  52.7 3.1 %collective-permute-start.9 = (bf16[96,1024]{1,0:T(8,128)(2,1)}, bf16[96,1024]{1,0:T(8,128)(2,1)S(1)}, u32[]{:S(2)}, u32[]{:S(2)}) collective-permute-start(bf16[96,1024]{1,0:T(8,128)(2,1)} %get-tuple-element.46), channel_id=1, source_target_pairs={{0,2},{1,3},{2,4},{3,5},{4,6},{5,7},{6,0},{7,1},{8,14},{9,15},{10,... | collective-permute-start | bytes 589832 | tf_op jit(solution)/shard_map/ppermute | solution.py:252
  55.8 9.7 %all-to-all-start = ((f32[32,1,1024]{2,1,0:T(1,128)}), f32[32,1,1024]{2,1,0:T(1,128)S(1)}, u32[]{:S(2)}, u32[]{:S(2)}) async-start(f32[32,1,1024]{2,1,0:T(1,128)} %get-tuple-element.33), calls=%async_computation | async-start | bytes 262144 | tf_op jit(solution)/shard_map/all_to_all | solution.py:311
  65.5 1.0 %add_convert_fusion = bf16[96,1024]{1,0:T(8,128)(2,1)S(1)} fusion(bf16[96,1024]{1,0:T(8,128)(2,1)} %get-tuple-element.51, bf16[192,1024]{1,0:T(8,128)(2,1)S(1)} %collective-permute-done.8), kind=kLoop, calls=%fused_computation.1 | loop fusion | flops 393216 | bytes 589824 | tf_op jit(solution)/shard_map/convert_element_type | solution.py:306
  66.5 3.1 %collective-permute-start.11 = (bf16[96,1024]{1,0:T(8,128)(2,1)S(1)}, bf16[96,1024]{1,0:T(8,128)(2,1)S(1)}, u32[]{:S(2)}, u32[]{:S(2)}) collective-permute-start(bf16[96,1024]{1,0:T(8,128)(2,1)S(1)} %add_convert_fusion), channel_id=1, source_target_pairs={{0,6},{1,7},{2,0},{3,1},{4,2},{5,3},{6,4},{7,5},{8,10},{9,11},{10,... | collective-permute-start | bytes 589832 | tf_op jit(solution)/shard_map/ppermute | solution.py:252
  69.6 1.0 %add_convert_fusion.1 = bf16[96,1024]{1,0:T(8,128)(2,1)S(1)} fusion(bf16[96,1024]{1,0:T(8,128)(2,1)S(1)} %collective-permute-done.9, bf16[96,1024]{1,0:T(8,128)(2,1)} %get-tuple-element.49, bf16[192,1024]{1,0:T(8,128)(2,1)S(1)} %collective-permute-done.7), kind=kLoop, calls=%fused_computation.2 | loop fusion | flops 589824 | bytes 786432 | tf_op jit(solution)/shard_map/convert_element_type | solution.py:305
  70.6 4.3 %collective-permute-start.10 = (bf16[96,1024]{1,0:T(8,128)(2,1)S(1)}, bf16[96,1024]{1,0:T(8,128)(2,1)S(1)}, u32[]{:S(2)}, u32[]{:S(2)}) collective-permute-start(bf16[96,1024]{1,0:T(8,128)(2,1)S(1)} %add_convert_fusion.1), channel_id=1, source_target_pairs={{0,2},{1,3},{2,4},{3,5},{4,6},{5,7},{6,0},{7,1},{8,14},{9,15},{10,... | collective-permute-start | bytes 589832 | tf_op jit(solution)/shard_map/ppermute | solution.py:252
  75.7 10.2 %all-to-all-start.1 = ((f32[16,1,1024]{2,1,0:T(1,128)}), f32[16,1,1024]{2,1,0:T(1,128)S(1)}, u32[]{:S(2)}, u32[]{:S(2)}) async-start(f32[16,1,1024]{2,1,0:T(1,128)} %broadcast_in_dim.27), calls=%async_computation.1 | async-start | bytes 131072 | tf_op jit(solution)/shard_map/all_to_all | solution.py:315
  85.9 4.6 %shard_map.138 = (bf16[256,1024]{1,0:T(8,128)(2,1)}, bf16[256,1024]{1,0:T(8,128)(2,1)}, bf16[256,1024]{1,0:T(8,128)(2,1)}) custom-call(bf16[256,1024]{1,0:T(8,128)(2,1)} %get-tuple-element.35.dmixed_hbm, bf16[256,1024]{1,0:T(8,128)(2,1)} %q_hbm.3, bf16[256,1024]{1,0:T(8,128)(2,1)} %k_hbm.3, bf16[256,1024]{1,0:T(8,128)(2,1)} %v_hbm.3, ...), custom_call_target="tpu_custom_call" | custom-call | flops 2000000000 | bytes 8000000 | tf_op jit(solution)/shard_map/pallas_call | solution.py:322
  90.5 0.9 convert_add_fusion
  91.4 1.6 %all-to-all-done.1 = f32[16,1,1024]{2,1,0:T(1,128)S(1)} async-done(((f32[16,1,1024]{2,1,0:T(1,128)}), f32[16,1,1024]{2,1,0:T(1,128)S(1)}, u32[]{:S(2)}, u32[]{:S(2)}) %all-to-all-start.1) | async-done | bytes 65568 | tf_op jit(solution)/shard_map/all_to_all | solution.py:315
  (35 shorter events, 3.3 us)
Async XLA Ops:
  2.4 36.7 %copy-start = (bf16[96,1152]{1,0:T(8,128)(2,1)}, bf16[96,1152]{1,0:T(8,128)(2,1)S(1)}, u32[]{:S(2)}) copy-start(bf16[96,1152]{1,0:T(8,128)(2,1)S(1)} %pad_maximum_fusion.own) | copy-start | bytes 663556
  2.4 19.9 %collective-permute-start.4 = (bf16[96,1152]{1,0:T(8,128)(2,1)S(1)}, bf16[96,1152]{1,0:T(8,128)(2,1)S(1)}, u32[]{:S(2)}, u32[]{:S(2)}) collective-permute-start(bf16[96,1152]{1,0:T(8,128)(2,1)S(1)} %pad_maximum_fusion.own), channel_id=1, source_target_pairs={{0,6},{1,7},{2,0},{3,1},{4,2},{5,3},{6,4},{7,5},{8,10},{9,11},{10,... | collective-permute-start | bytes 663560 | tf_op jit(solution)/shard_map/ppermute | solution.py:252
  9.0 18.6 %collective-permute-start.1 = (bf16[96,1152]{1,0:T(8,128)(2,1)S(1)}, bf16[96,1152]{1,0:T(8,128)(2,1)S(1)}, u32[]{:S(2)}, u32[]{:S(2)}) collective-permute-start(bf16[96,1152]{1,0:T(8,128)(2,1)S(1)} %pad_maximum_fusion.own), channel_id=1, source_target_pairs={{0,2},{1,3},{2,4},{3,5},{4,6},{5,7},{6,0},{7,1},{8,14},{9,15},{10,... | collective-permute-start | bytes 663560 | tf_op jit(solution)/shard_map/ppermute | solution.py:252
  15.8 20.3 %collective-permute-start.3 = (bf16[96,1152]{1,0:T(8,128)(2,1)S(1)}, bf16[96,1152]{1,0:T(8,128)(2,1)S(1)}, u32[]{:S(2)}, u32[]{:S(2)}) collective-permute-start(bf16[96,1152]{1,0:T(8,128)(2,1)S(1)} %pad_maximum_fusion.own), channel_id=1, source_target_pairs={{0,7},{1,0},{2,1},{3,2},{4,3},{5,4},{6,5},{7,6},{8,9},{9,10},{10,1... | collective-permute-start | bytes 663560 | tf_op jit(solution)/shard_map/ppermute | solution.py:252
  18.9 17.2 %collective-permute-start = (bf16[96,1152]{1,0:T(8,128)(2,1)S(1)}, bf16[96,1152]{1,0:T(8,128)(2,1)S(1)}, u32[]{:S(2)}, u32[]{:S(2)}) collective-permute-start(bf16[96,1152]{1,0:T(8,128)(2,1)S(1)} %pad_maximum_fusion.own), channel_id=1, source_target_pairs={{0,1},{1,2},{2,3},{3,4},{4,5},{5,6},{6,7},{7,0},{8,15},{9,8},{10,9... | collective-permute-start | bytes 663560 | tf_op jit(solution)/shard_map/ppermute | solution.py:252
  22.3 16.8 %copy-start.2 = (bf16[96,1152]{1,0:T(8,128)(2,1)}, bf16[96,1152]{1,0:T(8,128)(2,1)S(1)}, u32[]{:S(2)}) copy-start(bf16[96,1152]{1,0:T(8,128)(2,1)S(1)} %collective-permute-done.4.l2) | copy-start | bytes 663556
  22.3 14.3 %collective-permute-start.6 = (bf16[96,1152]{1,0:T(8,128)(2,1)S(1)}, bf16[96,1152]{1,0:T(8,128)(2,1)S(1)}, u32[]{:S(2)}, u32[]{:S(2)}) collective-permute-start(bf16[96,1152]{1,0:T(8,128)(2,1)S(1)} %collective-permute-done.4.l2), channel_id=1, source_target_pairs={{0,6},{1,7},{2,0},{3,1},{4,2},{5,3},{6,4},{7,5},{8,10},{9,11},{10,... | collective-permute-start | bytes 663560 | tf_op jit(solution)/shard_map/ppermute | solution.py:252
  24.3 13.7 %collective-permute-start.5 = (bf16[96,1152]{1,0:T(8,128)(2,1)S(1)}, bf16[96,1152]{1,0:T(8,128)(2,1)S(1)}, u32[]{:S(2)}, u32[]{:S(2)}) collective-permute-start(bf16[96,1152]{1,0:T(8,128)(2,1)S(1)} %collective-permute-done.4.l2), channel_id=1, source_target_pairs={{0,7},{1,0},{2,1},{3,2},{4,3},{5,4},{6,5},{7,6},{8,9},{9,10},{10,1... | collective-permute-start | bytes 663560 | tf_op jit(solution)/shard_map/ppermute | solution.py:252
  27.6 11.5 %copy-start.3 = (bf16[96,1152]{1,0:T(8,128)(2,1)}, bf16[96,1152]{1,0:T(8,128)(2,1)S(1)}, u32[]{:S(2)}) copy-start(bf16[96,1152]{1,0:T(8,128)(2,1)S(1)} %collective-permute-done.1.r2) | copy-start | bytes 663556
  27.6 11.5 %collective-permute-start.2 = (bf16[96,1152]{1,0:T(8,128)(2,1)S(1)}, bf16[96,1152]{1,0:T(8,128)(2,1)S(1)}, u32[]{:S(2)}, u32[]{:S(2)}) collective-permute-start(bf16[96,1152]{1,0:T(8,128)(2,1)S(1)} %collective-permute-done.1.r2), channel_id=1, source_target_pairs={{0,1},{1,2},{2,3},{3,4},{4,5},{5,6},{6,7},{7,0},{8,15},{9,8},{10,9... | collective-permute-start | bytes 663560 | tf_op jit(solution)/shard_map/ppermute | solution.py:252
  36.1 3.0 %copy-start.4 = (bf16[96,1152]{1,0:T(8,128)(2,1)}, bf16[96,1152]{1,0:T(8,128)(2,1)S(1)}, u32[]{:S(2)}) copy-start(bf16[96,1152]{1,0:T(8,128)(2,1)S(1)} %collective-permute-done.3.l1) | copy-start | bytes 663556
  36.1 3.0 %copy-start.5 = (bf16[96,1152]{1,0:T(8,128)(2,1)}, bf16[96,1152]{1,0:T(8,128)(2,1)S(1)}, u32[]{:S(2)}) copy-start(bf16[96,1152]{1,0:T(8,128)(2,1)S(1)} %collective-permute-done.r1) | copy-start | bytes 663556
  36.6 2.5 %copy-start.6 = (bf16[96,1152]{1,0:T(8,128)(2,1)}, bf16[96,1152]{1,0:T(8,128)(2,1)S(1)}, u32[]{:S(2)}) copy-start(bf16[96,1152]{1,0:T(8,128)(2,1)S(1)} %collective-permute-done.6.l4) | copy-start | bytes 663556
  37.9 1.2 %copy-start.7 = (bf16[96,1152]{1,0:T(8,128)(2,1)}, bf16[96,1152]{1,0:T(8,128)(2,1)S(1)}, u32[]{:S(2)}) copy-start(bf16[96,1152]{1,0:T(8,128)(2,1)S(1)} %collective-permute-done.5.l3) | copy-start | bytes 663556
  39.1 0.7 copy-start.8
  46.7 18.7 %collective-permute-start.7 = (bf16[192,1024]{1,0:T(8,128)(2,1)}, bf16[192,1024]{1,0:T(8,128)(2,1)S(1)}, u32[]{:S(2)}, u32[]{:S(2)}) collective-permute-start(bf16[192,1024]{1,0:T(8,128)(2,1)} %get-tuple-element.44), channel_id=1, source_target_pairs={{0,1},{1,2},{2,3},{3,4},{4,5},{5,6},{6,7},{7,0},{8,15},{9,8},{10,9... | collective-permute-start | bytes 1179656 | tf_op jit(solution)/shard_map/ppermute | solution.py:252
  50.7 14.7 %collective-permute-start.8 = (bf16[192,1024]{1,0:T(8,128)(2,1)}, bf16[192,1024]{1,0:T(8,128)(2,1)S(1)}, u32[]{:S(2)}, u32[]{:S(2)}) collective-permute-start(bf16[192,1024]{1,0:T(8,128)(2,1)} %get-tuple-element.45), channel_id=1, source_target_pairs={{0,7},{1,0},{2,1},{3,2},{4,3},{5,4},{6,5},{7,6},{8,9},{9,10},{10,1... | collective-permute-start | bytes 1179656 | tf_op jit(solution)/shard_map/ppermute | solution.py:252
  52.7 12.8 %collective-permute-start.9 = (bf16[96,1024]{1,0:T(8,128)(2,1)}, bf16[96,1024]{1,0:T(8,128)(2,1)S(1)}, u32[]{:S(2)}, u32[]{:S(2)}) collective-permute-start(bf16[96,1024]{1,0:T(8,128)(2,1)} %get-tuple-element.46), channel_id=1, source_target_pairs={{0,2},{1,3},{2,4},{3,5},{4,6},{5,7},{6,0},{7,1},{8,14},{9,15},{10,... | collective-permute-start | bytes 589832 | tf_op jit(solution)/shard_map/ppermute | solution.py:252
  55.8 19.1 %all-to-all-start = ((f32[32,1,1024]{2,1,0:T(1,128)}), f32[32,1,1024]{2,1,0:T(1,128)S(1)}, u32[]{:S(2)}, u32[]{:S(2)}) async-start(f32[32,1,1024]{2,1,0:T(1,128)} %get-tuple-element.33), calls=%async_computation | async-start | bytes 262144 | tf_op jit(solution)/shard_map/all_to_all | solution.py:311
  66.5 24.0 %collective-permute-start.11 = (bf16[96,1024]{1,0:T(8,128)(2,1)S(1)}, bf16[96,1024]{1,0:T(8,128)(2,1)S(1)}, u32[]{:S(2)}, u32[]{:S(2)}) collective-permute-start(bf16[96,1024]{1,0:T(8,128)(2,1)S(1)} %add_convert_fusion), channel_id=1, source_target_pairs={{0,6},{1,7},{2,0},{3,1},{4,2},{5,3},{6,4},{7,5},{8,10},{9,11},{10,... | collective-permute-start | bytes 589832 | tf_op jit(solution)/shard_map/ppermute | solution.py:252
  70.6 19.9 %collective-permute-start.10 = (bf16[96,1024]{1,0:T(8,128)(2,1)S(1)}, bf16[96,1024]{1,0:T(8,128)(2,1)S(1)}, u32[]{:S(2)}, u32[]{:S(2)}) collective-permute-start(bf16[96,1024]{1,0:T(8,128)(2,1)S(1)} %add_convert_fusion.1), channel_id=1, source_target_pairs={{0,2},{1,3},{2,4},{3,5},{4,6},{5,7},{6,0},{7,1},{8,14},{9,15},{10,... | collective-permute-start | bytes 589832 | tf_op jit(solution)/shard_map/ppermute | solution.py:252
  75.7 17.4 %all-to-all-start.1 = ((f32[16,1,1024]{2,1,0:T(1,128)}), f32[16,1,1024]{2,1,0:T(1,128)S(1)}, u32[]{:S(2)}, u32[]{:S(2)}) async-start(f32[16,1,1024]{2,1,0:T(1,128)} %broadcast_in_dim.27), calls=%async_computation.1 | async-start | bytes 131072 | tf_op jit(solution)/shard_map/all_to_all | solution.py:315
  85.9 4.7 %copy-start.1 = (bf16[96,1024]{1,0:T(8,128)(2,1)S(1)}, bf16[96,1024]{1,0:T(8,128)(2,1)}, u32[]{:S(2)}) copy-start(bf16[96,1024]{1,0:T(8,128)(2,1)} %get-tuple-element.43) | copy-start | bytes 589828

commit v6 on v5

--- a/solution.py
+++ b/solution.py
@@ -29,6 +29,22 @@
 
 def dot(a, b, dims=(((1,), (0,)), ((), ()))):
     return lax.dot_general(a, b, dims, preferred_element_type=F32)
+
+
+def prepare_kernel(ids_ref, rows_hbm, out_hbm, digits, went):
+    rows = pltpu.make_async_copy(rows_hbm, out_hbm.at[:, 0:WIDTH], went.at[0])
+    rows.start()
+    row = lax.broadcasted_iota(I32, (ROWS, ROWS), 0)
+    col = lax.broadcasted_iota(I32, (ROWS, ROWS), 1)
+    column = jnp.sum(jnp.where(row == col, ids_ref[...].astype(F32), F32(0.0)), axis=1, keepdims=True)
+    upper = jnp.floor(column * F32(1.0 / BASE))
+    lane = lax.broadcasted_iota(I32, (ROWS, EXTRA), 1)
+    both = jnp.where(lane == 0, upper, jnp.where(lane == 1, column - BASE * upper, F32(0.0)))
+    digits[...] = both.astype(BF16)
+    tail = pltpu.make_async_copy(digits, out_hbm.at[:, WIDTH : WIDTH + EXTRA], went.at[1])
+    tail.start()
+    rows.wait()
+    tail.wait()
 
 
 def forward_kernel(
@@ -180,8 +196,10 @@
         mean1 = jnp.mean(dnormed, axis=1, keepdims=True)
         mean2 = jnp.mean(product * gain, axis=1, keepdims=True)
         dmixed[at, :] = ((dnormed - mean1 - unit * mean2) * aux[at, 0:1]).astype(BF16)
-    store(dmixed, dmixed_hbm)
-    store(gate_grad, gate_grad_hbm)
+        if i % 4 == 3:
+            half = slice((i - 3) * step, (i + 1) * step)
+            store(dmixed.at[half], dmixed_hbm.at[half])
+            store(gate_grad.at[half], gate_grad_hbm.at[half])
     part = jnp.sum(sums, axis=0, keepdims=True)
     for i in range(XY):
         part_ref[i] = part
@@ -261,10 +279,14 @@
 
 
 def body(query_act, key_act, value_act, gate_act, lengths, targets, pool_rows, pool_ids, norm_gain):
-    lane = lax.broadcasted_iota(I32, (ROWS, EXTRA), 1)
-    column = pool_ids[:, None]
-    digits = jnp.where(lane == 0, column // BASE, jnp.where(lane == 1, column % BASE, 0))
-    mine = jnp.concatenate([pool_rows, digits.astype(BF16)], axis=1)
+    (mine,) = call(
+        prepare_kernel,
+        [VMEM, ANY],
+        [((ROWS, WIDTH + EXTRA), BF16, ANY)],
+        [((ROWS, EXTRA), BF16)],
+        (2,),
+        10**6,
+    )(pool_ids.reshape(1, ROWS), pool_rows)
     r2 = shift(mine, 2)
     l2 = shift(mine, -2)
     r1 = shift(mine, 1)
@@ -294,7 +316,7 @@
         [(TOKEN, BF16), ((POOL, WIDTH + EXTRA), BF16), (LANES, F32), (TOKEN, F32), (TOKEN, BF16)]
         + [((COUNT, POOL), F32), ((COUNT, POOL), BF16), (TABLE, BF16), (TOKEN, F32)]
         + [(TOKEN, BF16)] * 2,
-        (12, 10),
+        (12, 12),
         2 * 10**9,
     )(place, line, emb, normed, aux, gate_act, gain, mine, r1, r2, r3, l1, l2, l3, l4)
 

time: 94.4 us -> 101 us (1.070)
  Pallas kernels: 16.9 us -> 24.5 us
  other arithmetic: 5.32 us -> 3.61 us
    pallas_call x0 -> x1, Pallas kernels: none -> 7.73 us  [body(): call(prepare_kernel, [VMEM, ANY], [((ROWS, WIDTH + EXTRA), BF16, ANY)], [...]
  transfers between devices with their start and end apart: 14 -> 14, of which waited for: 4 -> 4; matrix products, arithmetic and copies ran while one was open for 4% -> 4% of each run, Pallas kernels for 11% -> 10%
where the time goes in v6:
time: 101 us; the launch traced here: 99.8 us
  starting transfers between devices  65 us (64%)
  Pallas kernels  24.5 us (24%)
  waiting for transfers between devices  4.41 us (4%)
  other arithmetic  3.61 us (4%)
  local copies, waits for them, and re-layouts  1.34 us (1%)
    ppermute x12, starting transfers between devices, shift(): return lax.ppermute(value, ('dp', 'pool'), pairs)  45.1 us
    all_to_all x1, starting transfers between devices, body(): lax.all_to_all(spread, ('dp', 'pool'), 0, 0, axis_index_groups=near, tile...  10.2 us
    all_to_all x1, starting transfers between devices, body(): lax.all_to_all(part, 'dp', 0, 0, axis_index_groups=plane, tiled=True)  9.69 us
    pallas_call x1, Pallas kernels, body(): call(prepare_kernel, [VMEM, ANY], [((ROWS, WIDTH + EXTRA), BF16, ANY)], [...  7.73 us
    pallas_call x1, Pallas kernels, body(): call(step_kernel, [SMEM, SMEM] + [ANY] * 4 + [VMEM] + [ANY] * 8, [(TOKEN,...  6.89 us
    pallas_call x1, Pallas kernels, body(): call(forward_kernel, [SMEM] + [ANY] * 4 + [VMEM] * 2, [(TOKEN, BF16, ANY)...  5.29 us
    pallas_call x1, Pallas kernels, body(): call(backward_kernel, [ANY] * 6, [(TOKEN, BF16, ANY)] * 3, [(TOKEN, BF16)...  4.62 us
    ppermute x12, waiting for transfers between devices, shift(): return lax.ppermute(value, ('dp', 'pool'), pairs)  2.8 us
  transfers between devices with their start and end apart: 14, of which 4 were waited for; matrix products, arithmetic and copies ran while one was open for 4% of the time, Pallas kernels for 10%

profile of v6, /device:TPU:1, one launch (start us, length us, event | category | flops | bytes accessed | tf_op | source)
XLA Modules:
  0.0 99.8 jit_solution(3212803652446043650)
XLA Ops:
  0.6 7.7 %shard_map.137.own = bf16[96,1152]{1,0:T(8,128)(2,1)} custom-call(s32[1,96]{1,0:T(1,128)} %bitcast.8, bf16[96,1024]{1,0:T(8,128)(2,1)} %rows_hbm.1), custom_call_target="tpu_custom_call" | custom-call | flops 1000000 | bytes 8000000 | tf_op jit(solution)/shard_map/pallas_call | solution.py:282
  8.4 6.6 %collective-permute-start.4 = (bf16[96,1152]{1,0:T(8,128)(2,1)}, bf16[96,1152]{1,0:T(8,128)(2,1)S(1)}, u32[]{:S(2)}, u32[]{:S(2)}) collective-permute-start(bf16[96,1152]{1,0:T(8,128)(2,1)} %shard_map.137.own), channel_id=1, source_target_pairs={{0,6},{1,7},{2,0},{3,1},{4,2},{5,3},{6,4},{7,5},{8,10},{9,11},{10,... | collective-permute-start | bytes 663560 | tf_op jit(solution)/shard_map/ppermute | solution.py:270
  15.0 6.8 %collective-permute-start.1 = (bf16[96,1152]{1,0:T(8,128)(2,1)}, bf16[96,1152]{1,0:T(8,128)(2,1)S(1)}, u32[]{:S(2)}, u32[]{:S(2)}) collective-permute-start(bf16[96,1152]{1,0:T(8,128)(2,1)} %shard_map.137.own), channel_id=1, source_target_pairs={{0,2},{1,3},{2,4},{3,5},{4,6},{5,7},{6,0},{7,1},{8,14},{9,15},{10,... | collective-permute-start | bytes 663560 | tf_op jit(solution)/shard_map/ppermute | solution.py:270
  21.8 3.1 %collective-permute-start.3 = (bf16[96,1152]{1,0:T(8,128)(2,1)}, bf16[96,1152]{1,0:T(8,128)(2,1)S(1)}, u32[]{:S(2)}, u32[]{:S(2)}) collective-permute-start(bf16[96,1152]{1,0:T(8,128)(2,1)} %shard_map.137.own), channel_id=1, source_target_pairs={{0,7},{1,0},{2,1},{3,2},{4,3},{5,4},{6,5},{7,6},{8,9},{9,10},{10,1... | collective-permute-start | bytes 663560 | tf_op jit(solution)/shard_map/ppermute | solution.py:270
  24.9 3.4 %collective-permute-start = (bf16[96,1152]{1,0:T(8,128)(2,1)}, bf16[96,1152]{1,0:T(8,128)(2,1)S(1)}, u32[]{:S(2)}, u32[]{:S(2)}) collective-permute-start(bf16[96,1152]{1,0:T(8,128)(2,1)} %shard_map.137.own), channel_id=1, source_target_pairs={{0,1},{1,2},{2,3},{3,4},{4,5},{5,6},{6,7},{7,0},{8,15},{9,8},{10,9... | collective-permute-start | bytes 663560 | tf_op jit(solution)/shard_map/ppermute | solution.py:270
  28.3 1.9 %collective-permute-start.6 = (bf16[96,1152]{1,0:T(8,128)(2,1)S(1)}, bf16[96,1152]{1,0:T(8,128)(2,1)S(1)}, u32[]{:S(2)}, u32[]{:S(2)}) collective-permute-start(bf16[96,1152]{1,0:T(8,128)(2,1)S(1)} %collective-permute-done.4.l2), channel_id=1, source_target_pairs={{0,6},{1,7},{2,0},{3,1},{4,2},{5,3},{6,4},{7,5},{8,10},{9,11},{10,... | collective-permute-start | bytes 663560 | tf_op jit(solution)/shard_map/ppermute | solution.py:270
  30.2 3.3 %collective-permute-start.5 = (bf16[96,1152]{1,0:T(8,128)(2,1)S(1)}, bf16[96,1152]{1,0:T(8,128)(2,1)S(1)}, u32[]{:S(2)}, u32[]{:S(2)}) collective-permute-start(bf16[96,1152]{1,0:T(8,128)(2,1)S(1)} %collective-permute-done.4.l2), channel_id=1, source_target_pairs={{0,7},{1,0},{2,1},{3,2},{4,3},{5,4},{6,5},{7,6},{8,9},{9,10},{10,1... | collective-permute-start | bytes 663560 | tf_op jit(solution)/shard_map/ppermute | solution.py:270
  33.6 3.3 %collective-permute-start.2 = (bf16[96,1152]{1,0:T(8,128)(2,1)S(1)}, bf16[96,1152]{1,0:T(8,128)(2,1)S(1)}, u32[]{:S(2)}, u32[]{:S(2)}) collective-permute-start(bf16[96,1152]{1,0:T(8,128)(2,1)S(1)} %collective-permute-done.1.r2), channel_id=1, source_target_pairs={{0,1},{1,2},{2,3},{3,4},{4,5},{5,6},{6,7},{7,0},{8,15},{9,8},{10,9... | collective-permute-start | bytes 663560 | tf_op jit(solution)/shard_map/ppermute | solution.py:270
  37.0 5.3 %shard_map.136 = (bf16[256,1024]{1,0:T(8,128)(2,1)}, f32[256,1024]{1,0:T(8,128)}, f32[256,128]{1,0:T(8,128)}, bf16[8,256,256]{2,1,0:T(8,128)(2,1)}, f32[8,256,256]{2,1,0:T(8,128)}) custom-call(s32[1,4]{1,0:T(1,128)} %lengths.1, bf16[256,1024]{1,0:T(8,128)(2,1)} %q_hbm.3, bf16[256,1024]{1,0:T(8,128)(2,1)} %k_hbm.3, bf16[256,1024]{1,0:T(8,128)(2,1)} %v_hbm.3, ...), custom_call_target="tpu_custom_call" | custom-call | flops 1000000000 | bytes 8000000 | tf_op jit(solution)/shard_map/pallas_call | solution.py:301
  42.8 1.3 %collective-permute-done.5.l3 = bf16[96,1152]{1,0:T(8,128)(2,1)S(1)} collective-permute-done((bf16[96,1152]{1,0:T(8,128)(2,1)S(1)}, bf16[96,1152]{1,0:T(8,128)(2,1)S(1)}, u32[]{:S(2)}, u32[]{:S(2)}) %collective-permute-start.5) | collective-permute-done | bytes 221216 | tf_op jit(solution)/shard_map/ppermute | solution.py:270
  44.1 1.0 collective-permute-done.2.r3
  45.8 6.9 %shard_map.138 = (bf16[256,1024]{1,0:T(8,128)(2,1)}, bf16[256,1024]{1,0:T(8,128)(2,1)}, f32[32,1,1024]{2,1,0:T(1,128)}, bf16[192,1024]{1,0:T(8,128)(2,1)}, bf16[...) custom-call(s32[1]{0:T(128)} %bitcast.place, ...), custom_call_target="tpu_custom_call" | custom-call | flops 2000000000 | bytes 8000000 | tf_op jit(solution)/shard_map/pallas_call | solution.py:310
  52.7 4.2 %collective-permute-start.7 = (bf16[192,1024]{1,0:T(8,128)(2,1)}, bf16[192,1024]{1,0:T(8,128)(2,1)S(1)}, u32[]{:S(2)}, u32[]{:S(2)}) collective-permute-start(bf16[192,1024]{1,0:T(8,128)(2,1)} %get-tuple-element.44), channel_id=1, source_target_pairs={{0,1},{1,2},{2,3},{3,4},{4,5},{5,6},{6,7},{7,0},{8,15},{9,8},{10,9... | collective-permute-start | bytes 1179656 | tf_op jit(solution)/shard_map/ppermute | solution.py:270
  56.9 1.9 %collective-permute-start.8 = (bf16[192,1024]{1,0:T(8,128)(2,1)}, bf16[192,1024]{1,0:T(8,128)(2,1)S(1)}, u32[]{:S(2)}, u32[]{:S(2)}) collective-permute-start(bf16[192,1024]{1,0:T(8,128)(2,1)} %get-tuple-element.45), channel_id=1, source_target_pairs={{0,7},{1,0},{2,1},{3,2},{4,3},{5,4},{6,5},{7,6},{8,9},{9,10},{10,1... | collective-permute-start | bytes 1179656 | tf_op jit(solution)/shard_map/ppermute | solution.py:270
  58.8 3.1 %collective-permute-start.9 = (bf16[96,1024]{1,0:T(8,128)(2,1)}, bf16[96,1024]{1,0:T(8,128)(2,1)S(1)}, u32[]{:S(2)}, u32[]{:S(2)}) collective-permute-start(bf16[96,1024]{1,0:T(8,128)(2,1)} %get-tuple-element.46), channel_id=1, source_target_pairs={{0,2},{1,3},{2,4},{3,5},{4,6},{5,7},{6,0},{7,1},{8,14},{9,15},{10,... | collective-permute-start | bytes 589832 | tf_op jit(solution)/shard_map/ppermute | solution.py:270
  61.9 9.7 %all-to-all-start = ((f32[32,1,1024]{2,1,0:T(1,128)}), f32[32,1,1024]{2,1,0:T(1,128)S(1)}, u32[]{:S(2)}, u32[]{:S(2)}) async-start(f32[32,1,1024]{2,1,0:T(1,128)} %get-tuple-element.33), calls=%async_computation | async-start | bytes 262144 | tf_op jit(solution)/shard_map/all_to_all | solution.py:333
  71.6 1.0 add_convert_fusion
  72.6 3.1 %collective-permute-start.11 = (bf16[96,1024]{1,0:T(8,128)(2,1)S(1)}, bf16[96,1024]{1,0:T(8,128)(2,1)S(1)}, u32[]{:S(2)}, u32[]{:S(2)}) collective-permute-start(bf16[96,1024]{1,0:T(8,128)(2,1)S(1)} %add_convert_fusion), channel_id=1, source_target_pairs={{0,6},{1,7},{2,0},{3,1},{4,2},{5,3},{6,4},{7,5},{8,10},{9,11},{10,... | collective-permute-start | bytes 589832 | tf_op jit(solution)/shard_map/ppermute | solution.py:270
  75.7 1.0 %add_convert_fusion.1 = bf16[96,1024]{1,0:T(8,128)(2,1)S(1)} fusion(bf16[96,1024]{1,0:T(8,128)(2,1)S(1)} %collective-permute-done.9, bf16[96,1024]{1,0:T(8,128)(2,1)} %get-tuple-element.49, bf16[192,1024]{1,0:T(8,128)(2,1)S(1)} %collective-permute-done.7), kind=kLoop, calls=%fused_computation.2 | loop fusion | flops 589824 | bytes 786432 | tf_op jit(solution)/shard_map/convert_element_type | solution.py:327
  76.7 4.3 %collective-permute-start.10 = (bf16[96,1024]{1,0:T(8,128)(2,1)S(1)}, bf16[96,1024]{1,0:T(8,128)(2,1)S(1)}, u32[]{:S(2)}, u32[]{:S(2)}) collective-permute-start(bf16[96,1024]{1,0:T(8,128)(2,1)S(1)} %add_convert_fusion.1), channel_id=1, source_target_pairs={{0,2},{1,3},{2,4},{3,5},{4,6},{5,7},{6,0},{7,1},{8,14},{9,15},{10,... | collective-permute-start | bytes 589832 | tf_op jit(solution)/shard_map/ppermute | solution.py:270
  81.8 10.2 %all-to-all-start.1 = ((f32[16,1,1024]{2,1,0:T(1,128)}), f32[16,1,1024]{2,1,0:T(1,128)S(1)}, u32[]{:S(2)}, u32[]{:S(2)}) async-start(f32[16,1,1024]{2,1,0:T(1,128)} %broadcast_in_dim.2), calls=%async_computation.1 | async-start | bytes 131072 | tf_op jit(solution)/shard_map/all_to_all | solution.py:337
  92.0 4.6 %shard_map.139 = (bf16[256,1024]{1,0:T(8,128)(2,1)}, bf16[256,1024]{1,0:T(8,128)(2,1)}, bf16[256,1024]{1,0:T(8,128)(2,1)}) custom-call(bf16[256,1024]{1,0:T(8,128)(2,1)} %get-tuple-element.35.dmixed_hbm, bf16[256,1024]{1,0:T(8,128)(2,1)} %q_hbm.3, bf16[256,1024]{1,0:T(8,128)(2,1)} %k_hbm.3, bf16[256,1024]{1,0:T(8,128)(2,1)} %v_hbm.3, ...), custom_call_target="tpu_custom_call" | custom-call | flops 2000000000 | bytes 8000000 | tf_op jit(solution)/shard_map/pallas_call | solution.py:344
  96.6 0.9 convert_add_fusion
  97.5 1.6 %all-to-all-done.1 = f32[16,1,1024]{2,1,0:T(1,128)S(1)} async-done(((f32[16,1,1024]{2,1,0:T(1,128)}), f32[16,1,1024]{2,1,0:T(1,128)S(1)}, u32[]{:S(2)}, u32[]{:S(2)}) %all-to-all-start.1) | async-done | bytes 65568 | tf_op jit(solution)/shard_map/all_to_all | solution.py:337
  (30 shorter events, 2.6 us)
Async XLA Ops:
  8.4 19.9 %collective-permute-start.4 = (bf16[96,1152]{1,0:T(8,128)(2,1)}, bf16[96,1152]{1,0:T(8,128)(2,1)S(1)}, u32[]{:S(2)}, u32[]{:S(2)}) collective-permute-start(bf16[96,1152]{1,0:T(8,128)(2,1)} %shard_map.137.own), channel_id=1, source_target_pairs={{0,6},{1,7},{2,0},{3,1},{4,2},{5,3},{6,4},{7,5},{8,10},{9,11},{10,... | collective-permute-start | bytes 663560 | tf_op jit(solution)/shard_map/ppermute | solution.py:270
  15.0 18.6 %collective-permute-start.1 = (bf16[96,1152]{1,0:T(8,128)(2,1)}, bf16[96,1152]{1,0:T(8,128)(2,1)S(1)}, u32[]{:S(2)}, u32[]{:S(2)}) collective-permute-start(bf16[96,1152]{1,0:T(8,128)(2,1)} %shard_map.137.own), channel_id=1, source_target_pairs={{0,2},{1,3},{2,4},{3,5},{4,6},{5,7},{6,0},{7,1},{8,14},{9,15},{10,... | collective-permute-start | bytes 663560 | tf_op jit(solution)/shard_map/ppermute | solution.py:270
  21.8 20.5 %collective-permute-start.3 = (bf16[96,1152]{1,0:T(8,128)(2,1)}, bf16[96,1152]{1,0:T(8,128)(2,1)S(1)}, u32[]{:S(2)}, u32[]{:S(2)}) collective-permute-start(bf16[96,1152]{1,0:T(8,128)(2,1)} %shard_map.137.own), channel_id=1, source_target_pairs={{0,7},{1,0},{2,1},{3,2},{4,3},{5,4},{6,5},{7,6},{8,9},{9,10},{10,1... | collective-permute-start | bytes 663560 | tf_op jit(solution)/shard_map/ppermute | solution.py:270
  24.9 17.4 %collective-permute-start = (bf16[96,1152]{1,0:T(8,128)(2,1)}, bf16[96,1152]{1,0:T(8,128)(2,1)S(1)}, u32[]{:S(2)}, u32[]{:S(2)}) collective-permute-start(bf16[96,1152]{1,0:T(8,128)(2,1)} %shard_map.137.own), channel_id=1, source_target_pairs={{0,1},{1,2},{2,3},{3,4},{4,5},{5,6},{6,7},{7,0},{8,15},{9,8},{10,9... | collective-permute-start | bytes 663560 | tf_op jit(solution)/shard_map/ppermute | solution.py:270
  28.3 16.8 %copy-start.1 = (bf16[96,1152]{1,0:T(8,128)(2,1)}, bf16[96,1152]{1,0:T(8,128)(2,1)S(1)}, u32[]{:S(2)}) copy-start(bf16[96,1152]{1,0:T(8,128)(2,1)S(1)} %collective-permute-done.4.l2) | copy-start | bytes 663556
  28.3 14.5 %collective-permute-start.6 = (bf16[96,1152]{1,0:T(8,128)(2,1)S(1)}, bf16[96,1152]{1,0:T(8,128)(2,1)S(1)}, u32[]{:S(2)}, u32[]{:S(2)}) collective-permute-start(bf16[96,1152]{1,0:T(8,128)(2,1)S(1)} %collective-permute-done.4.l2), channel_id=1, source_target_pairs={{0,6},{1,7},{2,0},{3,1},{4,2},{5,3},{6,4},{7,5},{8,10},{9,11},{10,... | collective-permute-start | bytes 663560 | tf_op jit(solution)/shard_map/ppermute | solution.py:270
  30.2 13.9 %collective-permute-start.5 = (bf16[96,1152]{1,0:T(8,128)(2,1)S(1)}, bf16[96,1152]{1,0:T(8,128)(2,1)S(1)}, u32[]{:S(2)}, u32[]{:S(2)}) collective-permute-start(bf16[96,1152]{1,0:T(8,128)(2,1)S(1)} %collective-permute-done.4.l2), channel_id=1, source_target_pairs={{0,7},{1,0},{2,1},{3,2},{4,3},{5,4},{6,5},{7,6},{8,9},{9,10},{10,1... | collective-permute-start | bytes 663560 | tf_op jit(solution)/shard_map/ppermute | solution.py:270
  33.6 11.5 %copy-start.2 = (bf16[96,1152]{1,0:T(8,128)(2,1)}, bf16[96,1152]{1,0:T(8,128)(2,1)S(1)}, u32[]{:S(2)}) copy-start(bf16[96,1152]{1,0:T(8,128)(2,1)S(1)} %collective-permute-done.1.r2) | copy-start | bytes 663556
  33.6 11.5 %collective-permute-start.2 = (bf16[96,1152]{1,0:T(8,128)(2,1)S(1)}, bf16[96,1152]{1,0:T(8,128)(2,1)S(1)}, u32[]{:S(2)}, u32[]{:S(2)}) collective-permute-start(bf16[96,1152]{1,0:T(8,128)(2,1)S(1)} %collective-permute-done.1.r2), channel_id=1, source_target_pairs={{0,1},{1,2},{2,3},{3,4},{4,5},{5,6},{6,7},{7,0},{8,15},{9,8},{10,9... | collective-permute-start | bytes 663560 | tf_op jit(solution)/shard_map/ppermute | solution.py:270
  42.3 2.8 %copy-start.3 = (bf16[96,1152]{1,0:T(8,128)(2,1)}, bf16[96,1152]{1,0:T(8,128)(2,1)S(1)}, u32[]{:S(2)}) copy-start(bf16[96,1152]{1,0:T(8,128)(2,1)S(1)} %collective-permute-done.3.l1) | copy-start | bytes 663556
  42.3 2.8 %copy-start.4 = (bf16[96,1152]{1,0:T(8,128)(2,1)}, bf16[96,1152]{1,0:T(8,128)(2,1)S(1)}, u32[]{:S(2)}) copy-start(bf16[96,1152]{1,0:T(8,128)(2,1)S(1)} %collective-permute-done.r1) | copy-start | bytes 663556
  42.8 2.3 %copy-start.5 = (bf16[96,1152]{1,0:T(8,128)(2,1)}, bf16[96,1152]{1,0:T(8,128)(2,1)S(1)}, u32[]{:S(2)}) copy-start(bf16[96,1152]{1,0:T(8,128)(2,1)S(1)} %collective-permute-done.6.l4) | copy-start | bytes 663556
  44.1 1.0 %copy-start.6 = (bf16[96,1152]{1,0:T(8,128)(2,1)}, bf16[96,1152]{1,0:T(8,128)(2,1)S(1)}, u32[]{:S(2)}) copy-start(bf16[96,1152]{1,0:T(8,128)(2,1)S(1)} %collective-permute-done.5.l3) | copy-start | bytes 663556
  45.1 0.7 copy-start.7
  52.7 18.9 %collective-permute-start.7 = (bf16[192,1024]{1,0:T(8,128)(2,1)}, bf16[192,1024]{1,0:T(8,128)(2,1)S(1)}, u32[]{:S(2)}, u32[]{:S(2)}) collective-permute-start(bf16[192,1024]{1,0:T(8,128)(2,1)} %get-tuple-element.44), channel_id=1, source_target_pairs={{0,1},{1,2},{2,3},{3,4},{4,5},{5,6},{6,7},{7,0},{8,15},{9,8},{10,9... | collective-permute-start | bytes 1179656 | tf_op jit(solution)/shard_map/ppermute | solution.py:270
  56.9 14.7 %collective-permute-start.8 = (bf16[192,1024]{1,0:T(8,128)(2,1)}, bf16[192,1024]{1,0:T(8,128)(2,1)S(1)}, u32[]{:S(2)}, u32[]{:S(2)}) collective-permute-start(bf16[192,1024]{1,0:T(8,128)(2,1)} %get-tuple-element.45), channel_id=1, source_target_pairs={{0,7},{1,0},{2,1},{3,2},{4,3},{5,4},{6,5},{7,6},{8,9},{9,10},{10,1... | collective-permute-start | bytes 1179656 | tf_op jit(solution)/shard_map/ppermute | solution.py:270
  58.8 12.8 %collective-permute-start.9 = (bf16[96,1024]{1,0:T(8,128)(2,1)}, bf16[96,1024]{1,0:T(8,128)(2,1)S(1)}, u32[]{:S(2)}, u32[]{:S(2)}) collective-permute-start(bf16[96,1024]{1,0:T(8,128)(2,1)} %get-tuple-element.46), channel_id=1, source_target_pairs={{0,2},{1,3},{2,4},{3,5},{4,6},{5,7},{6,0},{7,1},{8,14},{9,15},{10,... | collective-permute-start | bytes 589832 | tf_op jit(solution)/shard_map/ppermute | solution.py:270
  61.9 19.1 %all-to-all-start = ((f32[32,1,1024]{2,1,0:T(1,128)}), f32[32,1,1024]{2,1,0:T(1,128)S(1)}, u32[]{:S(2)}, u32[]{:S(2)}) async-start(f32[32,1,1024]{2,1,0:T(1,128)} %get-tuple-element.33), calls=%async_computation | async-start | bytes 262144 | tf_op jit(solution)/shard_map/all_to_all | solution.py:333
  72.6 24.0 %collective-permute-start.11 = (bf16[96,1024]{1,0:T(8,128)(2,1)S(1)}, bf16[96,1024]{1,0:T(8,128)(2,1)S(1)}, u32[]{:S(2)}, u32[]{:S(2)}) collective-permute-start(bf16[96,1024]{1,0:T(8,128)(2,1)S(1)} %add_convert_fusion), channel_id=1, source_target_pairs={{0,6},{1,7},{2,0},{3,1},{4,2},{5,3},{6,4},{7,5},{8,10},{9,11},{10,... | collective-permute-start | bytes 589832 | tf_op jit(solution)/shard_map/ppermute | solution.py:270
  76.7 19.9 %collective-permute-start.10 = (bf16[96,1024]{1,0:T(8,128)(2,1)S(1)}, bf16[96,1024]{1,0:T(8,128)(2,1)S(1)}, u32[]{:S(2)}, u32[]{:S(2)}) collective-permute-start(bf16[96,1024]{1,0:T(8,128)(2,1)S(1)} %add_convert_fusion.1), channel_id=1, source_target_pairs={{0,2},{1,3},{2,4},{3,5},{4,6},{5,7},{6,0},{7,1},{8,14},{9,15},{10,... | collective-permute-start | bytes 589832 | tf_op jit(solution)/shard_map/ppermute | solution.py:270
  81.8 17.4 %all-to-all-start.1 = ((f32[16,1,1024]{2,1,0:T(1,128)}), f32[16,1,1024]{2,1,0:T(1,128)S(1)}, u32[]{:S(2)}, u32[]{:S(2)}) async-start(f32[16,1,1024]{2,1,0:T(1,128)} %broadcast_in_dim.2), calls=%async_computation.1 | async-start | bytes 131072 | tf_op jit(solution)/shard_map/all_to_all | solution.py:337
  92.0 4.7 %copy-start = (bf16[96,1024]{1,0:T(8,128)(2,1)S(1)}, bf16[96,1024]{1,0:T(8,128)(2,1)}, u32[]{:S(2)}) copy-start(bf16[96,1024]{1,0:T(8,128)(2,1)} %get-tuple-element.43) | copy-start | bytes 589828

commit v7 on v6

--- a/solution.py
+++ b/solution.py
@@ -31,20 +31,20 @@
     return lax.dot_general(a, b, dims, preferred_element_type=F32)
 
 
-def prepare_kernel(ids_ref, rows_hbm, out_hbm, digits, went):
-    rows = pltpu.make_async_copy(rows_hbm, out_hbm.at[:, 0:WIDTH], went.at[0])
-    rows.start()
+def prepare_kernel(ids_ref, rows_hbm, out_hbm, wide, went):
+    load = pltpu.make_async_copy(rows_hbm, wide.at[:, 0:WIDTH], went.at[0])
+    load.start()
     row = lax.broadcasted_iota(I32, (ROWS, ROWS), 0)
     col = lax.broadcasted_iota(I32, (ROWS, ROWS), 1)
     column = jnp.sum(jnp.where(row == col, ids_ref[...].astype(F32), F32(0.0)), axis=1, keepdims=True)
     upper = jnp.floor(column * F32(1.0 / BASE))
     lane = lax.broadcasted_iota(I32, (ROWS, EXTRA), 1)
     both = jnp.where(lane == 0, upper, jnp.where(lane == 1, column - BASE * upper, F32(0.0)))
-    digits[...] = both.astype(BF16)
-    tail = pltpu.make_async_copy(digits, out_hbm.at[:, WIDTH : WIDTH + EXTRA], went.at[1])
-    tail.start()
-    rows.wait()
-    tail.wait()
+    wide[:, WIDTH : WIDTH + EXTRA] = both.astype(BF16)
+    load.wait()
+    store = pltpu.make_async_copy(wide, out_hbm, went.at[1])
+    store.start()
+    store.wait()
 
 
 def forward_kernel(
@@ -283,7 +283,7 @@
         prepare_kernel,
         [VMEM, ANY],
         [((ROWS, WIDTH + EXTRA), BF16, ANY)],
-        [((ROWS, EXTRA), BF16)],
+        [((ROWS, WIDTH + EXTRA), BF16)],
         (2,),
         10**6,
     )(pool_ids.reshape(1, ROWS), pool_rows)

time: 101 us -> 95.1 us (0.942)
  Pallas kernels: 24.5 us -> 19.1 us
    pallas_call x1, Pallas kernels: 7.73 us -> 2.28 us  [body(): call(prepare_kernel, [VMEM, ANY], [((ROWS, WIDTH + EXTRA), BF16, ANY)], [...]
  transfers between devices with their start and end apart: 14 -> 14, of which waited for: 4 -> 4; matrix products, arithmetic and copies ran while one was open for 4% -> 4% of each run, Pallas kernels for 10% -> 11%
where the time goes in v7:
time: 95.1 us; the launch traced here: 94.3 us
  starting transfers between devices  65 us (68%)
  Pallas kernels  19.1 us (20%)
  waiting for transfers between devices  4.41 us (5%)
  other arithmetic  3.61 us (4%)
  local copies, waits for them, and re-layouts  1.34 us (1%)
    ppermute x12, starting transfers between devices, shift(): return lax.ppermute(value, ('dp', 'pool'), pairs)  45.1 us
    all_to_all x1, starting transfers between devices, body(): lax.all_to_all(spread, ('dp', 'pool'), 0, 0, axis_index_groups=near, tile...  10.2 us
    all_to_all x1, starting transfers between devices, body(): lax.all_to_all(part, 'dp', 0, 0, axis_index_groups=plane, tiled=True)  9.69 us
    pallas_call x1, Pallas kernels, body(): call(step_kernel, [SMEM, SMEM] + [ANY] * 4 + [VMEM] + [ANY] * 8, [(TOKEN,...  6.89 us
    pallas_call x1, Pallas kernels, body(): call(forward_kernel, [SMEM] + [ANY] * 4 + [VMEM] * 2, [(TOKEN, BF16, ANY)...  5.29 us
    pallas_call x1, Pallas kernels, body(): call(backward_kernel, [ANY] * 6, [(TOKEN, BF16, ANY)] * 3, [(TOKEN, BF16)...  4.62 us
    ppermute x12, waiting for transfers between devices, shift(): return lax.ppermute(value, ('dp', 'pool'), pairs)  2.8 us
    pallas_call x1, Pallas kernels, body(): call(prepare_kernel, [VMEM, ANY], [((ROWS, WIDTH + EXTRA), BF16, ANY)], [...  2.28 us
  transfers between devices with their start and end apart: 14, of which 4 were waited for; matrix products, arithmetic and copies ran while one was open for 4% of the time, Pallas kernels for 11%

profile of v7, /device:TPU:1, one launch (start us, length us, event | category | flops | bytes accessed | tf_op | source)
XLA Modules:
  0.0 94.3 jit_solution(17020338969364677566)
XLA Ops:
  0.6 2.3 %shard_map.137.own = bf16[96,1152]{1,0:T(8,128)(2,1)} custom-call(s32[1,96]{1,0:T(1,128)} %bitcast.8, bf16[96,1024]{1,0:T(8,128)(2,1)} %rows_hbm.1), custom_call_target="tpu_custom_call" | custom-call | flops 1000000 | bytes 8000000 | tf_op jit(solution)/shard_map/pallas_call | solution.py:282
  2.9 6.6 %collective-permute-start.4 = (bf16[96,1152]{1,0:T(8,128)(2,1)}, bf16[96,1152]{1,0:T(8,128)(2,1)S(1)}, u32[]{:S(2)}, u32[]{:S(2)}) collective-permute-start(bf16[96,1152]{1,0:T(8,128)(2,1)} %shard_map.137.own), channel_id=1, source_target_pairs={{0,6},{1,7},{2,0},{3,1},{4,2},{5,3},{6,4},{7,5},{8,10},{9,11},{10,... | collective-permute-start | bytes 663560 | tf_op jit(solution)/shard_map/ppermute | solution.py:270
  9.6 6.8 %collective-permute-start.1 = (bf16[96,1152]{1,0:T(8,128)(2,1)}, bf16[96,1152]{1,0:T(8,128)(2,1)S(1)}, u32[]{:S(2)}, u32[]{:S(2)}) collective-permute-start(bf16[96,1152]{1,0:T(8,128)(2,1)} %shard_map.137.own), channel_id=1, source_target_pairs={{0,2},{1,3},{2,4},{3,5},{4,6},{5,7},{6,0},{7,1},{8,14},{9,15},{10,... | collective-permute-start | bytes 663560 | tf_op jit(solution)/shard_map/ppermute | solution.py:270
  16.3 3.1 %collective-permute-start.3 = (bf16[96,1152]{1,0:T(8,128)(2,1)}, bf16[96,1152]{1,0:T(8,128)(2,1)S(1)}, u32[]{:S(2)}, u32[]{:S(2)}) collective-permute-start(bf16[96,1152]{1,0:T(8,128)(2,1)} %shard_map.137.own), channel_id=1, source_target_pairs={{0,7},{1,0},{2,1},{3,2},{4,3},{5,4},{6,5},{7,6},{8,9},{9,10},{10,1... | collective-permute-start | bytes 663560 | tf_op jit(solution)/shard_map/ppermute | solution.py:270
  19.5 3.4 %collective-permute-start = (bf16[96,1152]{1,0:T(8,128)(2,1)}, bf16[96,1152]{1,0:T(8,128)(2,1)S(1)}, u32[]{:S(2)}, u32[]{:S(2)}) collective-permute-start(bf16[96,1152]{1,0:T(8,128)(2,1)} %shard_map.137.own), channel_id=1, source_target_pairs={{0,1},{1,2},{2,3},{3,4},{4,5},{5,6},{6,7},{7,0},{8,15},{9,8},{10,9... | collective-permute-start | bytes 663560 | tf_op jit(solution)/shard_map/ppermute | solution.py:270
  22.9 1.9 %collective-permute-start.6 = (bf16[96,1152]{1,0:T(8,128)(2,1)S(1)}, bf16[96,1152]{1,0:T(8,128)(2,1)S(1)}, u32[]{:S(2)}, u32[]{:S(2)}) collective-permute-start(bf16[96,1152]{1,0:T(8,128)(2,1)S(1)} %collective-permute-done.4.l2), channel_id=1, source_target_pairs={{0,6},{1,7},{2,0},{3,1},{4,2},{5,3},{6,4},{7,5},{8,10},{9,11},{10,... | collective-permute-start | bytes 663560 | tf_op jit(solution)/shard_map/ppermute | solution.py:270
  24.8 3.3 %collective-permute-start.5 = (bf16[96,1152]{1,0:T(8,128)(2,1)S(1)}, bf16[96,1152]{1,0:T(8,128)(2,1)S(1)}, u32[]{:S(2)}, u32[]{:S(2)}) collective-permute-start(bf16[96,1152]{1,0:T(8,128)(2,1)S(1)} %collective-permute-done.4.l2), channel_id=1, source_target_pairs={{0,7},{1,0},{2,1},{3,2},{4,3},{5,4},{6,5},{7,6},{8,9},{9,10},{10,1... | collective-permute-start | bytes 663560 | tf_op jit(solution)/shard_map/ppermute | solution.py:270
  28.2 3.3 %collective-permute-start.2 = (bf16[96,1152]{1,0:T(8,128)(2,1)S(1)}, bf16[96,1152]{1,0:T(8,128)(2,1)S(1)}, u32[]{:S(2)}, u32[]{:S(2)}) collective-permute-start(bf16[96,1152]{1,0:T(8,128)(2,1)S(1)} %collective-permute-done.1.r2), channel_id=1, source_target_pairs={{0,1},{1,2},{2,3},{3,4},{4,5},{5,6},{6,7},{7,0},{8,15},{9,8},{10,9... | collective-permute-start | bytes 663560 | tf_op jit(solution)/shard_map/ppermute | solution.py:270
  31.5 5.3 %shard_map.136 = (bf16[256,1024]{1,0:T(8,128)(2,1)}, f32[256,1024]{1,0:T(8,128)}, f32[256,128]{1,0:T(8,128)}, bf16[8,256,256]{2,1,0:T(8,128)(2,1)}, f32[8,256,256]{2,1,0:T(8,128)}) custom-call(s32[1,4]{1,0:T(1,128)} %lengths.1, bf16[256,1024]{1,0:T(8,128)(2,1)} %q_hbm.3, bf16[256,1024]{1,0:T(8,128)(2,1)} %k_hbm.3, bf16[256,1024]{1,0:T(8,128)(2,1)} %v_hbm.3, ...), custom_call_target="tpu_custom_call" | custom-call | flops 1000000000 | bytes 8000000 | tf_op jit(solution)/shard_map/pallas_call | solution.py:301
  37.4 1.3 %collective-permute-done.5.l3 = bf16[96,1152]{1,0:T(8,128)(2,1)S(1)} collective-permute-done((bf16[96,1152]{1,0:T(8,128)(2,1)S(1)}, bf16[96,1152]{1,0:T(8,128)(2,1)S(1)}, u32[]{:S(2)}, u32[]{:S(2)}) %collective-permute-start.5) | collective-permute-done | bytes 221216 | tf_op jit(solution)/shard_map/ppermute | solution.py:270
  38.7 1.0 %collective-permute-done.2.r3 = bf16[96,1152]{1,0:T(8,128)(2,1)S(1)} collective-permute-done((bf16[96,1152]{1,0:T(8,128)(2,1)S(1)}, bf16[96,1152]{1,0:T(8,128)(2,1)S(1)}, u32[]{:S(2)}, u32[]{:S(2)}) %collective-permute-start.2) | collective-permute-done | bytes 221216 | tf_op jit(solution)/shard_map/ppermute | solution.py:270
  40.3 6.9 %shard_map.138 = (bf16[256,1024]{1,0:T(8,128)(2,1)}, bf16[256,1024]{1,0:T(8,128)(2,1)}, f32[32,1,1024]{2,1,0:T(1,128)}, bf16[192,1024]{1,0:T(8,128)(2,1)}, bf16[...) custom-call(s32[1]{0:T(128)} %bitcast.place, ...), custom_call_target="tpu_custom_call" | custom-call | flops 2000000000 | bytes 8000000 | tf_op jit(solution)/shard_map/pallas_call | solution.py:310
  47.2 4.2 %collective-permute-start.7 = (bf16[192,1024]{1,0:T(8,128)(2,1)}, bf16[192,1024]{1,0:T(8,128)(2,1)S(1)}, u32[]{:S(2)}, u32[]{:S(2)}) collective-permute-start(bf16[192,1024]{1,0:T(8,128)(2,1)} %get-tuple-element.44), channel_id=1, source_target_pairs={{0,1},{1,2},{2,3},{3,4},{4,5},{5,6},{6,7},{7,0},{8,15},{9,8},{10,9... | collective-permute-start | bytes 1179656 | tf_op jit(solution)/shard_map/ppermute | solution.py:270
  51.4 1.9 %collective-permute-start.8 = (bf16[192,1024]{1,0:T(8,128)(2,1)}, bf16[192,1024]{1,0:T(8,128)(2,1)S(1)}, u32[]{:S(2)}, u32[]{:S(2)}) collective-permute-start(bf16[192,1024]{1,0:T(8,128)(2,1)} %get-tuple-element.45), channel_id=1, source_target_pairs={{0,7},{1,0},{2,1},{3,2},{4,3},{5,4},{6,5},{7,6},{8,9},{9,10},{10,1... | collective-permute-start | bytes 1179656 | tf_op jit(solution)/shard_map/ppermute | solution.py:270
  53.3 3.1 %collective-permute-start.9 = (bf16[96,1024]{1,0:T(8,128)(2,1)}, bf16[96,1024]{1,0:T(8,128)(2,1)S(1)}, u32[]{:S(2)}, u32[]{:S(2)}) collective-permute-start(bf16[96,1024]{1,0:T(8,128)(2,1)} %get-tuple-element.46), channel_id=1, source_target_pairs={{0,2},{1,3},{2,4},{3,5},{4,6},{5,7},{6,0},{7,1},{8,14},{9,15},{10,... | collective-permute-start | bytes 589832 | tf_op jit(solution)/shard_map/ppermute | solution.py:270
  56.4 9.7 %all-to-all-start = ((f32[32,1,1024]{2,1,0:T(1,128)}), f32[32,1,1024]{2,1,0:T(1,128)S(1)}, u32[]{:S(2)}, u32[]{:S(2)}) async-start(f32[32,1,1024]{2,1,0:T(1,128)} %get-tuple-element.33), calls=%async_computation | async-start | bytes 262144 | tf_op jit(solution)/shard_map/all_to_all | solution.py:333
  66.2 1.0 %add_convert_fusion = bf16[96,1024]{1,0:T(8,128)(2,1)S(1)} fusion(bf16[96,1024]{1,0:T(8,128)(2,1)} %get-tuple-element.51, bf16[192,1024]{1,0:T(8,128)(2,1)S(1)} %collective-permute-done.8), kind=kLoop, calls=%fused_computation.1 | loop fusion | flops 393216 | bytes 589824 | tf_op jit(solution)/shard_map/convert_element_type | solution.py:328
  67.1 3.1 %collective-permute-start.11 = (bf16[96,1024]{1,0:T(8,128)(2,1)S(1)}, bf16[96,1024]{1,0:T(8,128)(2,1)S(1)}, u32[]{:S(2)}, u32[]{:S(2)}) collective-permute-start(bf16[96,1024]{1,0:T(8,128)(2,1)S(1)} %add_convert_fusion), channel_id=1, source_target_pairs={{0,6},{1,7},{2,0},{3,1},{4,2},{5,3},{6,4},{7,5},{8,10},{9,11},{10,... | collective-permute-start | bytes 589832 | tf_op jit(solution)/shard_map/ppermute | solution.py:270
  70.2 1.0 %add_convert_fusion.1 = bf16[96,1024]{1,0:T(8,128)(2,1)S(1)} fusion(bf16[96,1024]{1,0:T(8,128)(2,1)S(1)} %collective-permute-done.9, bf16[96,1024]{1,0:T(8,128)(2,1)} %get-tuple-element.49, bf16[192,1024]{1,0:T(8,128)(2,1)S(1)} %collective-permute-done.7), kind=kLoop, calls=%fused_computation.2 | loop fusion | flops 589824 | bytes 786432 | tf_op jit(solution)/shard_map/convert_element_type | solution.py:327
  71.3 4.3 %collective-permute-start.10 = (bf16[96,1024]{1,0:T(8,128)(2,1)S(1)}, bf16[96,1024]{1,0:T(8,128)(2,1)S(1)}, u32[]{:S(2)}, u32[]{:S(2)}) collective-permute-start(bf16[96,1024]{1,0:T(8,128)(2,1)S(1)} %add_convert_fusion.1), channel_id=1, source_target_pairs={{0,2},{1,3},{2,4},{3,5},{4,6},{5,7},{6,0},{7,1},{8,14},{9,15},{10,... | collective-permute-start | bytes 589832 | tf_op jit(solution)/shard_map/ppermute | solution.py:270
  76.3 10.2 %all-to-all-start.1 = ((f32[16,1,1024]{2,1,0:T(1,128)}), f32[16,1,1024]{2,1,0:T(1,128)S(1)}, u32[]{:S(2)}, u32[]{:S(2)}) async-start(f32[16,1,1024]{2,1,0:T(1,128)} %broadcast_in_dim.2), calls=%async_computation.1 | async-start | bytes 131072 | tf_op jit(solution)/shard_map/all_to_all | solution.py:337
  86.5 4.6 %shard_map.139 = (bf16[256,1024]{1,0:T(8,128)(2,1)}, bf16[256,1024]{1,0:T(8,128)(2,1)}, bf16[256,1024]{1,0:T(8,128)(2,1)}) custom-call(bf16[256,1024]{1,0:T(8,128)(2,1)} %get-tuple-element.35.dmixed_hbm, bf16[256,1024]{1,0:T(8,128)(2,1)} %q_hbm.3, bf16[256,1024]{1,0:T(8,128)(2,1)} %k_hbm.3, bf16[256,1024]{1,0:T(8,128)(2,1)} %v_hbm.3, ...), custom_call_target="tpu_custom_call" | custom-call | flops 2000000000 | bytes 8000000 | tf_op jit(solution)/shard_map/pallas_call | solution.py:344
  91.2 0.9 convert_add_fusion
  92.1 1.6 %all-to-all-done.1 = f32[16,1,1024]{2,1,0:T(1,128)S(1)} async-done(((f32[16,1,1024]{2,1,0:T(1,128)}), f32[16,1,1024]{2,1,0:T(1,128)S(1)}, u32[]{:S(2)}, u32[]{:S(2)}) %all-to-all-start.1) | async-done | bytes 65568 | tf_op jit(solution)/shard_map/all_to_all | solution.py:337
  (30 shorter events, 2.6 us)
Async XLA Ops:
  2.9 19.9 %collective-permute-start.4 = (bf16[96,1152]{1,0:T(8,128)(2,1)}, bf16[96,1152]{1,0:T(8,128)(2,1)S(1)}, u32[]{:S(2)}, u32[]{:S(2)}) collective-permute-start(bf16[96,1152]{1,0:T(8,128)(2,1)} %shard_map.137.own), channel_id=1, source_target_pairs={{0,6},{1,7},{2,0},{3,1},{4,2},{5,3},{6,4},{7,5},{8,10},{9,11},{10,... | collective-permute-start | bytes 663560 | tf_op jit(solution)/shard_map/ppermute | solution.py:270
  9.6 18.6 %collective-permute-start.1 = (bf16[96,1152]{1,0:T(8,128)(2,1)}, bf16[96,1152]{1,0:T(8,128)(2,1)S(1)}, u32[]{:S(2)}, u32[]{:S(2)}) collective-permute-start(bf16[96,1152]{1,0:T(8,128)(2,1)} %shard_map.137.own), channel_id=1, source_target_pairs={{0,2},{1,3},{2,4},{3,5},{4,6},{5,7},{6,0},{7,1},{8,14},{9,15},{10,... | collective-permute-start | bytes 663560 | tf_op jit(solution)/shard_map/ppermute | solution.py:270
  16.3 20.5 %collective-permute-start.3 = (bf16[96,1152]{1,0:T(8,128)(2,1)}, bf16[96,1152]{1,0:T(8,128)(2,1)S(1)}, u32[]{:S(2)}, u32[]{:S(2)}) collective-permute-start(bf16[96,1152]{1,0:T(8,128)(2,1)} %shard_map.137.own), channel_id=1, source_target_pairs={{0,7},{1,0},{2,1},{3,2},{4,3},{5,4},{6,5},{7,6},{8,9},{9,10},{10,1... | collective-permute-start | bytes 663560 | tf_op jit(solution)/shard_map/ppermute | solution.py:270
  19.5 17.4 %collective-permute-start = (bf16[96,1152]{1,0:T(8,128)(2,1)}, bf16[96,1152]{1,0:T(8,128)(2,1)S(1)}, u32[]{:S(2)}, u32[]{:S(2)}) collective-permute-start(bf16[96,1152]{1,0:T(8,128)(2,1)} %shard_map.137.own), channel_id=1, source_target_pairs={{0,1},{1,2},{2,3},{3,4},{4,5},{5,6},{6,7},{7,0},{8,15},{9,8},{10,9... | collective-permute-start | bytes 663560 | tf_op jit(solution)/shard_map/ppermute | solution.py:270
  22.9 16.8 %copy-start.1 = (bf16[96,1152]{1,0:T(8,128)(2,1)}, bf16[96,1152]{1,0:T(8,128)(2,1)S(1)}, u32[]{:S(2)}) copy-start(bf16[96,1152]{1,0:T(8,128)(2,1)S(1)} %collective-permute-done.4.l2) | copy-start | bytes 663556
  22.9 14.5 %collective-permute-start.6 = (bf16[96,1152]{1,0:T(8,128)(2,1)S(1)}, bf16[96,1152]{1,0:T(8,128)(2,1)S(1)}, u32[]{:S(2)}, u32[]{:S(2)}) collective-permute-start(bf16[96,1152]{1,0:T(8,128)(2,1)S(1)} %collective-permute-done.4.l2), channel_id=1, source_target_pairs={{0,6},{1,7},{2,0},{3,1},{4,2},{5,3},{6,4},{7,5},{8,10},{9,11},{10,... | collective-permute-start | bytes 663560 | tf_op jit(solution)/shard_map/ppermute | solution.py:270
  24.8 13.9 %collective-permute-start.5 = (bf16[96,1152]{1,0:T(8,128)(2,1)S(1)}, bf16[96,1152]{1,0:T(8,128)(2,1)S(1)}, u32[]{:S(2)}, u32[]{:S(2)}) collective-permute-start(bf16[96,1152]{1,0:T(8,128)(2,1)S(1)} %collective-permute-done.4.l2), channel_id=1, source_target_pairs={{0,7},{1,0},{2,1},{3,2},{4,3},{5,4},{6,5},{7,6},{8,9},{9,10},{10,1... | collective-permute-start | bytes 663560 | tf_op jit(solution)/shard_map/ppermute | solution.py:270
  28.2 11.5 %copy-start.2 = (bf16[96,1152]{1,0:T(8,128)(2,1)}, bf16[96,1152]{1,0:T(8,128)(2,1)S(1)}, u32[]{:S(2)}) copy-start(bf16[96,1152]{1,0:T(8,128)(2,1)S(1)} %collective-permute-done.1.r2) | copy-start | bytes 663556
  28.2 11.5 %collective-permute-start.2 = (bf16[96,1152]{1,0:T(8,128)(2,1)S(1)}, bf16[96,1152]{1,0:T(8,128)(2,1)S(1)}, u32[]{:S(2)}, u32[]{:S(2)}) collective-permute-start(bf16[96,1152]{1,0:T(8,128)(2,1)S(1)} %collective-permute-done.1.r2), channel_id=1, source_target_pairs={{0,1},{1,2},{2,3},{3,4},{4,5},{5,6},{6,7},{7,0},{8,15},{9,8},{10,9... | collective-permute-start | bytes 663560 | tf_op jit(solution)/shard_map/ppermute | solution.py:270
  36.8 2.8 %copy-start.3 = (bf16[96,1152]{1,0:T(8,128)(2,1)}, bf16[96,1152]{1,0:T(8,128)(2,1)S(1)}, u32[]{:S(2)}) copy-start(bf16[96,1152]{1,0:T(8,128)(2,1)S(1)} %collective-permute-done.3.l1) | copy-start | bytes 663556
  36.8 2.8 %copy-start.4 = (bf16[96,1152]{1,0:T(8,128)(2,1)}, bf16[96,1152]{1,0:T(8,128)(2,1)S(1)}, u32[]{:S(2)}) copy-start(bf16[96,1152]{1,0:T(8,128)(2,1)S(1)} %collective-permute-done.r1) | copy-start | bytes 663556
  37.4 2.3 %copy-start.5 = (bf16[96,1152]{1,0:T(8,128)(2,1)}, bf16[96,1152]{1,0:T(8,128)(2,1)S(1)}, u32[]{:S(2)}) copy-start(bf16[96,1152]{1,0:T(8,128)(2,1)S(1)} %collective-permute-done.6.l4) | copy-start | bytes 663556
  38.7 1.0 %copy-start.6 = (bf16[96,1152]{1,0:T(8,128)(2,1)}, bf16[96,1152]{1,0:T(8,128)(2,1)S(1)}, u32[]{:S(2)}) copy-start(bf16[96,1152]{1,0:T(8,128)(2,1)S(1)} %collective-permute-done.5.l3) | copy-start | bytes 663556
  39.6 0.7 copy-start.7
  47.2 18.9 %collective-permute-start.7 = (bf16[192,1024]{1,0:T(8,128)(2,1)}, bf16[192,1024]{1,0:T(8,128)(2,1)S(1)}, u32[]{:S(2)}, u32[]{:S(2)}) collective-permute-start(bf16[192,1024]{1,0:T(8,128)(2,1)} %get-tuple-element.44), channel_id=1, source_target_pairs={{0,1},{1,2},{2,3},{3,4},{4,5},{5,6},{6,7},{7,0},{8,15},{9,8},{10,9... | collective-permute-start | bytes 1179656 | tf_op jit(solution)/shard_map/ppermute | solution.py:270
  51.4 14.7 %collective-permute-start.8 = (bf16[192,1024]{1,0:T(8,128)(2,1)}, bf16[192,1024]{1,0:T(8,128)(2,1)S(1)}, u32[]{:S(2)}, u32[]{:S(2)}) collective-permute-start(bf16[192,1024]{1,0:T(8,128)(2,1)} %get-tuple-element.45), channel_id=1, source_target_pairs={{0,7},{1,0},{2,1},{3,2},{4,3},{5,4},{6,5},{7,6},{8,9},{9,10},{10,1... | collective-permute-start | bytes 1179656 | tf_op jit(solution)/shard_map/ppermute | solution.py:270
  53.3 12.8 %collective-permute-start.9 = (bf16[96,1024]{1,0:T(8,128)(2,1)}, bf16[96,1024]{1,0:T(8,128)(2,1)S(1)}, u32[]{:S(2)}, u32[]{:S(2)}) collective-permute-start(bf16[96,1024]{1,0:T(8,128)(2,1)} %get-tuple-element.46), channel_id=1, source_target_pairs={{0,2},{1,3},{2,4},{3,5},{4,6},{5,7},{6,0},{7,1},{8,14},{9,15},{10,... | collective-permute-start | bytes 589832 | tf_op jit(solution)/shard_map/ppermute | solution.py:270
  56.4 19.1 %all-to-all-start = ((f32[32,1,1024]{2,1,0:T(1,128)}), f32[32,1,1024]{2,1,0:T(1,128)S(1)}, u32[]{:S(2)}, u32[]{:S(2)}) async-start(f32[32,1,1024]{2,1,0:T(1,128)} %get-tuple-element.33), calls=%async_computation | async-start | bytes 262144 | tf_op jit(solution)/shard_map/all_to_all | solution.py:333
  67.1 24.0 %collective-permute-start.11 = (bf16[96,1024]{1,0:T(8,128)(2,1)S(1)}, bf16[96,1024]{1,0:T(8,128)(2,1)S(1)}, u32[]{:S(2)}, u32[]{:S(2)}) collective-permute-start(bf16[96,1024]{1,0:T(8,128)(2,1)S(1)} %add_convert_fusion), channel_id=1, source_target_pairs={{0,6},{1,7},{2,0},{3,1},{4,2},{5,3},{6,4},{7,5},{8,10},{9,11},{10,... | collective-permute-start | bytes 589832 | tf_op jit(solution)/shard_map/ppermute | solution.py:270
  71.3 19.9 %collective-permute-start.10 = (bf16[96,1024]{1,0:T(8,128)(2,1)S(1)}, bf16[96,1024]{1,0:T(8,128)(2,1)S(1)}, u32[]{:S(2)}, u32[]{:S(2)}) collective-permute-start(bf16[96,1024]{1,0:T(8,128)(2,1)S(1)} %add_convert_fusion.1), channel_id=1, source_target_pairs={{0,2},{1,3},{2,4},{3,5},{4,6},{5,7},{6,0},{7,1},{8,14},{9,15},{10,... | collective-permute-start | bytes 589832 | tf_op jit(solution)/shard_map/ppermute | solution.py:270
  76.3 17.4 %all-to-all-start.1 = ((f32[16,1,1024]{2,1,0:T(1,128)}), f32[16,1,1024]{2,1,0:T(1,128)S(1)}, u32[]{:S(2)}, u32[]{:S(2)}) async-start(f32[16,1,1024]{2,1,0:T(1,128)} %broadcast_in_dim.2), calls=%async_computation.1 | async-start | bytes 131072 | tf_op jit(solution)/shard_map/all_to_all | solution.py:337
  86.5 4.7 %copy-start = (bf16[96,1024]{1,0:T(8,128)(2,1)S(1)}, bf16[96,1024]{1,0:T(8,128)(2,1)}, u32[]{:S(2)}) copy-start(bf16[96,1024]{1,0:T(8,128)(2,1)} %get-tuple-element.43) | copy-start | bytes 589828
